TPU v7x, 256 devices: a whole 4x4x8 slice. The times are simulated.
256 devices in a mesh: prompt: 16 (over y, x_hi, core), seq: 16 (over z, x_lo).
Axes of the slice: x: 4 (x_hi: 2, x_lo: 2; x = x_hi * 2 + x_lo), y: 4, z: 8, core: 2. Of those that a mesh axis runs over, the one named last changes fastest.
Arguments:
- queries: bfloat16 [16, 2048, 4096], P('prompt', 'seq'), may hold values from -8 to 8
- self_keys: bfloat16 [16, 2048, 4096], P('prompt', 'seq'), may hold values from -8 to 8
- self_values: bfloat16 [16, 2048, 4096], P('prompt', 'seq'), may hold values from -6 to 6
- cross_queries: bfloat16 [16, 2048, 4096], P('prompt', 'seq')
- context: bfloat16 [16, 512, 5120], P('prompt', 'seq')
- key_weight: bfloat16 [5120, 4096], P('prompt', 'seq')
- value_weight: bfloat16 [5120, 4096], P('prompt', 'seq'), may hold values from -0.078125 to 0.078125
- lengths: int32 [16], P('prompt'), may hold values from 64 to 512, as said below
Outputs:
- attended: bfloat16 [16, 2048, 4096], P('prompt', 'seq')
Inputs may be any that keep to these rules, and one draw needn't show every extreme that they name: `lengths`: each prompt's number of text tokens; some prompt has all 512.
All inputs are finite; a program needn't handle non-finite values.
Results may differ from a plain program's by a relative error of at most 0.007.
Values may be sent and summed in bfloat16 or wider, within the bound.
No kernel may reach another device: no remote copies, remote signals or barrier semaphores. Data moves between devices by JAX's collectives and lax.ppermute only.
A program may use at most 64 MiB of HBM per device.

v0:
```python
import math

import jax
import jax.numpy as jnp
from jax import lax
from jax.sharding import PartitionSpec as P

HD = 128
HEADS = 32


def head_attend(query_rows, key_rows, value_rows, length, head_count):
    scaling = 1.0 / math.sqrt(HD)
    row_count = query_rows.shape[0]
    key_count = key_rows.shape[0]
    query_split = query_rows.reshape(row_count, head_count, HD)
    key_split = key_rows.reshape(key_count, head_count, HD)
    value_split = value_rows.reshape(key_count, head_count, HD)
    scores = (
        jnp.einsum("rhd,lhd->hrl", query_split, key_split, preferred_element_type=jnp.float32)
        * scaling
    )
    if length is None:
        row_max = jnp.max(scores, axis=2)
        weights = jnp.exp(scores - row_max[:, :, None])
    else:
        usable = (jnp.arange(key_count, dtype=jnp.int32) < length)[None, None, :]
        row_max = jnp.max(jnp.where(usable, scores, -jnp.inf), axis=2)
        shifted = jnp.where(usable, scores, row_max[:, :, None]) - row_max[:, :, None]
        weights = jnp.where(usable, jnp.exp(shifted), jnp.zeros_like(shifted))
    totals = jnp.sum(weights, axis=2)
    mixed = jnp.einsum(
        "hrl,lhd->rhd",
        weights.astype(jnp.bfloat16),
        value_split,
        preferred_element_type=jnp.float32,
    )
    return (
        (mixed / jnp.transpose(totals)[:, :, None])
        .reshape(row_count, head_count * HD)
        .astype(jnp.bfloat16)
    )


def by_blocks(function, query_rows):
    row_count = query_rows.shape[0]
    block_rows = math.gcd(row_count, 512)
    stacked = query_rows.reshape(row_count // block_rows, block_rows, query_rows.shape[1])
    return lax.map(function, stacked).reshape(row_count, -1)


def self_attend(query_heads, key_heads, value_heads, head_count):

    def self_run_block(block):
        return head_attend(block, key_heads, value_heads, None, head_count)

    return by_blocks(self_run_block, query_heads)


def cross_attend(query_rows, key_rows, value_rows, length, head_count):

    def cross_run_block(block):
        return head_attend(block, key_rows, value_rows, length, head_count)

    return by_blocks(cross_run_block, query_rows)


def body(
    queries, self_keys, self_values, cross_queries, context, key_weight, value_weight, lengths
):
    query_local = queries[0]
    key_local = self_keys[0]
    value_local = self_values[0]
    cross_local = cross_queries[0]
    length = lengths[0]
    head_local = key_weight.shape[1] // HD
    text_full = lax.all_gather(context[0], "seq", axis=0, tiled=True)
    key_sums = jnp.dot(
        text_full,
        lax.all_gather(key_weight, "prompt", axis=0, tiled=True),
        preferred_element_type=jnp.float32,
    )
    value_sums = jnp.dot(
        text_full,
        lax.all_gather(value_weight, "prompt", axis=0, tiled=True),
        preferred_element_type=jnp.float32,
    )
    text_keys = key_sums.astype(jnp.bfloat16)
    text_values = value_sums.astype(jnp.bfloat16)
    query_heads, key_heads, value_heads = (
        lax.all_to_all(query_local, "seq", split_axis=1, concat_axis=0, tiled=True),
        lax.all_to_all(key_local, "seq", split_axis=1, concat_axis=0, tiled=True),
        lax.all_to_all(value_local, "seq", split_axis=1, concat_axis=0, tiled=True),
    )
    self_heads = self_attend(query_heads, key_heads, value_heads, head_local)
    self_tokens = lax.all_to_all(self_heads, "seq", split_axis=0, concat_axis=1, tiled=True)
    all_keys, all_values = (
        lax.all_gather(text_keys, "seq", axis=1, tiled=True),
        lax.all_gather(text_values, "seq", axis=1, tiled=True),
    )
    cross_part = cross_attend(cross_local, all_keys, all_values, length, HEADS)
    attended = (self_tokens.astype(jnp.float32) + cross_part.astype(jnp.float32)).astype(
        jnp.bfloat16
    )
    return attended[None]


def solution(mesh):
    in_specs = (
        P("prompt", "seq", None),
        P("prompt", "seq", None),
        P("prompt", "seq", None),
        P("prompt", "seq", None),
        P("prompt", "seq", None),
        P("prompt", "seq"),
        P("prompt", "seq"),
        P("prompt"),
    )
    out_specs = P("prompt", "seq", None)
    return jax.shard_map(body, mesh=mesh, in_specs=in_specs, out_specs=out_specs, check_vma=False)
```

profile of v0, /device:TPU:8, one launch (start us, length us, event | category | flops | bytes accessed | tf_op | source)
XLA Modules:
  0.0 538.4 jit_solution(14828133115319314972)
XLA Ops:
  8.8 58.1 %all-gather.11.cloned.1.call-done = bf16[5120,256]{1,0:T(8,128)(2,1)} async-done(((bf16[320,256]{1,0:T(8,128)(2,1)}), bf16[5120,256]{1,0:T(8,128)(2,1)}) %all-gather.11.cloned.1.call-update) | async-done | bytes 2621456 | tf_op jit(solution)/shard_map/all_gather | solution.py:80
  66.9 120.4 %all-gather.15.cloned.1.call-done = bf16[1,512,5120]{2,1,0:T(8,128)(2,1)} async-done(((bf16[1,32,5120]{2,1,0:T(8,128)(2,1)}), bf16[1,512,5120]{2,1,0:T(8,128)(2,1)}) %all-gather.15.cloned.1.call-update) | async-done | bytes 5242896 | tf_op jit(solution)/shard_map/all_gather | solution.py:77
  187.4 5.5 %fusion.36 = bf16[512,256]{1,0:T(8,128)(2,1)} fusion(bf16[5120,256]{1,0:T(8,128)(2,1)} %all-gather.11.cloned.1.call-done, bf16[1,512,5120]{2,1,0:T(8,128)(2,1)} %all-gather.15.cloned.1.call-done), kind=kOutput, calls=%fused_computation.38 | convolution fusion | flops 1342308352 | bytes 8126464 | tf_op jit(solution)/shard_map/dot_general | solution.py:78
  194.3 6.9 %all-to-all-start.2 = ((bf16[128,16,256]{0,2,1:T(8,128)(2,1)}), bf16[128,16,256]{0,2,1:T(8,128)(2,1)S(1)}, u32[]{:S(2)}, u32[]{:S(2)}) async-start(bf16[128,16,256]{0,2,1:T(8,128)(2,1)} %bitcast.10), calls=%async_computation.2 | async-start | bytes 2097152 | tf_op jit(solution)/shard_map/all_to_all | solution.py:93
  202.6 27.5 %all-to-all-done.2 = bf16[128,16,256]{0,2,1:T(8,128)(2,1)S(1)} async-done(((bf16[128,16,256]{0,2,1:T(8,128)(2,1)}), bf16[128,16,256]{0,2,1:T(8,128)(2,1)S(1)}, u32[]{:S(2)}, u32[]{:S(2)}) %all-to-all-start.2) | async-done | bytes 1048608 | tf_op jit(solution)/shard_map/all_to_all | solution.py:93
  230.0 3.7 all-to-all-start
  233.7 1.5 copy.92
  236.5 24.8 %all-to-all-done = bf16[128,16,256]{0,2,1:T(8,128)(2,1)S(1)} async-done(((bf16[128,16,256]{0,2,1:T(8,128)(2,1)}), bf16[128,16,256]{0,2,1:T(8,128)(2,1)S(1)}, u32[]{:S(2)}, u32[]{:S(2)}) %all-to-all-start) | async-done | bytes 1048608 | tf_op jit(solution)/shard_map/all_to_all | solution.py:91
  261.4 4.3 all-to-all-start.1
  267.1 2.3 copy.76
  269.9 5.5 %fusion.33 = bf16[512,256]{1,0:T(8,128)(2,1)} fusion(bf16[5120,256]{1,0:T(8,128)(2,1)} %all-gather.7.cloned.1.call-done, bf16[1,512,5120]{2,1,0:T(8,128)(2,1)} %all-gather.15.cloned.1.call-done), kind=kOutput, calls=%fused_computation.37 | convolution fusion | flops 1342308352 | bytes 8126464 | tf_op jit(solution)/shard_map/dot_general | solution.py:83
  275.5 24.3 %all-to-all-done.1 = bf16[128,16,256]{2,0,1:T(8,128)(2,1)S(1)} async-done(((bf16[128,16,256]{2,0,1:T(8,128)(2,1)}), bf16[128,16,256]{2,0,1:T(8,128)(2,1)S(1)}, u32[]{:S(2)}, u32[]{:S(2)}) %all-to-all-start.1) | async-done | bytes 1048608 | tf_op jit(solution)/shard_map/all_to_all | solution.py:92
  299.8 23.7 %while.2 = (s32[]{:T(128)}, bf16[4,512,256]{2,1,0:T(8,128)(2,1)}, bf16[4,512,256]{2,1,0:T(8,128)(2,1)S(1)}, bf16[2048,256]{1,0:T(8,128)(2,1)S(1)}, bf16[2048,256]{0,1:T(8,128)(2,1)}, /*index=5*/s32[]{:T(128)}) while((s32[]{:T(128)}, bf16[4,512,256]{2,1,0:T(8,128)(2,1)}, bf16[4,512,256]{2,1,0:T(8,128)(2,1)S(1)}, ...), condition=%wide.region_3.4_spmd, body=%wide.region_0.3_spmd.sunk | while | flops 1090779136 | bytes 34099812 | solution.py:49
  301.4 1.6 fusion.59
  303.0 1.8 fusion.60
  307.3 1.6 fusion.59
  308.9 1.8 fusion.60
  313.2 1.6 fusion.59
  314.8 1.8 fusion.60
  319.1 1.6 fusion.59
  320.8 1.8 fusion.60
  323.4 9.0 %all-to-all-start.3 = ((bf16[16,128,256]{2,1,0:T(8,128)(2,1)}), bf16[16,128,256]{2,1,0:T(8,128)(2,1)S(1)}, u32[]{:S(2)}, u32[]{:S(2)}) async-start(bf16[16,128,256]{2,1,0:T(8,128)(2,1)} %bitcast.109), calls=%async_computation.3 | async-start | bytes 2097152 | tf_op jit(solution)/shard_map/all_to_all | solution.py:96
  334.6 30.5 %all-to-all-done.3 = bf16[16,128,256]{2,1,0:T(8,128)(2,1)S(1)} async-done(((bf16[16,128,256]{2,1,0:T(8,128)(2,1)}), bf16[16,128,256]{2,1,0:T(8,128)(2,1)S(1)}, u32[]{:S(2)}, u32[]{:S(2)}) %all-to-all-start.3) | async-done | bytes 1048608 | tf_op jit(solution)/shard_map/all_to_all | solution.py:96
  365.1 1.5 convert_bitcast_fusion
  366.7 1.9 copy.78
  368.6 29.0 %all-gather.13.cloned.1.call-done = bf16[512,4096]{1,0:T(8,128)(2,1)} async-done(((bf16[512,256]{1,0:T(8,128)(2,1)}), bf16[512,4096]{1,0:T(8,128)(2,1)}) %all-gather.13.cloned.1.call-update) | async-done | bytes 4194320 | tf_op jit(solution)/shard_map/all_gather | solution.py:98
  397.7 3.7 select_reduce_fusion
  401.4 3.2 copy-done
  404.6 2.3 bitcast_reduce_fusion
  407.0 109.3 %all-gather.9.cloned.1.call-done = bf16[512,4096]{1,0:T(8,128)(2,1)} async-done(((bf16[512,256]{1,0:T(8,128)(2,1)}), bf16[512,4096]{1,0:T(8,128)(2,1)}) %all-gather.9.cloned.1.call-update) | async-done | bytes 4194320 | tf_op jit(solution)/shard_map/all_gather | solution.py:99
  516.3 6.5 %copy.86 = bf16[512,4096]{0,1:T(8,128)(2,1)} copy(bf16[512,4096]{1,0:T(8,128)(2,1)} %all-gather.9.cloned.1.call-done) | data formatting | bytes 8388608 | tf_op jit(solution)/shard_map/while/body/eval_jaxpr/reshape | solution.py:18
  522.7 7.5 %fusion.32 = bf16[128,32,128]{0,2,1:T(8,128)(2,1)S(1)} fusion(bf16[512,32,128]{0,2,1:T(8,128)(2,1)} %bitcast.102, f32[32,512,128]{2,1,0:T(8,128)} %copy-done, f32[32,128]{1,0:T(8,128)S(1)} %get-tuple-element.83, pred[512]{0:T(512)(128)(4,1)S(1)} %iota_compare_fusion, f32[128,32]{0,1:T(8,128)S(1)} %bitcast.112), kind=kOutput, calls=%fused_computation.35 | convolution fusion | flops 548405248 | bytes 13664768 | tf_op jit(solution)/shard_map/while/body/eval_jaxpr/hrl,lhd->rhd/dot_general | solution.py:32
  (54 shorter events, 20.9 us)
Async XLA Ops:
  6.5 60.4 %all-gather.11.cloned.1.call-start = ((), (), s32[]{:S(2)}) async-start(), calls=%async_computation.6 | async-start | bytes 2785280 | tf_op jit(solution)/shard_map/all_gather | solution.py:80
  7.3 185.7 %copy-start.1 = (bf16[1,128,4096]{2,1,0:T(8,128)(2,1)S(1)}, bf16[1,128,4096]{2,1,0:T(8,128)(2,1)}, u32[]{:S(2)}) copy-start(bf16[1,128,4096]{2,1,0:T(8,128)(2,1)} %param.12) | copy-start | bytes 3145732
  7.3 180.1 %all-gather.15.cloned.1.call-start = ((), (), s32[]{:S(2)}) async-start(), calls=%async_computation.8 | async-start | bytes 5570560 | tf_op jit(solution)/shard_map/all_gather | solution.py:77
  8.0 261.9 %all-gather.7.cloned.1.call-start = ((), (), s32[]{:S(2)}) async-start(), calls=%async_computation.4 | async-start | bytes 2785280 | tf_op jit(solution)/shard_map/all_gather | solution.py:85
  8.8 192.5 %copy-start.2 = (bf16[1,128,4096]{2,1,0:T(8,128)(2,1)S(1)}, bf16[1,128,4096]{2,1,0:T(8,128)(2,1)}, u32[]{:S(2)}) copy-start(bf16[1,128,4096]{2,1,0:T(8,128)(2,1)} %param.10) | copy-start | bytes 3145732
  8.8 388.9 %all-gather.13.cloned.1.call-start = ((), (), s32[]{:S(2)}) async-start(), calls=%async_computation.7 | async-start | bytes 4456448 | tf_op jit(solution)/shard_map/all_gather | solution.py:98
  194.3 35.7 %all-to-all-start.2 = ((bf16[128,16,256]{0,2,1:T(8,128)(2,1)}), bf16[128,16,256]{0,2,1:T(8,128)(2,1)S(1)}, u32[]{:S(2)}, u32[]{:S(2)}) async-start(bf16[128,16,256]{0,2,1:T(8,128)(2,1)} %bitcast.10), calls=%async_computation.2 | async-start | bytes 2097152 | tf_op jit(solution)/shard_map/all_to_all | solution.py:93
  230.0 31.3 %all-to-all-start = ((bf16[128,16,256]{0,2,1:T(8,128)(2,1)}), bf16[128,16,256]{0,2,1:T(8,128)(2,1)S(1)}, u32[]{:S(2)}, u32[]{:S(2)}) async-start(bf16[128,16,256]{0,2,1:T(8,128)(2,1)} %bitcast.5), calls=%async_computation | async-start | bytes 2097152 | tf_op jit(solution)/shard_map/all_to_all | solution.py:91
  261.4 38.4 %all-to-all-start.1 = ((bf16[128,16,256]{2,0,1:T(8,128)(2,1)}), bf16[128,16,256]{2,0,1:T(8,128)(2,1)S(1)}, u32[]{:S(2)}, u32[]{:S(2)}) async-start(bf16[128,16,256]{2,0,1:T(8,128)(2,1)} %copy.72), calls=%async_computation.1 | async-start | bytes 2097152 | tf_op jit(solution)/shard_map/all_to_all | solution.py:92
  265.7 250.6 %all-gather.9.cloned.1.call-start = ((), (), s32[]{:S(2)}) async-start(), calls=%async_computation.5 | async-start | bytes 4456448 | tf_op jit(solution)/shard_map/all_gather | solution.py:99
  301.4 1.7 copy-start.3
  307.3 1.7 copy-start.3
  313.2 1.7 copy-start.3
  319.1 1.7 copy-start.3
  323.4 41.7 %all-to-all-start.3 = ((bf16[16,128,256]{2,1,0:T(8,128)(2,1)}), bf16[16,128,256]{2,1,0:T(8,128)(2,1)S(1)}, u32[]{:S(2)}, u32[]{:S(2)}) async-start(bf16[16,128,256]{2,1,0:T(8,128)(2,1)} %bitcast.109), calls=%async_computation.3 | async-start | bytes 2097152 | tf_op jit(solution)/shard_map/all_to_all | solution.py:96
  401.4 3.2 copy-start
Sparse Core Ops, SparseCore 0:
  10.1 56.7 all-gather.10
  68.7 118.6 all-gather.14
  190.1 54.7 all-gather.6
  246.5 151.0 all-gather.12
  399.2 117.0 all-gather.8
where the time goes:
time: 541 us; the launch traced here: 538 us
  waiting for transfers between devices  426 us (79%)
  matrix products  35.1 us (6%)
  local copies, waits for them, and re-layouts  28.1 us (5%)
  starting transfers between devices  24.1 us (4%)
  between operations  13.9 us (3%)
  other arithmetic  10.7 us (2%)
    all_gather x1, waiting for transfers between devices, body(): text_full = lax.all_gather(context[0], 'seq', axis=0, tiled=True)  120 us
    all_gather x1, waiting for transfers between devices, body(): lax.all_gather(text_values, 'seq', axis=1, tiled=True)  109 us
    all_gather x1, waiting for transfers between devices, body(): lax.all_gather(key_weight, 'prompt', axis=0, tiled=True)  58.1 us
    all_to_all x1, waiting for transfers between devices, body(): lax.all_to_all(self_heads, 'seq', split_axis=0, concat_axis=1, tiled=True)  30.5 us
    all_gather x1, waiting for transfers between devices, body(): lax.all_gather(text_keys, 'seq', axis=1, tiled=True)  29 us
    all_to_all x1, waiting for transfers between devices, body(): lax.all_to_all(value_local, 'seq', split_axis=1, concat_axis=0, tiled=True)  27.5 us
    all_to_all x1, waiting for transfers between devices, body(): lax.all_to_all(query_local, 'seq', split_axis=1, concat_axis=0, tiled=True)  24.8 us
    all_to_all x1, waiting for transfers between devices, body(): lax.all_to_all(key_local, 'seq', split_axis=1, concat_axis=0, tiled=True)  24.3 us
  transfers between devices with their start and end apart: 9, of which 8 were waited for; matrix products, arithmetic and copies ran while one was open for 10% of the time, Pallas kernels for 0%

commit v1 on v0

v1 whole, which is shorter than its diff:
```python
import math

import jax
import jax.numpy as jnp
from jax import lax
from jax.experimental import pallas as pl
from jax.experimental.pallas import tpu as pltpu
from jax.sharding import PartitionSpec as P

HD = 128
EXP2_SCALE = math.log2(math.e) / math.sqrt(HD)


def softmax_mix(query, keys, values, usable):
    scores = lax.dot_general(
        query, keys, (((1,), (1,)), ((), ())), preferred_element_type=jnp.float32
    )
    if usable is not None:
        scores = jnp.where(usable, scores, -jnp.inf)
    row_max = jnp.max(scores, axis=1, keepdims=True)
    weights = jnp.exp2((scores - row_max) * EXP2_SCALE)
    totals = jnp.sum(weights, axis=1, keepdims=True)
    mixed = jnp.dot(weights.astype(jnp.bfloat16), values, preferred_element_type=jnp.float32)
    return mixed / totals


def attend_kernel(length_ref, q_ref, k_ref, v_ref, cq_ref, tk_ref, tv_ref, out_ref):
    text_slots = tk_ref.shape[0]
    usable = lax.broadcasted_iota(jnp.int32, (1, text_slots), 1) < length_ref[0]
    for head in range(q_ref.shape[1] // HD):
        cols = slice(head * HD, (head + 1) * HD)
        self_out = softmax_mix(q_ref[:, cols], k_ref[:, cols], v_ref[:, cols], None)
        cross_out = softmax_mix(cq_ref[:, cols], tk_ref[:, cols], tv_ref[:, cols], usable)
        out_ref[:, cols] = (
            self_out.astype(jnp.bfloat16).astype(jnp.float32)
            + cross_out.astype(jnp.bfloat16).astype(jnp.float32)
        ).astype(jnp.bfloat16)


def attend(length, q, k, v, cq, tk, tv):
    rows, width = q.shape
    block = math.gcd(rows, 256)
    row_spec = pl.BlockSpec((block, width), lambda i: (i, 0))

    def whole(array):
        return pl.BlockSpec(array.shape, lambda i: (0, 0))

    pairs = rows * width * (k.shape[0] + tk.shape[0])
    return pl.pallas_call(
        attend_kernel,
        grid=(rows // block,),
        in_specs=[
            pl.BlockSpec(memory_space=pltpu.SMEM),
            row_spec,
            whole(k),
            whole(v),
            row_spec,
            whole(tk),
            whole(tv),
        ],
        out_specs=row_spec,
        out_shape=jax.ShapeDtypeStruct((rows, width), jnp.bfloat16),
        compiler_params=pltpu.CompilerParams(vmem_limit_bytes=40 << 20),
        cost_estimate=pl.CostEstimate(
            flops=4 * pairs,
            bytes_accessed=10 * rows * width,
            transcendentals=pairs // HD,
        ),
        name="attend",
    )(length, q, k, v, cq, tk, tv)


def body(
    queries, self_keys, self_values, cross_queries, context, key_weight, value_weight, lengths
):
    def to_heads(rows):
        return lax.all_to_all(rows, "seq", split_axis=1, concat_axis=0, tiled=True)

    text_full = lax.all_gather(context[0], "seq", axis=0, tiled=True)
    key_full = lax.all_gather(key_weight, "prompt", axis=0, tiled=True)
    value_full = lax.all_gather(value_weight, "prompt", axis=0, tiled=True)
    q = to_heads(queries[0])
    k = to_heads(self_keys[0])
    v = to_heads(self_values[0])
    cq = to_heads(cross_queries[0])
    tk = jnp.dot(text_full, key_full, preferred_element_type=jnp.float32).astype(jnp.bfloat16)
    tv = jnp.dot(text_full, value_full, preferred_element_type=jnp.float32).astype(jnp.bfloat16)
    attended = attend(lengths, q, k, v, cq, tk, tv)
    return lax.all_to_all(attended, "seq", split_axis=0, concat_axis=1, tiled=True)[None]


def solution(mesh):
    in_specs = (
        P("prompt", "seq", None),
        P("prompt", "seq", None),
        P("prompt", "seq", None),
        P("prompt", "seq", None),
        P("prompt", "seq", None),
        P("prompt", "seq"),
        P("prompt", "seq"),
        P("prompt"),
    )
    out_specs = P("prompt", "seq", None)
    return jax.shard_map(body, mesh=mesh, in_specs=in_specs, out_specs=out_specs, check_vma=False)
```

time: 541 us -> 342 us (0.63)
  waiting for transfers between devices: 426 us -> 226 us
  blocking collectives: 0 us -> 36.2 us
  matrix products: 35.1 us -> 10.4 us
  Pallas kernels: 0 us -> 19 us
  local copies, waits for them, and re-layouts: 28.1 us -> 11.6 us
  other arithmetic: 10.7 us -> 0 us
    all_gather x4 -> x2, waiting for transfers between devices: 196 us -> 53.6 us  [the longest x1 53.6 us: body(): value_full = lax.all_gather(value_weight, 'prompt', axis=0, tiled=True)]
    all_to_all x0 -> x1, blocking collectives: none -> 36.2 us  [body(): lax.all_to_all(attended, 'seq', split_axis=0, concat_axis=1, tiled=True)]
    all_gather x1, waiting for transfers between devices: 120 us -> 85.4 us  [body(): text_full = lax.all_gather(context[0], 'seq', axis=0, tiled=True)]
    dot_general x12 -> x2, matrix products: 35.1 us -> 10.4 us  [the longest x1 5.53 us: body(): jnp.dot(text_full, value_full, preferred_element_type=jnp.float32)]
    all_to_all x4, waiting for transfers between devices: 107 us -> 84.7 us  [to_heads(): return lax.all_to_all(rows, 'seq', split_axis=1, concat_axis=0, tiled=True)]
    pallas_call x0 -> x1, Pallas kernels: none -> 19 us  [attend(): pl.pallas_call(attend_kernel, grid=(rows // block,), in_specs=[pl.BlockSp...]
    reduce_sum x5 -> x0, other arithmetic: 8.92 us -> none  [head_attend(): totals = jnp.sum(weights, axis=2)]
    reshape x1 -> x0, local copies, waits for them, and re-layouts: 6.45 us -> none  [head_attend(): value_split = value_rows.reshape(key_count, head_count, HD)]
  transfers between devices with their start and end apart: 9 -> 7, of which waited for: 8 -> 5; matrix products, arithmetic and copies ran while one was open for 10% -> 6% of each run, Pallas kernels for 0% -> 0%
where the time goes in v1:
time: 342 us; the launch traced here: 341 us
  waiting for transfers between devices  226 us (66%)
  blocking collectives  36.2 us (11%)
  starting transfers between devices  24.6 us (7%)
  Pallas kernels  19 us (6%)
  between operations  13.9 us (4%)
  local copies, waits for them, and re-layouts  11.6 us (3%)
  matrix products  10.4 us (3%)
    all_gather x1, waiting for transfers between devices, body(): text_full = lax.all_gather(context[0], 'seq', axis=0, tiled=True)  85.4 us
    all_to_all x4, waiting for transfers between devices, to_heads(): return lax.all_to_all(rows, 'seq', split_axis=1, concat_axis=0, tiled=True)  84.7 us
    all_gather x1, waiting for transfers between devices, body(): value_full = lax.all_gather(value_weight, 'prompt', axis=0, tiled=True)  53.6 us
    all_to_all x1, blocking collectives, body(): lax.all_to_all(attended, 'seq', split_axis=0, concat_axis=1, tiled=True)  36.2 us
    all_to_all x4, starting transfers between devices, to_heads(): return lax.all_to_all(rows, 'seq', split_axis=1, concat_axis=0, tiled=True)  24.5 us
    pallas_call x1, Pallas kernels, attend(): pl.pallas_call(attend_kernel, grid=(rows // block,), in_specs=[pl.BlockSp...  19 us
  transfers between devices with their start and end apart: 7, of which 5 were waited for; matrix products, arithmetic and copies ran while one was open for 6% of the time, Pallas kernels for 0%

profile of v1, /device:TPU:8, one launch (start us, length us, event | category | flops | bytes accessed | tf_op | source)
XLA Modules:
  0.0 341.4 jit_solution(7791795567592702308)
XLA Ops:
  6.5 0.7 all-gather.5.cloned.1.call-update
  7.3 0.0 all-gather.9.cloned.1.call-start
  7.3 0.7 all-gather.9.cloned.1.call-update
  8.0 1.5 copy.14
  9.5 0.0 copy-start.1
  9.5 1.3 copy.9
  10.8 9.5 %all-to-all-start = ((bf16[128,16,256]{2,0,1:T(8,128)(2,1)}), bf16[128,16,256]{2,0,1:T(8,128)(2,1)S(1)}, u32[]{:S(2)}, u32[]{:S(2)}) async-start(bf16[128,16,256]{2,0,1:T(8,128)(2,1)} %copy.9), calls=%async_computation | async-start | bytes 2097152 | tf_op jit(solution)/shard_map/all_to_all | solution.py:77
  20.3 0.2 copy.15
  20.6 0.0 copy-start.2
  20.6 1.3 copy.10
  21.9 27.1 %all-to-all-done = bf16[128,16,256]{2,0,1:T(8,128)(2,1)S(1)} async-done(((bf16[128,16,256]{2,0,1:T(8,128)(2,1)}), bf16[128,16,256]{2,0,1:T(8,128)(2,1)S(1)}, u32[]{:S(2)}, u32[]{:S(2)}) %all-to-all-start) | async-done | bytes 1048608 | tf_op jit(solution)/shard_map/all_to_all | solution.py:77
  49.0 3.7 %all-to-all-start.1 = ((bf16[128,16,256]{2,0,1:T(8,128)(2,1)}), bf16[128,16,256]{2,0,1:T(8,128)(2,1)S(1)}, u32[]{:S(2)}, u32[]{:S(2)}) async-start(bf16[128,16,256]{2,0,1:T(8,128)(2,1)} %copy.10), calls=%async_computation.1 | async-start | bytes 2097152 | tf_op jit(solution)/shard_map/all_to_all | solution.py:77
  52.7 0.0 all-gather.7.cloned.1.call-start
  52.7 0.7 all-gather.7.cloned.1.call-update
  53.4 0.2 copy.16
  53.7 1.3 copy.11
  55.0 25.3 %all-to-all-done.1 = bf16[128,16,256]{2,0,1:T(8,128)(2,1)S(1)} async-done(((bf16[128,16,256]{2,0,1:T(8,128)(2,1)}), bf16[128,16,256]{2,0,1:T(8,128)(2,1)S(1)}, u32[]{:S(2)}, u32[]{:S(2)}) %all-to-all-start.1) | async-done | bytes 1048608 | tf_op jit(solution)/shard_map/all_to_all | solution.py:77
  80.3 3.7 %all-to-all-start.2 = ((bf16[128,16,256]{2,0,1:T(8,128)(2,1)}), bf16[128,16,256]{2,0,1:T(8,128)(2,1)S(1)}, u32[]{:S(2)}, u32[]{:S(2)}) async-start(bf16[128,16,256]{2,0,1:T(8,128)(2,1)} %copy.11), calls=%async_computation.2 | async-start | bytes 2097152 | tf_op jit(solution)/shard_map/all_to_all | solution.py:77
  84.0 1.5 copy.17
  85.5 1.4 copy.12
  86.8 32.2 %all-to-all-done.2 = bf16[128,16,256]{2,0,1:T(8,128)(2,1)S(1)} async-done(((bf16[128,16,256]{2,0,1:T(8,128)(2,1)}), bf16[128,16,256]{2,0,1:T(8,128)(2,1)S(1)}, u32[]{:S(2)}, u32[]{:S(2)}) %all-to-all-start.2) | async-done | bytes 1048608 | tf_op jit(solution)/shard_map/all_to_all | solution.py:77
  119.0 7.7 %all-to-all-start.3 = ((bf16[128,16,256]{2,0,1:T(8,128)(2,1)}), bf16[128,16,256]{2,0,1:T(8,128)(2,1)}, u32[]{:S(2)}, u32[]{:S(2)}) async-start(bf16[128,16,256]{2,0,1:T(8,128)(2,1)} %copy.12), calls=%async_computation.3 | async-start | bytes 2097152 | tf_op jit(solution)/shard_map/all_to_all | solution.py:77
  127.4 0.0 all-gather.5.cloned.1.call-done
  127.4 85.4 %all-gather.9.cloned.1.call-done = bf16[1,512,5120]{2,1,0:T(8,128)(2,1)} async-done(((bf16[1,32,5120]{2,1,0:T(8,128)(2,1)}), bf16[1,512,5120]{2,1,0:T(8,128)(2,1)}) %all-gather.9.cloned.1.call-update) | async-done | bytes 5242896 | tf_op jit(solution)/shard_map/all_gather | solution.py:79
  212.8 4.8 %fusion.4.tk_ref = bf16[512,256]{1,0:T(8,128)(2,1)S(1)} fusion(bf16[5120,256]{1,0:T(8,128)(2,1)} %all-gather.5.cloned.1.call-done, bf16[1,512,5120]{2,1,0:T(8,128)(2,1)} %all-gather.9.cloned.1.call-done), kind=kOutput, calls=%fused_computation.4 | convolution fusion | flops 1342308352 | bytes 8126464 | tf_op jit(solution)/shard_map/dot_general | solution.py:86
  217.6 53.6 %all-gather.7.cloned.1.call-done = bf16[5120,256]{1,0:T(8,128)(2,1)} async-done(((bf16[320,256]{1,0:T(8,128)(2,1)}), bf16[5120,256]{1,0:T(8,128)(2,1)}) %all-gather.7.cloned.1.call-update) | async-done | bytes 2621456 | tf_op jit(solution)/shard_map/all_gather | solution.py:81
  271.3 5.5 %fusion.7.tv_ref = bf16[512,256]{1,0:T(8,128)(2,1)} fusion(bf16[5120,256]{1,0:T(8,128)(2,1)} %all-gather.7.cloned.1.call-done, bf16[1,512,5120]{2,1,0:T(8,128)(2,1)} %all-gather.9.cloned.1.call-done), kind=kOutput, calls=%fused_computation.5 | convolution fusion | flops 1342308352 | bytes 8126464 | tf_op jit(solution)/shard_map/dot_general | solution.py:87
  276.8 0.9 copy-done
  277.8 19.0 %attend.1 = bf16[2048,256]{1,0:T(8,128)(2,1)S(1)} custom-call(s32[1]{0:T(128)S(6)} %copy.18.length_ref, bf16[2048,256]{1,0:T(8,128)(2,1)S(1)} %bitcast.37, bf16[2048,256]{1,0:T(8,128)(2,1)S(1)} %bitcast.38, bf16[2048,256]{1,0:T(8,128)(2,1)S(1)} %bitcast.39, bf16[2048,256]{1,0:T(8,128)(2,1)} %bitcast.7.cq_ref, bf16[512,256]{1,0:T(8,128)(2,1)S(1)} %fusion.4.tk_ref, ...), custom_call_target="tpu_custom_call" | custom-call | flops 5368709120 | bytes 5242880 | tf_op jit(solution)/shard_map/attend/pallas_call | solution.py:49
  296.7 36.2 %all_to_all.92 = bf16[16,128,256]{2,1,0:T(8,128)(2,1)S(1)} all-to-all(bf16[16,128,256]{2,1,0:T(8,128)(2,1)S(1)} %bitcast.40), channel_id=1, replica_groups=mesh['prompt'=16,'seq'=16] {'seq'}, dimensions={0} | all-to-all | bytes 2097152 | tf_op jit(solution)/shard_map/all_to_all | solution.py:89
  333.0 0.6 copy.13
  333.6 1.3 broadcast_in_dim.3
  (5 shorter events, 0.0 us)
Async XLA Ops:
  6.5 120.9 %all-gather.5.cloned.1.call-start = ((), (), s32[]{:S(2)}) async-start(), calls=%async_computation.5 | async-start | bytes 2785280 | tf_op jit(solution)/shard_map/all_gather | solution.py:80
  7.3 205.6 %all-gather.9.cloned.1.call-start = ((), (), s32[]{:S(2)}) async-start(), calls=%async_computation.7 | async-start | bytes 5570560 | tf_op jit(solution)/shard_map/all_gather | solution.py:79
  9.5 10.8 %copy-start.1 = (bf16[1,128,4096]{2,1,0:T(8,128)(2,1)S(1)}, bf16[1,128,4096]{2,1,0:T(8,128)(2,1)}, u32[]{:S(2)}) copy-start(bf16[1,128,4096]{2,1,0:T(8,128)(2,1)} %param.9) | copy-start | bytes 3145732
  10.8 38.2 %all-to-all-start = ((bf16[128,16,256]{2,0,1:T(8,128)(2,1)}), bf16[128,16,256]{2,0,1:T(8,128)(2,1)S(1)}, u32[]{:S(2)}, u32[]{:S(2)}) async-start(bf16[128,16,256]{2,0,1:T(8,128)(2,1)} %copy.9), calls=%async_computation | async-start | bytes 2097152 | tf_op jit(solution)/shard_map/all_to_all | solution.py:77
  20.6 32.8 %copy-start.2 = (bf16[1,128,4096]{2,1,0:T(8,128)(2,1)S(1)}, bf16[1,128,4096]{2,1,0:T(8,128)(2,1)}, u32[]{:S(2)}) copy-start(bf16[1,128,4096]{2,1,0:T(8,128)(2,1)} %param.10) | copy-start | bytes 3145732
  49.0 31.3 %all-to-all-start.1 = ((bf16[128,16,256]{2,0,1:T(8,128)(2,1)}), bf16[128,16,256]{2,0,1:T(8,128)(2,1)S(1)}, u32[]{:S(2)}, u32[]{:S(2)}) async-start(bf16[128,16,256]{2,0,1:T(8,128)(2,1)} %copy.10), calls=%async_computation.1 | async-start | bytes 2097152 | tf_op jit(solution)/shard_map/all_to_all | solution.py:77
  52.7 218.6 %all-gather.7.cloned.1.call-start = ((), (), s32[]{:S(2)}) async-start(), calls=%async_computation.6 | async-start | bytes 2785280 | tf_op jit(solution)/shard_map/all_gather | solution.py:81
  80.3 38.7 %all-to-all-start.2 = ((bf16[128,16,256]{2,0,1:T(8,128)(2,1)}), bf16[128,16,256]{2,0,1:T(8,128)(2,1)S(1)}, u32[]{:S(2)}, u32[]{:S(2)}) async-start(bf16[128,16,256]{2,0,1:T(8,128)(2,1)} %copy.11), calls=%async_computation.2 | async-start | bytes 2097152 | tf_op jit(solution)/shard_map/all_to_all | solution.py:77
  119.0 157.8 %all-to-all-start.3 = ((bf16[128,16,256]{2,0,1:T(8,128)(2,1)}), bf16[128,16,256]{2,0,1:T(8,128)(2,1)}, u32[]{:S(2)}, u32[]{:S(2)}) async-start(bf16[128,16,256]{2,0,1:T(8,128)(2,1)} %copy.12), calls=%async_computation.3 | async-start | bytes 2097152 | tf_op jit(solution)/shard_map/all_to_all | solution.py:77
  276.8 1.0 copy-start
Sparse Core Ops, SparseCore 0:
  10.1 58.3 all-gather.4
  70.3 142.5 all-gather.8
  215.6 55.6 all-gather.6

commit v2 on v1

v2 whole, which is shorter than its diff:
```python
import math

import jax
import jax.numpy as jnp
from jax import lax
from jax.experimental import pallas as pl
from jax.experimental.pallas import tpu as pltpu
from jax.sharding import PartitionSpec as P

HD = 128
EXP2_SCALE = math.log2(math.e) / math.sqrt(HD)
Y, XH, CORE = 4, 2, 2
Z, XL = 8, 2


def y_shift(step):
    block = XH * CORE
    return [(p, (p + step * block) % (Y * block)) for p in range(Y * block)]


def z_shift(step):
    return [(s, (s + step * XL) % (Z * XL)) for s in range(Z * XL)]


CORE_SWAP = [(p, p ^ 1) for p in range(Y * XH * CORE)]
XL_SWAP = [(s, s ^ 1) for s in range(Z * XL)]
REGROUP_A = [(4 * y + a, 4 * y + b) for y in range(Y) for a, b in ((0, 2), (2, 3), (3, 1), (1, 0))]
REGROUP_B = [(4 * y + a, 4 * y + b) for y in range(Y) for a, b in ((1, 2), (2, 1))]


def pack_kernel(*refs):
    out_ref = refs[-1]
    width = refs[0].shape[1]
    for place, ref in enumerate(refs[:-1]):
        out_ref[0, :, place * width : (place + 1) * width] = ref[...]


def pack(arrays, parts):
    rows, columns = arrays[0].shape
    width = columns // parts
    return pl.pallas_call(
        pack_kernel,
        grid=(parts,),
        in_specs=[pl.BlockSpec((rows, width), lambda i: (0, i)) for _ in arrays],
        out_specs=pl.BlockSpec((1, rows, width * len(arrays)), lambda i: (i, 0, 0)),
        out_shape=jax.ShapeDtypeStruct((parts, rows, width * len(arrays)), jnp.bfloat16),
        cost_estimate=pl.CostEstimate(
            flops=0, bytes_accessed=4 * rows * columns * len(arrays), transcendentals=0
        ),
        name="pack",
    )(*arrays)


def unpack_kernel(in_ref, out_ref):
    out_ref[...] = in_ref[0]


def unpack(blocks):
    parts, rows, width = blocks.shape
    return pl.pallas_call(
        unpack_kernel,
        grid=(parts,),
        in_specs=[pl.BlockSpec((1, rows, width), lambda i: (i, 0, 0))],
        out_specs=pl.BlockSpec((rows, width), lambda i: (0, i)),
        out_shape=jax.ShapeDtypeStruct((rows, parts * width), jnp.bfloat16),
        name="unpack",
    )(blocks)


def softmax_mix(query, keys, values, bias):
    scores = lax.dot_general(
        query, keys, (((1,), (1,)), ((), ())), preferred_element_type=jnp.float32
    )
    if bias is not None:
        scores = scores + bias
    row_max = jnp.max(scores, axis=1, keepdims=True)
    weights = jnp.exp2((scores - row_max) * EXP2_SCALE)
    totals = jnp.sum(weights, axis=1, keepdims=True)
    mixed = jnp.dot(weights.astype(jnp.bfloat16), values, preferred_element_type=jnp.float32)
    return mixed / totals


def self_kernel(q_ref, k_ref, v_ref, out_ref):
    for head in range(q_ref.shape[1] // HD):
        cols = slice(head * HD, (head + 1) * HD)
        out_ref[:, cols] = softmax_mix(
            q_ref[:, cols], k_ref[:, cols], v_ref[:, cols], None
        ).astype(jnp.bfloat16)


def cross_kernel(bias_ref, cq_ref, tk_ref, tv_ref, self_ref, out_ref):
    for head in range(cq_ref.shape[1] // HD):
        cols = slice(head * HD, (head + 1) * HD)
        cross_out = softmax_mix(cq_ref[:, cols], tk_ref[:, cols], tv_ref[:, cols], bias_ref[...])
        out_ref[:, cols] = (
            self_ref[:, cols].astype(jnp.float32)
            + cross_out.astype(jnp.bfloat16).astype(jnp.float32)
        ).astype(jnp.bfloat16)


def self_attend(qkv, width):
    rows = qkv.shape[0]
    block = math.gcd(rows, 256)
    pairs = rows * width * rows
    return pl.pallas_call(
        self_kernel,
        grid=(rows // block,),
        in_specs=[
            pl.BlockSpec((block, width), lambda i: (i, 0)),
            pl.BlockSpec((rows, width), lambda i: (0, 1)),
            pl.BlockSpec((rows, width), lambda i: (0, 2)),
        ],
        out_specs=pl.BlockSpec((block, width), lambda i: (i, 0)),
        out_shape=jax.ShapeDtypeStruct((rows, width), jnp.bfloat16),
        compiler_params=pltpu.CompilerParams(vmem_limit_bytes=32 << 20),
        cost_estimate=pl.CostEstimate(
            flops=4 * pairs, bytes_accessed=8 * rows * width, transcendentals=pairs // HD
        ),
        name="self_attend",
    )(qkv, qkv, qkv)


def cross_attend(bias, cq, text, self_out):
    rows, width = cq.shape
    slots = text.shape[0]
    block = math.gcd(rows, 512)
    pairs = rows * width * slots
    row_spec = pl.BlockSpec((block, width), lambda i: (i, 0))
    return pl.pallas_call(
        cross_kernel,
        grid=(rows // block,),
        in_specs=[
            pl.BlockSpec((1, slots), lambda i: (0, 0)),
            row_spec,
            pl.BlockSpec((slots, width), lambda i: (0, 0)),
            pl.BlockSpec((slots, width), lambda i: (0, 1)),
            row_spec,
        ],
        out_specs=row_spec,
        out_shape=jax.ShapeDtypeStruct((rows, width), jnp.bfloat16),
        compiler_params=pltpu.CompilerParams(vmem_limit_bytes=32 << 20),
        cost_estimate=pl.CostEstimate(
            flops=4 * pairs, bytes_accessed=6 * rows * width, transcendentals=pairs // HD
        ),
        name="cross_attend",
    )(bias, cq, text, text, self_out)


def gather_weights(weights, x_hi, core):
    wide = jnp.concatenate([weights, lax.ppermute(weights, "seq", XL_SWAP)], axis=1)
    first = lax.ppermute(wide, "prompt", REGROUP_A)
    second = lax.ppermute(wide, "prompt", REGROUP_B)
    same = x_hi == core
    keep = jnp.where(same, wide, second)
    chunk = jnp.where(
        core == 0,
        jnp.where(same, jnp.concatenate([keep, first]), jnp.concatenate([first, keep])),
        jnp.where(same, jnp.concatenate([first, keep]), jnp.concatenate([keep, first])),
    )
    return chunk


def ring_y(chunk):
    half = chunk.shape[0] // 2
    before = lax.ppermute(chunk, "prompt", y_shift(1))
    after = lax.ppermute(chunk, "prompt", y_shift(-1))
    far_top = lax.ppermute(before[:half], "prompt", y_shift(1))
    far_bottom = lax.ppermute(after[half:], "prompt", y_shift(-1))
    return jnp.concatenate([chunk, after, far_top, far_bottom, before], axis=0)


def ring_z(block):
    half = block.shape[0] // 2
    found = [(0, block)]
    up = down = block
    for step in range(1, Z // 2):
        up = lax.ppermute(up, "seq", z_shift(1))
        down = lax.ppermute(down, "seq", z_shift(-1))
        found += [(-step, up), (step, down)]
    far_top = lax.ppermute(up[:half], "seq", z_shift(1))
    far_bottom = lax.ppermute(down[half:], "seq", z_shift(-1))
    return found + [(Z // 2, jnp.concatenate([far_top, far_bottom], axis=0))]


def body(
    queries, self_keys, self_values, cross_queries, context, key_weight, value_weight, lengths
):
    prompt, seq = lax.axis_index("prompt"), lax.axis_index("seq")
    y, x_hi, core = prompt // 4, (prompt // 2) % 2, prompt % 2
    z, x_lo = seq // 2, seq % 2
    parts = lax.axis_size("seq")
    width = queries.shape[2] // parts

    def to_heads(packed):
        heads = lax.all_to_all(packed, "seq", split_axis=0, concat_axis=0)
        return heads.reshape(-1, packed.shape[2])

    chunk = gather_weights(jnp.concatenate([key_weight, value_weight], axis=1), x_hi, core)
    text = context[0]
    text_rows, depth = text.shape
    piece = depth // (Y * CORE)
    rolled = lax.dynamic_slice(
        jnp.concatenate([text, text], axis=1), (0, y * (CORE * piece)), text.shape
    )
    halves = [
        jnp.concatenate(
            [rolled[:, (2 * k + h) * piece : (2 * k + h + 1) * piece] for k in range(Y)], axis=1
        )
        for h in range(CORE)
    ]
    mine = jnp.where(core == 0, halves[0], halves[1])
    theirs = jnp.where(core == 0, halves[1], halves[0])
    block = jnp.stack([mine, lax.ppermute(theirs, "prompt", CORE_SWAP)])

    qkv = to_heads(pack([queries[0], self_keys[0], self_values[0]], parts))
    weights = ring_y(chunk)
    found = ring_z(block.reshape(CORE * text_rows, -1))
    all_text = jnp.stack([rows.reshape(CORE, text_rows, -1) for _, rows in found], axis=1)
    offsets = jnp.array([offset for offset, _ in found], jnp.int32)
    slots = Z * text_rows
    partial = jnp.dot(
        all_text.reshape(CORE * slots, -1), weights, preferred_element_type=jnp.float32
    )
    from_core = lax.ppermute(partial[slots:], "prompt", CORE_SWAP)
    summed = (partial[:slots] + from_core).astype(jnp.bfloat16)
    own_columns, their_columns = summed[:, : 2 * width], summed[:, 2 * width :]
    text_kv = jnp.concatenate(
        [own_columns, lax.ppermute(their_columns, "seq", XL_SWAP)], axis=0
    )
    source_z = (z + offsets) % Z
    source_seq = jnp.stack([source_z * 2 + x_lo, source_z * 2 + 1 - x_lo]).reshape(-1, 1)
    slot = (source_seq * text_rows + jnp.arange(text_rows, dtype=jnp.int32)[None, :]).reshape(1, -1)
    bias = jnp.where(slot < lengths[0], 0.0, -jnp.inf).astype(jnp.float32)

    cq = to_heads(pack([cross_queries[0]], parts))
    self_out = self_attend(qkv, width)
    attended = cross_attend(bias, cq, text_kv, self_out)
    back = lax.all_to_all(
        attended.reshape(parts, -1, width), "seq", split_axis=0, concat_axis=0
    )
    return unpack(back)[None]


def solution(mesh):
    in_specs = (
        P("prompt", "seq", None),
        P("prompt", "seq", None),
        P("prompt", "seq", None),
        P("prompt", "seq", None),
        P("prompt", "seq", None),
        P("prompt", "seq"),
        P("prompt", "seq"),
        P("prompt"),
    )
    out_specs = P("prompt", "seq", None)
    return jax.shard_map(body, mesh=mesh, in_specs=in_specs, out_specs=out_specs, check_vma=False)
```

time: 342 us -> 268 us (0.78)
  the two profiles are of different devices: /device:TPU:8 before, /device:TPU:28 now
where the time goes in v2:
time: 268 us; the launch traced here: 266 us
  waiting for transfers between devices  124 us (46%)
  Pallas kernels  46.7 us (17%)
  starting transfers between devices  39.3 us (15%)
  blocking collectives  32.9 us (12%)
  local copies, waits for them, and re-layouts  12.3 us (5%)
  other arithmetic  6.75 us (3%)
  matrix products  2.87 us (1%)
    ppermute x3, waiting for transfers between devices, ring_z(): up = lax.ppermute(up, 'seq', z_shift(1))  76.3 us
    all_to_all x1, blocking collectives, body(): lax.all_to_all(attended.reshape(parts, -1, width), 'seq', split_axis=0, c...  32.9 us
    ppermute x1, waiting for transfers between devices, ring_y(): before = lax.ppermute(chunk, 'prompt', y_shift(1))  21.4 us
    pallas_call x2, Pallas kernels, pack(): pl.pallas_call(pack_kernel, grid=(parts,), in_specs=[pl.BlockSpec((rows,...  18.6 us
    all_to_all x2, starting transfers between devices, to_heads(): heads = lax.all_to_all(packed, 'seq', split_axis=0, concat_axis=0)  16.6 us
    pallas_call x1, Pallas kernels, self_attend(): pl.pallas_call(self_kernel, grid=(rows // block,), in_specs=[pl.BlockSpec...  14.8 us
    ppermute x1, waiting for transfers between devices, ring_y(): far_top = lax.ppermute(before[:half], 'prompt', y_shift(1))  11.6 us
    pallas_call x1, Pallas kernels, unpack(): pl.pallas_call(unpack_kernel, grid=(parts,), in_specs=[pl.BlockSpec((1, r...  8.86 us
  transfers between devices with their start and end apart: 20, of which 10 were waited for; matrix products, arithmetic and copies ran while one was open for 6% of the time, Pallas kernels for 13%

profile of v2, /device:TPU:28, one launch (start us, length us, event | category | flops | bytes accessed | tf_op | source)
XLA Modules:
  0.0 265.9 jit_solution(950537547570500482)
XLA Ops:
  0.0 1.8 pad_maximum_fusion.5
  5.5 9.7 %pack.3 = bf16[16,128,768]{2,1,0:T(8,128)(2,1)} custom-call(bf16[128,4096]{1,0:T(8,128)(2,1)} %bitcast.52, bf16[128,4096]{1,0:T(8,128)(2,1)} %bitcast.53, bf16[128,4096]{1,0:T(8,128)(2,1)} %bitcast.54), custom_call_target="tpu_custom_call" | custom-call | bytes 6291456 | tf_op jit(solution)/shard_map/pack/pallas_call | solution.py:41
  15.2 8.8 %all-to-all-start.1 = ((bf16[16,128,768]{2,1,0:T(8,128)(2,1)}), bf16[16,128,768]{2,1,0:T(8,128)(2,1)S(1)}, u32[]{:S(2)}, u32[]{:S(2)}) async-start(bf16[16,128,768]{2,1,0:T(8,128)(2,1)} %pack.3), calls=%async_computation.1 | async-start | bytes 6291456 | tf_op jit(solution)/shard_map/all_to_all | solution.py:195
  25.0 1.6 constant_dynamic-update-slice_fusion.9
  26.6 1.6 constant_dynamic-update-slice_fusion.8
  28.2 2.0 collective-permute-start.1
  31.5 1.7 constant_dynamic-update-slice_fusion.7
  33.3 1.9 collective-permute-start.10
  35.3 67.3 %collective-permute-done.1 = bf16[64,2560]{1,0:T(8,128)(2,1)S(1)} collective-permute-done((bf16[64,2560]{1,0:T(8,128)(2,1)S(1)}, bf16[64,2560]{1,0:T(8,128)(2,1)S(1)}, u32[]{:S(2)}, u32[]{:S(2)}) %collective-permute-start.1) | collective-permute-done | bytes 327712 | tf_op jit(solution)/shard_map/ppermute | solution.py:177
  102.7 2.1 collective-permute-done.2
  106.0 7.0 %collective-permute-done.3 = bf16[64,2560]{1,0:T(8,128)(2,1)S(1)} collective-permute-done((bf16[64,2560]{1,0:T(8,128)(2,1)S(1)}, bf16[64,2560]{1,0:T(8,128)(2,1)S(1)}, u32[]{:S(2)}, u32[]{:S(2)}) %collective-permute-start.3) | collective-permute-done | bytes 327712 | tf_op jit(solution)/shard_map/ppermute | solution.py:177
  113.9 2.3 collective-permute-start.6
  117.7 2.5 collective-permute-start.13
  120.3 2.0 collective-permute-done.5
  122.4 3.3 %collective-permute-start.8 = (bf16[32,2560]{1,0:T(8,128)(2,1)S(1)}, bf16[32,2560]{1,0:T(8,128)(2,1)S(1)}, u32[]{:S(2)}, u32[]{:S(2)}) collective-permute-start(bf16[32,2560]{1,0:T(8,128)(2,1)S(1)} %slice.73), channel_id=1, source_target_pairs={{0,14},{1,15},{2,0},{3,1},{4,2},{5,3},{6,4},{7,5},{8,6},{9,7},{10,... | collective-permute-start | bytes 491528 | tf_op jit(solution)/shard_map/ppermute | solution.py:181
  125.7 21.4 %collective-permute-done.13 = bf16[640,1024]{1,0:T(8,128)(2,1)S(1)} collective-permute-done((bf16[640,1024]{1,0:T(8,128)(2,1)S(1)}, bf16[640,1024]{1,0:T(8,128)(2,1)S(1)}, u32[]{:S(2)}, u32[]{:S(2)}) %collective-permute-start.13) | collective-permute-done | bytes 1310752 | tf_op jit(solution)/shard_map/ppermute | solution.py:165
  147.2 4.0 %collective-permute-start.14 = (bf16[320,1024]{1,0:T(8,128)(2,1)S(1)}, bf16[320,1024]{1,0:T(8,128)(2,1)S(1)}, u32[]{:S(2)}, u32[]{:S(2)}) collective-permute-start(bf16[320,1024]{1,0:T(8,128)(2,1)S(1)} %slice.74), channel_id=1, source_target_pairs={{0,64},{16,80},{32,96},{48,112},{64,128},{80,144},{96,160},{112,17... | collective-permute-start | bytes 1966088 | tf_op jit(solution)/shard_map/ppermute | solution.py:167
  151.5 11.6 %collective-permute-done.14 = bf16[320,1024]{1,0:T(8,128)(2,1)S(1)} collective-permute-done((bf16[320,1024]{1,0:T(8,128)(2,1)S(1)}, bf16[320,1024]{1,0:T(8,128)(2,1)S(1)}, u32[]{:S(2)}, u32[]{:S(2)}) %collective-permute-start.14) | collective-permute-done | bytes 655392 | tf_op jit(solution)/shard_map/ppermute | solution.py:167
  163.1 3.5 %collective-permute-done.15 = bf16[320,1024]{1,0:T(8,128)(2,1)S(1)} collective-permute-done((bf16[320,1024]{1,0:T(8,128)(2,1)S(1)}, bf16[320,1024]{1,0:T(8,128)(2,1)S(1)}, u32[]{:S(2)}, u32[]{:S(2)}) %collective-permute-start.15) | collective-permute-done | bytes 655392 | tf_op jit(solution)/shard_map/ppermute | solution.py:168
  166.8 2.9 %fusion.7 = f32[512,1024]{1,0:T(8,128)S(1)} fusion(bf16[512,2560]{1,0:T(8,128)(2,1)S(1)} %bitcast.66, bf16[2560,1024]{1,0:T(8,128)(2,1)S(1)} %constant_dynamic-update-slice_fusion.10), kind=kOutput, calls=%fused_computation.50 | convolution fusion | flops 2684354560 | bytes 9961472 | tf_op jit(solution)/shard_map/dot_general | solution.py:221
  172.0 8.9 %pack.2 = bf16[16,128,256]{2,1,0:T(8,128)(2,1)} custom-call(bf16[128,4096]{1,0:T(8,128)(2,1)} %bitcast.51), custom_call_target="tpu_custom_call" | custom-call | bytes 2097152 | tf_op jit(solution)/shard_map/pack/pallas_call | solution.py:41
  180.9 1.6 copy-done
  182.5 7.7 %all-to-all-start = ((bf16[16,128,256]{2,1,0:T(8,128)(2,1)}), bf16[16,128,256]{2,1,0:T(8,128)(2,1)S(1)}, u32[]{:S(2)}, u32[]{:S(2)}) async-start(bf16[16,128,256]{2,1,0:T(8,128)(2,1)} %pack.2), calls=%async_computation | async-start | bytes 2097152 | tf_op jit(solution)/shard_map/all_to_all | solution.py:195
  190.4 1.4 fusion
  191.8 2.0 collective-permute-start.17
  194.6 5.8 %collective-permute-done.17 = bf16[256,512]{1,0:T(8,128)(2,1)S(1)} collective-permute-done((bf16[256,512]{1,0:T(8,128)(2,1)S(1)}, bf16[256,512]{1,0:T(8,128)(2,1)S(1)}, u32[]{:S(2)}, u32[]{:S(2)}) %collective-permute-start.17) | collective-permute-done | bytes 262176 | tf_op jit(solution)/shard_map/ppermute | solution.py:228
  200.5 1.9 copy-done.1
  202.4 14.8 %self_attend.1.self_ref = bf16[2048,256]{1,0:T(8,128)(2,1)S(1)} custom-call(bf16[2048,768]{1,0:T(8,128)(2,1)S(1)} %bitcast.47, bf16[2048,768]{1,0:T(8,128)(2,1)S(1)} %bitcast.48, bf16[2048,768]{1,0:T(8,128)(2,1)S(1)} %bitcast.49), custom_call_target="tpu_custom_call" | custom-call | flops 4294967296 | bytes 4194304 | tf_op jit(solution)/shard_map/self_attend/pallas_call | solution.py:105
  217.2 2.5 all-to-all-done
  219.7 4.4 %cross_attend.1 = bf16[2048,256]{1,0:T(8,128)(2,1)S(1)} custom-call(f32[1,512]{1,0:T(1,128)S(1)} %select_n.91.bias_ref, bf16[2048,256]{1,0:T(8,128)(2,1)S(1)} %bitcast.45, bf16[512,512]{1,0:T(8,128)(2,1)S(1)} %pad_maximum_fusion.2.tk_ref.tv_ref, bf16[512,512]{1,0:T(8,128)(2,1)S(1)} %pad_maximum_fusion.2.tk_ref.tv_ref, bf16[2048,256]{1,0:T(8,128)(2,1)S(1)} %self_attend.1.self_ref), custom_call_target="tpu_custom_call" | custom-call | flops 1073741824 | bytes 3145728 | tf_op jit(solution)/shard_map/cross_attend/pallas_call | solution.py:129
  224.1 32.9 %all_to_all.15.in_ref = bf16[16,128,256]{2,1,0:T(8,128)(2,1)} all-to-all(bf16[16,128,256]{2,1,0:T(8,128)(2,1)S(1)} %bitcast.46), channel_id=1, replica_groups=mesh['prompt'=16,'seq'=16] {'seq'}, dimensions={0} | all-to-all | bytes 2097152 | tf_op jit(solution)/shard_map/all_to_all | solution.py:238
  257.0 8.9 %unpack.1 = bf16[128,4096]{1,0:T(8,128)(2,1)} custom-call(bf16[16,128,256]{2,1,0:T(8,128)(2,1)} %all_to_all.15.in_ref), custom_call_target="tpu_custom_call" | custom-call | tf_op jit(solution)/shard_map/unpack/pallas_call | solution.py:60
  (63 shorter events, 13.3 us)
Async XLA Ops:
  1.8 29.8 %collective-permute-start.9 = (bf16[320,512]{1,0:T(8,128)(2,1)}, bf16[320,512]{1,0:T(8,128)(2,1)}, u32[]{:S(2)}, u32[]{:S(2)}) collective-permute-start(bf16[320,512]{1,0:T(8,128)(2,1)} %pad_maximum_fusion.5), channel_id=1, source_target_pairs={{0,1},{1,0},{2,3},{3,2},{4,5},{5,4},{6,7},{7,6},{8,9},{9,8},{10,11... | collective-permute-start | bytes 983048 | tf_op jit(solution)/shard_map/ppermute | solution.py:150
  5.5 22.7 %collective-permute-start = (bf16[32,2560]{1,0:T(8,128)(2,1)}, bf16[32,2560]{1,0:T(8,128)(2,1)S(1)}, u32[]{:S(2)}, u32[]{:S(2)}) collective-permute-start(bf16[32,2560]{1,0:T(8,128)(2,1)} %maximum_select_fusion.1), channel_id=1, source_target_pairs={{0,16},{16,0},{32,48},{48,32},{64,80},{80,64},{96,112},{112,96},{1... | collective-permute-start | bytes 491528 | tf_op jit(solution)/shard_map/ppermute | solution.py:213
  15.2 165.7 %all-to-all-start.1 = ((bf16[16,128,768]{2,1,0:T(8,128)(2,1)}), bf16[16,128,768]{2,1,0:T(8,128)(2,1)S(1)}, u32[]{:S(2)}, u32[]{:S(2)}) async-start(bf16[16,128,768]{2,1,0:T(8,128)(2,1)} %pack.3), calls=%async_computation.1 | async-start | bytes 6291456 | tf_op jit(solution)/shard_map/all_to_all | solution.py:195
  28.2 74.4 %collective-permute-start.1 = (bf16[64,2560]{1,0:T(8,128)(2,1)S(1)}, bf16[64,2560]{1,0:T(8,128)(2,1)S(1)}, u32[]{:S(2)}, u32[]{:S(2)}) collective-permute-start(bf16[64,2560]{1,0:T(8,128)(2,1)S(1)} %bitcast.63), channel_id=1, source_target_pairs={{0,2},{1,3},{2,4},{3,5},{4,6},{5,7},{6,8},{7,9},{8,10},{9,11},{10,... | collective-permute-start | bytes 983048 | tf_op jit(solution)/shard_map/ppermute | solution.py:177
  30.2 74.7 %collective-permute-start.2 = (bf16[64,2560]{1,0:T(8,128)(2,1)S(1)}, bf16[64,2560]{1,0:T(8,128)(2,1)S(1)}, u32[]{:S(2)}, u32[]{:S(2)}) collective-permute-start(bf16[64,2560]{1,0:T(8,128)(2,1)S(1)} %bitcast.64), channel_id=1, source_target_pairs={{0,14},{1,15},{2,0},{3,1},{4,2},{5,3},{6,4},{7,5},{8,6},{9,7},{10,... | collective-permute-start | bytes 983048 | tf_op jit(solution)/shard_map/ppermute | solution.py:178
  33.3 82.9 %collective-permute-start.10 = (bf16[320,1024]{1,0:T(8,128)(2,1)}, bf16[320,1024]{1,0:T(8,128)(2,1)S(1)}, u32[]{:S(2)}, u32[]{:S(2)}) collective-permute-start(bf16[320,1024]{1,0:T(8,128)(2,1)} %constant_dynamic-update-slice_fusion.7), channel_id=1, source_target_pairs={{16,32},{32,16},{80,96},{96,80},{144,160},{160,144},{208,224},{224... | collective-permute-start | bytes 1966088 | tf_op jit(solution)/shard_map/ppermute | solution.py:152
  35.2 81.1 %collective-permute-start.11 = (bf16[320,1024]{1,0:T(8,128)(2,1)}, bf16[320,1024]{1,0:T(8,128)(2,1)S(1)}, u32[]{:S(2)}, u32[]{:S(2)}) collective-permute-start(bf16[320,1024]{1,0:T(8,128)(2,1)} %constant_dynamic-update-slice_fusion.7), channel_id=1, source_target_pairs={{0,32},{32,48},{48,16},{16,0},{64,96},{96,112},{112,80},{80,64},{1... | collective-permute-start | bytes 1966088 | tf_op jit(solution)/shard_map/ppermute | solution.py:151
  102.6 10.3 %collective-permute-start.3 = (bf16[64,2560]{1,0:T(8,128)(2,1)S(1)}, bf16[64,2560]{1,0:T(8,128)(2,1)S(1)}, u32[]{:S(2)}, u32[]{:S(2)}) collective-permute-start(bf16[64,2560]{1,0:T(8,128)(2,1)S(1)} %collective-permute-done.1), channel_id=1, source_target_pairs={{0,2},{1,3},{2,4},{3,5},{4,6},{5,7},{6,8},{7,9},{8,10},{9,11},{10,... | collective-permute-start | bytes 983048 | tf_op jit(solution)/shard_map/ppermute | solution.py:177
  104.9 9.0 %collective-permute-start.4 = (bf16[64,2560]{1,0:T(8,128)(2,1)S(1)}, bf16[64,2560]{1,0:T(8,128)(2,1)S(1)}, u32[]{:S(2)}, u32[]{:S(2)}) collective-permute-start(bf16[64,2560]{1,0:T(8,128)(2,1)S(1)} %collective-permute-done.2), channel_id=1, source_target_pairs={{0,14},{1,15},{2,0},{3,1},{4,2},{5,3},{6,4},{7,5},{8,6},{9,7},{10,... | collective-permute-start | bytes 983048 | tf_op jit(solution)/shard_map/ppermute | solution.py:178
  112.9 9.3 %collective-permute-start.5 = (bf16[64,2560]{1,0:T(8,128)(2,1)S(1)}, bf16[64,2560]{1,0:T(8,128)(2,1)S(1)}, u32[]{:S(2)}, u32[]{:S(2)}) collective-permute-start(bf16[64,2560]{1,0:T(8,128)(2,1)S(1)} %collective-permute-done.3), channel_id=1, source_target_pairs={{0,2},{1,3},{2,4},{3,5},{4,6},{5,7},{6,8},{7,9},{8,10},{9,11},{10,... | collective-permute-start | bytes 983048 | tf_op jit(solution)/shard_map/ppermute | solution.py:177
  113.9 8.5 %collective-permute-start.6 = (bf16[64,2560]{1,0:T(8,128)(2,1)S(1)}, bf16[64,2560]{1,0:T(8,128)(2,1)S(1)}, u32[]{:S(2)}, u32[]{:S(2)}) collective-permute-start(bf16[64,2560]{1,0:T(8,128)(2,1)S(1)} %collective-permute-done.4), channel_id=1, source_target_pairs={{0,14},{1,15},{2,0},{3,1},{4,2},{5,3},{6,4},{7,5},{8,6},{9,7},{10,... | collective-permute-start | bytes 983048 | tf_op jit(solution)/shard_map/ppermute | solution.py:178
  116.9 34.2 %collective-permute-start.12 = (bf16[640,1024]{1,0:T(8,128)(2,1)S(1)}, bf16[640,1024]{1,0:T(8,128)(2,1)S(1)}, u32[]{:S(2)}, u32[]{:S(2)}) collective-permute-start(bf16[640,1024]{1,0:T(8,128)(2,1)S(1)} %get-tuple-element.6), channel_id=1, source_target_pairs={{0,192},{16,208},{32,224},{48,240},{64,0},{80,16},{96,32},{112,48}... | collective-permute-start | bytes 3932168 | tf_op jit(solution)/shard_map/ppermute | solution.py:166
  117.7 29.4 %collective-permute-start.13 = (bf16[640,1024]{1,0:T(8,128)(2,1)S(1)}, bf16[640,1024]{1,0:T(8,128)(2,1)S(1)}, u32[]{:S(2)}, u32[]{:S(2)}) collective-permute-start(bf16[640,1024]{1,0:T(8,128)(2,1)S(1)} %get-tuple-element.6), channel_id=1, source_target_pairs={{0,64},{16,80},{32,96},{48,112},{64,128},{80,144},{96,160},{112,17... | collective-permute-start | bytes 3932168 | tf_op jit(solution)/shard_map/ppermute | solution.py:165
  122.3 29.0 %collective-permute-start.7 = (bf16[32,2560]{1,0:T(8,128)(2,1)S(1)}, bf16[32,2560]{1,0:T(8,128)(2,1)S(1)}, u32[]{:S(2)}, u32[]{:S(2)}) collective-permute-start(bf16[32,2560]{1,0:T(8,128)(2,1)S(1)} %slice.72), channel_id=1, source_target_pairs={{0,2},{1,3},{2,4},{3,5},{4,6},{5,7},{6,8},{7,9},{8,10},{9,11},{10,... | collective-permute-start | bytes 491528 | tf_op jit(solution)/shard_map/ppermute | solution.py:180
  122.4 28.9 %collective-permute-start.8 = (bf16[32,2560]{1,0:T(8,128)(2,1)S(1)}, bf16[32,2560]{1,0:T(8,128)(2,1)S(1)}, u32[]{:S(2)}, u32[]{:S(2)}) collective-permute-start(bf16[32,2560]{1,0:T(8,128)(2,1)S(1)} %slice.73), channel_id=1, source_target_pairs={{0,14},{1,15},{2,0},{3,1},{4,2},{5,3},{6,4},{7,5},{8,6},{9,7},{10,... | collective-permute-start | bytes 491528 | tf_op jit(solution)/shard_map/ppermute | solution.py:181
  147.2 15.9 %collective-permute-start.14 = (bf16[320,1024]{1,0:T(8,128)(2,1)S(1)}, bf16[320,1024]{1,0:T(8,128)(2,1)S(1)}, u32[]{:S(2)}, u32[]{:S(2)}) collective-permute-start(bf16[320,1024]{1,0:T(8,128)(2,1)S(1)} %slice.74), channel_id=1, source_target_pairs={{0,64},{16,80},{32,96},{48,112},{64,128},{80,144},{96,160},{112,17... | collective-permute-start | bytes 1966088 | tf_op jit(solution)/shard_map/ppermute | solution.py:167
  151.2 15.5 %collective-permute-start.15 = (bf16[320,1024]{1,0:T(8,128)(2,1)S(1)}, bf16[320,1024]{1,0:T(8,128)(2,1)S(1)}, u32[]{:S(2)}, u32[]{:S(2)}) collective-permute-start(bf16[320,1024]{1,0:T(8,128)(2,1)S(1)} %slice.75), channel_id=1, source_target_pairs={{0,192},{16,208},{32,224},{48,240},{64,0},{80,16},{96,32},{112,48}... | collective-permute-start | bytes 1966088 | tf_op jit(solution)/shard_map/ppermute | solution.py:168
  169.6 1.4 copy-start.2
  172.0 18.3 %copy-start.4 = (s32[8]{0:T(128)S(1)}, s32[8]{0:T(128)}, u32[]{:S(2)}) copy-start(s32[8]{0:T(128)} %constant.85.clone) | copy-start | bytes 100
  172.0 18.3 %collective-permute-start.16 = (f32[256,1024]{1,0:T(8,128)}, f32[256,1024]{1,0:T(8,128)}, u32[]{:S(2)}, u32[]{:S(2)}) collective-permute-start(f32[256,1024]{1,0:T(8,128)} %slice.77), channel_id=1, source_target_pairs={{0,16},{16,0},{32,48},{48,32},{64,80},{80,64},{96,112},{112,96},{1... | collective-permute-start | bytes 3145736 | tf_op jit(solution)/shard_map/ppermute | solution.py:224
  180.9 1.6 copy-start
  182.5 7.8 %copy-start.3 = (f32[512,1024]{1,0:T(8,128)S(1)}, f32[512,1024]{1,0:T(8,128)}, u32[]{:S(2)}) copy-start(f32[512,1024]{1,0:T(8,128)} %copy-done.2) | copy-start | bytes 6291460
  182.5 37.2 %all-to-all-start = ((bf16[16,128,256]{2,1,0:T(8,128)(2,1)}), bf16[16,128,256]{2,1,0:T(8,128)(2,1)S(1)}, u32[]{:S(2)}, u32[]{:S(2)}) async-start(bf16[16,128,256]{2,1,0:T(8,128)(2,1)} %pack.2), calls=%async_computation | async-start | bytes 2097152 | tf_op jit(solution)/shard_map/all_to_all | solution.py:195
  191.8 8.7 %collective-permute-start.17 = (bf16[256,512]{1,0:T(8,128)(2,1)S(1)}, bf16[256,512]{1,0:T(8,128)(2,1)S(1)}, u32[]{:S(2)}, u32[]{:S(2)}) collective-permute-start(bf16[256,512]{1,0:T(8,128)(2,1)S(1)} %get-tuple-element.10), channel_id=1, source_target_pairs={{0,1},{1,0},{2,3},{3,2},{4,5},{5,4},{6,7},{7,6},{8,9},{9,8},{10,11... | collective-permute-start | bytes 786440 | tf_op jit(solution)/shard_map/ppermute | solution.py:228
  200.5 1.9 copy-start.1

commit v3 on v2

--- a/solution.py
+++ b/solution.py
@@ -1,3 +1,4 @@
+import functools
 import math
 
 import jax
@@ -28,21 +29,24 @@
 REGROUP_B = [(4 * y + a, 4 * y + b) for y in range(Y) for a, b in ((1, 2), (2, 1))]
 
 
-def pack_kernel(*refs):
+def pack_kernel(width, parts, *refs):
     out_ref = refs[-1]
-    width = refs[0].shape[1]
     for place, ref in enumerate(refs[:-1]):
-        out_ref[0, :, place * width : (place + 1) * width] = ref[...]
+        for part in range(parts):
+            out_ref[part, :, place * width : (place + 1) * width] = ref[
+                :, part * width : (part + 1) * width
+            ]
 
 
 def pack(arrays, parts):
     rows, columns = arrays[0].shape
     width = columns // parts
-    return pl.pallas_call(
-        pack_kernel,
-        grid=(parts,),
-        in_specs=[pl.BlockSpec((rows, width), lambda i: (0, i)) for _ in arrays],
-        out_specs=pl.BlockSpec((1, rows, width * len(arrays)), lambda i: (i, 0, 0)),
+    block = math.gcd(rows, 64)
+    return pl.pallas_call(
+        functools.partial(pack_kernel, width, parts),
+        grid=(rows // block,),
+        in_specs=[pl.BlockSpec((block, columns), lambda i: (i, 0)) for _ in arrays],
+        out_specs=pl.BlockSpec((parts, block, width * len(arrays)), lambda i: (0, i, 0)),
         out_shape=jax.ShapeDtypeStruct((parts, rows, width * len(arrays)), jnp.bfloat16),
         cost_estimate=pl.CostEstimate(
             flops=0, bytes_accessed=4 * rows * columns * len(arrays), transcendentals=0
@@ -51,17 +55,36 @@
     )(*arrays)
 
 
+def hold_kernel(*refs):
+    del refs
+
+
+def hold(array, *until):
+    marks = [mark[:16, :HD] for mark in until]
+    return pl.pallas_call(
+        hold_kernel,
+        in_specs=[pl.BlockSpec(memory_space=pl.ANY)] * (1 + len(marks)),
+        out_specs=pl.BlockSpec(memory_space=pl.ANY),
+        out_shape=jax.ShapeDtypeStruct(array.shape, array.dtype),
+        input_output_aliases={0: 0},
+        name="hold",
+    )(array, *marks)
+
+
 def unpack_kernel(in_ref, out_ref):
-    out_ref[...] = in_ref[0]
+    parts, _, width = in_ref.shape
+    for part in range(parts):
+        out_ref[:, part * width : (part + 1) * width] = in_ref[part]
 
 
 def unpack(blocks):
     parts, rows, width = blocks.shape
+    block = math.gcd(rows, 128)
     return pl.pallas_call(
         unpack_kernel,
-        grid=(parts,),
-        in_specs=[pl.BlockSpec((1, rows, width), lambda i: (i, 0, 0))],
-        out_specs=pl.BlockSpec((rows, width), lambda i: (0, i)),
+        grid=(rows // block,),
+        in_specs=[pl.BlockSpec((parts, block, width), lambda i: (0, i, 0))],
+        out_specs=pl.BlockSpec((block, parts * width), lambda i: (i, 0)),
         out_shape=jax.ShapeDtypeStruct((rows, parts * width), jnp.bfloat16),
         name="unpack",
     )(blocks)
@@ -171,15 +194,54 @@
 
 def ring_z(block):
     half = block.shape[0] // 2
-    found = [(0, block)]
+    offsets, pieces = [0], [block]
     up = down = block
     for step in range(1, Z // 2):
         up = lax.ppermute(up, "seq", z_shift(1))
         down = lax.ppermute(down, "seq", z_shift(-1))
-        found += [(-step, up), (step, down)]
-    far_top = lax.ppermute(up[:half], "seq", z_shift(1))
-    far_bottom = lax.ppermute(down[half:], "seq", z_shift(-1))
-    return found + [(Z // 2, jnp.concatenate([far_top, far_bottom], axis=0))]
+        offsets += [-step, step]
+        pieces += [up, down]
+    pieces.append(lax.ppermute(up[:half], "seq", z_shift(1)))
+    pieces.append(lax.ppermute(down[half:], "seq", z_shift(-1)))
+    return offsets + [Z // 2], pieces
+
+
+def split_kernel(count, where_ref, *refs):
+    del where_ref
+    for half in range(CORE):
+        place = 0
+        for ref in refs[half * count : (half + 1) * count]:
+            refs[CORE * count + half][place : place + ref.shape[0], :] = ref[...]
+            place += ref.shape[0]
+
+
+def split_text(pieces, y, core):
+    depth = pieces[0].shape[1]
+    rows = sum(piece.shape[0] for piece in pieces)
+    wide = depth // (Y * CORE)
+
+    def chunk(flip):
+        def place(k, where):
+            return 0, ((where[0] + k) % Y) * CORE + (where[1] + flip) % CORE
+
+        return [pl.BlockSpec((piece.shape[0], wide), place) for piece in pieces]
+
+    shape = jax.ShapeDtypeStruct((rows, Y * wide), jnp.bfloat16)
+    spec = pl.BlockSpec((rows, wide), lambda k, where: (0, k))
+    return pl.pallas_call(
+        functools.partial(split_kernel, len(pieces)),
+        grid_spec=pltpu.PrefetchScalarGridSpec(
+            num_scalar_prefetch=1,
+            grid=(Y,),
+            in_specs=chunk(0) + chunk(1),
+            out_specs=[spec, spec],
+        ),
+        out_shape=[shape, shape],
+        cost_estimate=pl.CostEstimate(
+            flops=0, bytes_accessed=4 * rows * depth, transcendentals=0
+        ),
+        name="split_text",
+    )(jnp.stack([y, core]), *pieces, *pieces)
 
 
 def body(
@@ -195,39 +257,22 @@
         heads = lax.all_to_all(packed, "seq", split_axis=0, concat_axis=0)
         return heads.reshape(-1, packed.shape[2])
 
+    offsets, pieces = ring_z(context[0])
     chunk = gather_weights(jnp.concatenate([key_weight, value_weight], axis=1), x_hi, core)
-    text = context[0]
-    text_rows, depth = text.shape
-    piece = depth // (Y * CORE)
-    rolled = lax.dynamic_slice(
-        jnp.concatenate([text, text], axis=1), (0, y * (CORE * piece)), text.shape
-    )
-    halves = [
-        jnp.concatenate(
-            [rolled[:, (2 * k + h) * piece : (2 * k + h + 1) * piece] for k in range(Y)], axis=1
-        )
-        for h in range(CORE)
-    ]
-    mine = jnp.where(core == 0, halves[0], halves[1])
-    theirs = jnp.where(core == 0, halves[1], halves[0])
-    block = jnp.stack([mine, lax.ppermute(theirs, "prompt", CORE_SWAP)])
-
-    qkv = to_heads(pack([queries[0], self_keys[0], self_values[0]], parts))
+    packed = pack([queries[0], self_keys[0], self_values[0]], parts)
+    qkv = to_heads(hold(packed, chunk, *pieces[-4:]))
     weights = ring_y(chunk)
-    found = ring_z(block.reshape(CORE * text_rows, -1))
-    all_text = jnp.stack([rows.reshape(CORE, text_rows, -1) for _, rows in found], axis=1)
-    offsets = jnp.array([offset for offset, _ in found], jnp.int32)
-    slots = Z * text_rows
-    partial = jnp.dot(
-        all_text.reshape(CORE * slots, -1), weights, preferred_element_type=jnp.float32
-    )
-    from_core = lax.ppermute(partial[slots:], "prompt", CORE_SWAP)
-    summed = (partial[:slots] + from_core).astype(jnp.bfloat16)
+    text_rows = context.shape[1]
+    mine, theirs = split_text(pieces, y, core)
+    other = lax.ppermute(theirs, "prompt", CORE_SWAP)
+    other_part = jnp.dot(other, weights, preferred_element_type=jnp.float32)
+    own_part = jnp.dot(mine, weights, preferred_element_type=jnp.float32)
+    summed = (own_part + lax.ppermute(other_part, "prompt", CORE_SWAP)).astype(jnp.bfloat16)
     own_columns, their_columns = summed[:, : 2 * width], summed[:, 2 * width :]
     text_kv = jnp.concatenate(
         [own_columns, lax.ppermute(their_columns, "seq", XL_SWAP)], axis=0
     )
-    source_z = (z + offsets) % Z
+    source_z = (z + jnp.array(offsets, jnp.int32)) % Z
     source_seq = jnp.stack([source_z * 2 + x_lo, source_z * 2 + 1 - x_lo]).reshape(-1, 1)
     slot = (source_seq * text_rows + jnp.arange(text_rows, dtype=jnp.int32)[None, :]).reshape(1, -1)
     bias = jnp.where(slot < lengths[0], 0.0, -jnp.inf).astype(jnp.float32)

time: 268 us -> 203 us (0.76)
  the two profiles are of different devices: /device:TPU:28 before, /device:TPU:8 now
where the time goes in v3:
time: 203 us; the launch traced here: 202 us
  waiting for transfers between devices  62 us (31%)
  starting transfers between devices  40.1 us (20%)
  blocking collectives  34.8 us (17%)
  Pallas kernels  31.7 us (16%)
  local copies, waits for them, and re-layouts  17.9 us (9%)
  matrix products  9.77 us (5%)
  other arithmetic  4.77 us (2%)
    all_to_all x1, blocking collectives, body(): lax.all_to_all(attended.reshape(parts, -1, width), 'seq', split_axis=0, c...  34.8 us
    ppermute x1, waiting for transfers between devices, ring_y(): before = lax.ppermute(chunk, 'prompt', y_shift(1))  23.8 us
    pallas_call x1, Pallas kernels, self_attend(): pl.pallas_call(self_kernel, grid=(rows // block,), in_specs=[pl.BlockSpec...  14.8 us
    all_to_all x2, waiting for transfers between devices, to_heads(): heads = lax.all_to_all(packed, 'seq', split_axis=0, concat_axis=0)  12.7 us
    all_to_all x2, starting transfers between devices, to_heads(): heads = lax.all_to_all(packed, 'seq', split_axis=0, concat_axis=0)  11.1 us
    ppermute x1, waiting for transfers between devices, ring_y(): far_top = lax.ppermute(before[:half], 'prompt', y_shift(1))  10.5 us
    ppermute x3, starting transfers between devices, ring_z(): down = lax.ppermute(down, 'seq', z_shift(-1))  10.5 us
    unnamed x29, local copies, waits for them, and re-layouts  9.78 us
  transfers between devices with their start and end apart: 20, of which 8 were waited for; matrix products, arithmetic and copies ran while one was open for 14% of the time, Pallas kernels for 12%

profile of v3, /device:TPU:8, one launch (start us, length us, event | category | flops | bytes accessed | tf_op | source)
XLA Modules:
  0.0 201.8 jit_solution(9864867644679999253)
XLA Ops:
  0.0 1.9 collective-permute-start
  1.9 3.9 %collective-permute-start.1 = (bf16[32,5120]{1,0:T(8,128)(2,1)}, bf16[32,5120]{1,0:T(8,128)(2,1)S(1)}, u32[]{:S(2)}, u32[]{:S(2)}) collective-permute-start(bf16[32,5120]{1,0:T(8,128)(2,1)} %bitcast.27), channel_id=1, source_target_pairs={{0,14},{1,15},{2,0},{3,1},{4,2},{5,3},{6,4},{7,5},{8,6},{9,7},{10,... | collective-permute-start | bytes 983048 | tf_op jit(solution)/shard_map/ppermute | solution.py:201
  10.3 3.4 %collective-permute-done.refs_1_.refs_10_ = bf16[32,5120]{1,0:T(8,128)(2,1)S(1)} collective-permute-done((bf16[32,5120]{1,0:T(8,128)(2,1)}, bf16[32,5120]{1,0:T(8,128)(2,1)S(1)}, u32[]{:S(2)}, u32[]{:S(2)}) %collective-permute-start) | collective-permute-done | bytes 327712 | tf_op jit(solution)/shard_map/ppermute | solution.py:200
  13.8 3.2 %collective-permute-start.3 = (bf16[32,5120]{1,0:T(8,128)(2,1)S(1)}, bf16[32,5120]{1,0:T(8,128)(2,1)S(1)}, u32[]{:S(2)}, u32[]{:S(2)}) collective-permute-start(bf16[32,5120]{1,0:T(8,128)(2,1)S(1)} %collective-permute-done.1.refs_2_.refs_11_), channel_id=1, source_target_pairs={{0,14},{1,15},{2,0},{3,1},{4,2},{5,3},{6,4},{7,5},{8,6},{9,7},{10,... | collective-permute-start | bytes 983048 | tf_op jit(solution)/shard_map/ppermute | solution.py:201
  17.8 4.3 %collective-permute-start.10 = (bf16[320,1024]{1,0:T(8,128)(2,1)S(1)}, bf16[320,1024]{1,0:T(8,128)(2,1)}, u32[]{:S(2)}, u32[]{:S(2)}) collective-permute-start(bf16[320,1024]{1,0:T(8,128)(2,1)S(1)} %constant_dynamic-update-slice_fusion), channel_id=1, source_target_pairs={{0,32},{32,48},{48,16},{16,0},{64,96},{96,112},{112,80},{80,64},{1... | collective-permute-start | bytes 1966088 | tf_op jit(solution)/shard_map/ppermute | solution.py:174
  22.1 1.8 collective-permute-done.2.refs_3_.refs_12_
  23.9 3.3 %collective-permute-start.5 = (bf16[32,5120]{1,0:T(8,128)(2,1)S(1)}, bf16[32,5120]{1,0:T(8,128)(2,1)S(1)}, u32[]{:S(2)}, u32[]{:S(2)}) collective-permute-start(bf16[32,5120]{1,0:T(8,128)(2,1)S(1)} %collective-permute-done.3.refs_4_.refs_13_), channel_id=1, source_target_pairs={{0,14},{1,15},{2,0},{3,1},{4,2},{5,3},{6,4},{7,5},{8,6},{9,7},{10,... | collective-permute-start | bytes 983048 | tf_op jit(solution)/shard_map/ppermute | solution.py:201
  27.2 3.2 %pack.3.refs_0_ = bf16[16,128,768]{2,1,0:T(8,128)(2,1)} custom-call(bf16[128,4096]{1,0:T(8,128)(2,1)} %bitcast.31, bf16[128,4096]{1,0:T(8,128)(2,1)} %bitcast.32, bf16[128,4096]{1,0:T(8,128)(2,1)} %bitcast.33), custom_call_target="tpu_custom_call" | custom-call | bytes 6291456 | tf_op jit(solution)/shard_map/pack/pallas_call | solution.py:45
  30.4 2.8 %collective-permute-done.4.refs_5_.refs_14_ = bf16[32,5120]{1,0:T(8,128)(2,1)S(1)} collective-permute-done((bf16[32,5120]{1,0:T(8,128)(2,1)S(1)}, bf16[32,5120]{1,0:T(8,128)(2,1)S(1)}, u32[]{:S(2)}, u32[]{:S(2)}) %collective-permute-start.4) | collective-permute-done | bytes 327712 | tf_op jit(solution)/shard_map/ppermute | solution.py:200
  33.3 3.3 %collective-permute-start.7 = (bf16[16,5120]{1,0:T(8,128)(2,1)S(1)}, bf16[16,5120]{1,0:T(8,128)(2,1)S(1)}, u32[]{:S(2)}, u32[]{:S(2)}) collective-permute-start(bf16[16,5120]{1,0:T(8,128)(2,1)S(1)} %slice.45), channel_id=1, source_target_pairs={{0,14},{1,15},{2,0},{3,1},{4,2},{5,3},{6,4},{7,5},{8,6},{9,7},{10,... | collective-permute-start | bytes 491528 | tf_op jit(solution)/shard_map/ppermute | solution.py:205
  36.7 3.0 %constant_dynamic-update-slice_fusion.7 = (bf16[2560,1024]{1,0:T(8,128)(2,1)}, bf16[640,1024]{1,0:T(8,128)(2,1)S(1)}) fusion(bf16[320,1024]{1,0:T(8,128)(2,1)S(1)} %broadcast_select_fusion, bf16[320,1024]{1,0:T(8,128)(2,1)} %collective-permute-done.10, pred[]{:T(512)S(6)} %eq.13, pred[]{:T(512)S(6)} %eq.12), kind=kLoop, calls=%fused_computation.15 | loop fusion | flops 7208959 | bytes 3932162
  42.8 5.9 %all-to-all-start.1 = ((bf16[16,128,768]{2,1,0:T(8,128)(2,1)}), bf16[16,128,768]{2,1,0:T(8,128)(2,1)S(1)}, u32[]{:S(2)}, u32[]{:S(2)}) async-start(bf16[16,128,768]{2,1,0:T(8,128)(2,1)} %hold.1), calls=%async_computation.1 | async-start | bytes 6291456 | tf_op jit(solution)/shard_map/all_to_all | solution.py:257
  48.7 1.7 collective-permute-start.12
  51.3 4.9 %split_text.1 = (bf16[256,2560]{1,0:T(8,128)(2,1)}, bf16[256,2560]{1,0:T(8,128)(2,1)}) custom-call(s32[2]{0:T(128)} %pad_add_fusion.where_ref, bf16[32,5120]{1,0:T(8,128)(2,1)} %bitcast.28, bf16[32,5120]{1,0:T(8,128)(2,1)} %copy-done.5, bf16[32,5120]{1,0:T(8,128)(2,1)} %copy-done.6, bf16[32,5120]{1,0:T(8,128)(2,1)} %copy-done.7, bf16[32,5120]{1,0:T(8,128)(2,1)} %copy-done.8, ...), custom_call_target="tpu_custom_call" | custom-call | bytes 5242880 | tf_op jit(solution)/shard_map/split_text/pallas_call | solution.py:231
  56.3 23.8 %collective-permute-done.12 = bf16[640,1024]{1,0:T(8,128)(2,1)} collective-permute-done((bf16[640,1024]{1,0:T(8,128)(2,1)}, bf16[640,1024]{1,0:T(8,128)(2,1)}, u32[]{:S(2)}, u32[]{:S(2)}) %collective-permute-start.12) | collective-permute-done | bytes 1310752 | tf_op jit(solution)/shard_map/ppermute | solution.py:188
  81.2 1.8 collective-permute-start.13
  84.7 2.5 %constant_dynamic-update-slice_fusion.6 = bf16[2560,1024]{1,0:T(8,128)(2,1)} fusion(bf16[2560,1024]{1,0:T(8,128)(2,1)} %get-tuple-element.9, bf16[640,1024]{1,0:T(8,128)(2,1)} %collective-permute-done.11), kind=kLoop, calls=%fused_computation.14 | loop fusion | bytes 2621440
  87.2 10.5 %collective-permute-done.13 = bf16[320,1024]{1,0:T(8,128)(2,1)S(1)} collective-permute-done((bf16[320,1024]{1,0:T(8,128)(2,1)S(1)}, bf16[320,1024]{1,0:T(8,128)(2,1)S(1)}, u32[]{:S(2)}, u32[]{:S(2)}) %collective-permute-start.13) | collective-permute-done | bytes 655392 | tf_op jit(solution)/shard_map/ppermute | solution.py:190
  101.1 2.5 %constant_dynamic-update-slice_fusion.3 = bf16[2560,1024]{1,0:T(8,128)(2,1)} fusion(bf16[2560,1024]{1,0:T(8,128)(2,1)} %constant_dynamic-update-slice_fusion.4, bf16[640,1024]{1,0:T(8,128)(2,1)} %collective-permute-done.12), kind=kLoop, calls=%fused_computation.11 | loop fusion | bytes 2621440 | tf_op jit(solution)/shard_map/concatenate | solution.py:192
  103.6 5.1 %fusion.6 = f32[256,1024]{1,0:T(8,128)} fusion(bf16[256,2560]{1,0:T(8,128)(2,1)S(1)} %collective-permute-done.15, bf16[2560,1024]{1,0:T(8,128)(2,1)} %constant_dynamic-update-slice_fusion.3), kind=kOutput, calls=%fused_computation.28 | convolution fusion | flops 1342177280 | bytes 7602176 | tf_op jit(solution)/shard_map/dot_general | solution.py:268
  108.7 2.1 %pack.2 = bf16[16,128,256]{2,1,0:T(8,128)(2,1)} custom-call(bf16[128,4096]{1,0:T(8,128)(2,1)} %bitcast.30), custom_call_target="tpu_custom_call" | custom-call | bytes 2097152 | tf_op jit(solution)/shard_map/pack/pallas_call | solution.py:45
  110.7 12.7 %all-to-all-done.1 = bf16[16,128,768]{2,1,0:T(8,128)(2,1)S(1)} async-done(((bf16[16,128,768]{2,1,0:T(8,128)(2,1)}), bf16[16,128,768]{2,1,0:T(8,128)(2,1)S(1)}, u32[]{:S(2)}, u32[]{:S(2)}) %all-to-all-start.1) | async-done | bytes 3145760 | tf_op jit(solution)/shard_map/all_to_all | solution.py:257
  123.4 1.7 copy-done
  125.1 5.3 %all-to-all-start = ((bf16[16,128,256]{2,1,0:T(8,128)(2,1)}), bf16[16,128,256]{2,1,0:T(8,128)(2,1)S(1)}, u32[]{:S(2)}, u32[]{:S(2)}) async-start(bf16[16,128,256]{2,1,0:T(8,128)(2,1)} %pack.2), calls=%async_computation | async-start | bytes 2097152 | tf_op jit(solution)/shard_map/all_to_all | solution.py:257
  130.4 4.7 %fusion = bf16[256,1024]{1,0:T(8,128)(2,1)S(1)} fusion(f32[256,1024]{1,0:T(8,128)} %collective-permute-done.16, bf16[256,2560]{1,0:T(8,128)(2,1)} %get-tuple-element.7, bf16[2560,1024]{1,0:T(8,128)(2,1)} %constant_dynamic-update-slice_fusion.3), kind=kOutput, calls=%fused_computation.4 | convolution fusion | flops 1342701568 | bytes 8126464 | tf_op jit(solution)/shard_map/dot_general | solution.py:269
  135.2 2.0 collective-permute-start.17
  138.1 5.4 %collective-permute-done.17 = bf16[256,512]{1,0:T(8,128)(2,1)S(1)} collective-permute-done((bf16[256,512]{1,0:T(8,128)(2,1)S(1)}, bf16[256,512]{1,0:T(8,128)(2,1)S(1)}, u32[]{:S(2)}, u32[]{:S(2)}) %collective-permute-start.17) | collective-permute-done | bytes 262176 | tf_op jit(solution)/shard_map/ppermute | solution.py:273
  143.5 1.9 copy-done.1
  145.4 14.8 %self_attend.1.self_ref = bf16[2048,256]{1,0:T(8,128)(2,1)S(1)} custom-call(bf16[2048,768]{1,0:T(8,128)(2,1)S(1)} %bitcast.23, bf16[2048,768]{1,0:T(8,128)(2,1)S(1)} %bitcast.24, bf16[2048,768]{1,0:T(8,128)(2,1)S(1)} %bitcast.25), custom_call_target="tpu_custom_call" | custom-call | flops 4294967296 | bytes 4194304 | tf_op jit(solution)/shard_map/self_attend/pallas_call | solution.py:128
  160.3 4.5 %cross_attend.1 = bf16[2048,256]{1,0:T(8,128)(2,1)S(1)} custom-call(f32[1,512]{1,0:T(1,128)S(1)} %select_n.67.bias_ref, bf16[2048,256]{1,0:T(8,128)(2,1)S(1)} %bitcast.21, bf16[512,512]{1,0:T(8,128)(2,1)S(1)} %pad_maximum_fusion.2.tk_ref.tv_ref, bf16[512,512]{1,0:T(8,128)(2,1)S(1)} %pad_maximum_fusion.2.tk_ref.tv_ref, bf16[2048,256]{1,0:T(8,128)(2,1)S(1)} %self_attend.1.self_ref), custom_call_target="tpu_custom_call" | custom-call | flops 1073741824 | bytes 3145728 | tf_op jit(solution)/shard_map/cross_attend/pallas_call | solution.py:152
  164.7 34.8 %all_to_all.15.in_ref = bf16[16,128,256]{2,1,0:T(8,128)(2,1)} all-to-all(bf16[16,128,256]{2,1,0:T(8,128)(2,1)S(1)} %bitcast.22), channel_id=1, replica_groups=mesh['prompt'=16,'seq'=16] {'seq'}, dimensions={0} | all-to-all | bytes 2097152 | tf_op jit(solution)/shard_map/all_to_all | solution.py:283
  199.5 2.3 %unpack.1 = bf16[128,4096]{1,0:T(8,128)(2,1)} custom-call(bf16[16,128,256]{2,1,0:T(8,128)(2,1)} %all_to_all.15.in_ref), custom_call_target="tpu_custom_call" | custom-call | tf_op jit(solution)/shard_map/unpack/pallas_call | solution.py:83
  (70 shorter events, 16.1 us)
Async XLA Ops:
  0.0 13.8 %collective-permute-start = (bf16[32,5120]{1,0:T(8,128)(2,1)}, bf16[32,5120]{1,0:T(8,128)(2,1)S(1)}, u32[]{:S(2)}, u32[]{:S(2)}) collective-permute-start(bf16[32,5120]{1,0:T(8,128)(2,1)} %bitcast.26), channel_id=1, source_target_pairs={{0,2},{1,3},{2,4},{3,5},{4,6},{5,7},{6,8},{7,9},{8,10},{9,11},{10,... | collective-permute-start | bytes 983048 | tf_op jit(solution)/shard_map/ppermute | solution.py:200
  1.9 11.9 %collective-permute-start.1 = (bf16[32,5120]{1,0:T(8,128)(2,1)}, bf16[32,5120]{1,0:T(8,128)(2,1)S(1)}, u32[]{:S(2)}, u32[]{:S(2)}) collective-permute-start(bf16[32,5120]{1,0:T(8,128)(2,1)} %bitcast.27), channel_id=1, source_target_pairs={{0,14},{1,15},{2,0},{3,1},{4,2},{5,3},{6,4},{7,5},{8,6},{9,7},{10,... | collective-permute-start | bytes 983048 | tf_op jit(solution)/shard_map/ppermute | solution.py:201
  6.9 10.1 %collective-permute-start.8 = (bf16[320,512]{1,0:T(8,128)(2,1)S(1)}, bf16[320,512]{1,0:T(8,128)(2,1)S(1)}, u32[]{:S(2)}, u32[]{:S(2)}) collective-permute-start(bf16[320,512]{1,0:T(8,128)(2,1)S(1)} %pad_maximum_fusion.3), channel_id=1, source_target_pairs={{0,1},{1,0},{2,3},{3,2},{4,5},{5,4},{6,7},{7,6},{8,9},{9,8},{10,11... | collective-permute-start | bytes 983048 | tf_op jit(solution)/shard_map/ppermute | solution.py:173
  13.8 16.6 %copy-start.5 = (bf16[32,5120]{1,0:T(8,128)(2,1)}, bf16[32,5120]{1,0:T(8,128)(2,1)S(1)}, u32[]{:S(2)}) copy-start(bf16[32,5120]{1,0:T(8,128)(2,1)S(1)} %collective-permute-done.refs_1_.refs_10_) | copy-start | bytes 983044
  13.8 10.1 %collective-permute-start.2 = (bf16[32,5120]{1,0:T(8,128)(2,1)S(1)}, bf16[32,5120]{1,0:T(8,128)(2,1)S(1)}, u32[]{:S(2)}, u32[]{:S(2)}) collective-permute-start(bf16[32,5120]{1,0:T(8,128)(2,1)S(1)} %collective-permute-done.refs_1_.refs_10_), channel_id=1, source_target_pairs={{0,2},{1,3},{2,4},{3,5},{4,6},{5,7},{6,8},{7,9},{8,10},{9,11},{10,... | collective-permute-start | bytes 983048 | tf_op jit(solution)/shard_map/ppermute | solution.py:200
  13.8 10.1 %copy-start.6 = (bf16[32,5120]{1,0:T(8,128)(2,1)}, bf16[32,5120]{1,0:T(8,128)(2,1)S(1)}, u32[]{:S(2)}) copy-start(bf16[32,5120]{1,0:T(8,128)(2,1)S(1)} %collective-permute-done.1.refs_2_.refs_11_) | copy-start | bytes 983044
  13.8 10.1 %collective-permute-start.3 = (bf16[32,5120]{1,0:T(8,128)(2,1)S(1)}, bf16[32,5120]{1,0:T(8,128)(2,1)S(1)}, u32[]{:S(2)}, u32[]{:S(2)}) collective-permute-start(bf16[32,5120]{1,0:T(8,128)(2,1)S(1)} %collective-permute-done.1.refs_2_.refs_11_), channel_id=1, source_target_pairs={{0,14},{1,15},{2,0},{3,1},{4,2},{5,3},{6,4},{7,5},{8,6},{9,7},{10,... | collective-permute-start | bytes 983048 | tf_op jit(solution)/shard_map/ppermute | solution.py:201
  17.1 19.5 %collective-permute-start.9 = (bf16[320,1024]{1,0:T(8,128)(2,1)S(1)}, bf16[320,1024]{1,0:T(8,128)(2,1)S(1)}, u32[]{:S(2)}, u32[]{:S(2)}) collective-permute-start(bf16[320,1024]{1,0:T(8,128)(2,1)S(1)} %constant_dynamic-update-slice_fusion), channel_id=1, source_target_pairs={{16,32},{32,16},{80,96},{96,80},{144,160},{160,144},{208,224},{224... | collective-permute-start | bytes 1966088 | tf_op jit(solution)/shard_map/ppermute | solution.py:175
  17.8 18.9 %collective-permute-start.10 = (bf16[320,1024]{1,0:T(8,128)(2,1)S(1)}, bf16[320,1024]{1,0:T(8,128)(2,1)}, u32[]{:S(2)}, u32[]{:S(2)}) collective-permute-start(bf16[320,1024]{1,0:T(8,128)(2,1)S(1)} %constant_dynamic-update-slice_fusion), channel_id=1, source_target_pairs={{0,32},{32,48},{48,16},{16,0},{64,96},{96,112},{112,80},{80,64},{1... | collective-permute-start | bytes 1966088 | tf_op jit(solution)/shard_map/ppermute | solution.py:174
  23.9 6.5 %copy-start.7 = (bf16[32,5120]{1,0:T(8,128)(2,1)}, bf16[32,5120]{1,0:T(8,128)(2,1)S(1)}, u32[]{:S(2)}) copy-start(bf16[32,5120]{1,0:T(8,128)(2,1)S(1)} %collective-permute-done.2.refs_3_.refs_12_) | copy-start | bytes 983044
  23.9 9.3 %collective-permute-start.4 = (bf16[32,5120]{1,0:T(8,128)(2,1)S(1)}, bf16[32,5120]{1,0:T(8,128)(2,1)S(1)}, u32[]{:S(2)}, u32[]{:S(2)}) collective-permute-start(bf16[32,5120]{1,0:T(8,128)(2,1)S(1)} %collective-permute-done.2.refs_3_.refs_12_), channel_id=1, source_target_pairs={{0,2},{1,3},{2,4},{3,5},{4,6},{5,7},{6,8},{7,9},{8,10},{9,11},{10,... | collective-permute-start | bytes 983048 | tf_op jit(solution)/shard_map/ppermute | solution.py:200
  23.9 6.5 %copy-start.8 = (bf16[32,5120]{1,0:T(8,128)(2,1)}, bf16[32,5120]{1,0:T(8,128)(2,1)S(1)}, u32[]{:S(2)}) copy-start(bf16[32,5120]{1,0:T(8,128)(2,1)S(1)} %collective-permute-done.3.refs_4_.refs_13_) | copy-start | bytes 983044
  23.9 9.3 %collective-permute-start.5 = (bf16[32,5120]{1,0:T(8,128)(2,1)S(1)}, bf16[32,5120]{1,0:T(8,128)(2,1)S(1)}, u32[]{:S(2)}, u32[]{:S(2)}) collective-permute-start(bf16[32,5120]{1,0:T(8,128)(2,1)S(1)} %collective-permute-done.3.refs_4_.refs_13_), channel_id=1, source_target_pairs={{0,14},{1,15},{2,0},{3,1},{4,2},{5,3},{6,4},{7,5},{8,6},{9,7},{10,... | collective-permute-start | bytes 983048 | tf_op jit(solution)/shard_map/ppermute | solution.py:201
  33.1 7.1 %copy-start.2 = (bf16[32,5120]{1,0:T(8,128)(2,1)}, bf16[32,5120]{1,0:T(8,128)(2,1)S(1)}, u32[]{:S(2)}) copy-start(bf16[32,5120]{1,0:T(8,128)(2,1)S(1)} %collective-permute-done.4.refs_5_.refs_14_) | copy-start | bytes 983044
  33.2 8.3 %collective-permute-start.6 = (bf16[16,5120]{1,0:T(8,128)(2,1)S(1)}, bf16[16,5120]{1,0:T(8,128)(2,1)S(1)}, u32[]{:S(2)}, u32[]{:S(2)}) collective-permute-start(bf16[16,5120]{1,0:T(8,128)(2,1)S(1)} %slice.44), channel_id=1, source_target_pairs={{0,2},{1,3},{2,4},{3,5},{4,6},{5,7},{6,8},{7,9},{8,10},{9,11},{10,... | collective-permute-start | bytes 491528 | tf_op jit(solution)/shard_map/ppermute | solution.py:204
  33.3 7.6 %copy-start.3 = (bf16[32,5120]{1,0:T(8,128)(2,1)}, bf16[32,5120]{1,0:T(8,128)(2,1)S(1)}, u32[]{:S(2)}) copy-start(bf16[32,5120]{1,0:T(8,128)(2,1)S(1)} %collective-permute-done.5.refs_6_.refs_15_) | copy-start | bytes 983044
  33.3 8.8 %collective-permute-start.7 = (bf16[16,5120]{1,0:T(8,128)(2,1)S(1)}, bf16[16,5120]{1,0:T(8,128)(2,1)S(1)}, u32[]{:S(2)}, u32[]{:S(2)}) collective-permute-start(bf16[16,5120]{1,0:T(8,128)(2,1)S(1)} %slice.45), channel_id=1, source_target_pairs={{0,14},{1,15},{2,0},{3,1},{4,2},{5,3},{6,4},{7,5},{8,6},{9,7},{10,... | collective-permute-start | bytes 491528 | tf_op jit(solution)/shard_map/ppermute | solution.py:205
  39.7 1.8 copy-start.4
  41.5 1.2 copy-start.9
  42.1 0.7 copy-start.10
  42.8 80.6 %all-to-all-start.1 = ((bf16[16,128,768]{2,1,0:T(8,128)(2,1)}), bf16[16,128,768]{2,1,0:T(8,128)(2,1)S(1)}, u32[]{:S(2)}, u32[]{:S(2)}) async-start(bf16[16,128,768]{2,1,0:T(8,128)(2,1)} %hold.1), calls=%async_computation.1 | async-start | bytes 6291456 | tf_op jit(solution)/shard_map/all_to_all | solution.py:257
  48.7 31.4 %collective-permute-start.12 = (bf16[640,1024]{1,0:T(8,128)(2,1)}, bf16[640,1024]{1,0:T(8,128)(2,1)}, u32[]{:S(2)}, u32[]{:S(2)}) collective-permute-start(bf16[640,1024]{1,0:T(8,128)(2,1)} %copy-done.4), channel_id=1, source_target_pairs={{0,64},{16,80},{32,96},{48,112},{64,128},{80,144},{96,160},{112,17... | collective-permute-start | bytes 3932168 | tf_op jit(solution)/shard_map/ppermute | solution.py:188
  50.3 32.7 %collective-permute-start.11 = (bf16[640,1024]{1,0:T(8,128)(2,1)}, bf16[640,1024]{1,0:T(8,128)(2,1)}, u32[]{:S(2)}, u32[]{:S(2)}) collective-permute-start(bf16[640,1024]{1,0:T(8,128)(2,1)} %copy-done.4), channel_id=1, source_target_pairs={{0,192},{16,208},{32,224},{48,240},{64,0},{80,16},{96,32},{112,48}... | collective-permute-start | bytes 3932168 | tf_op jit(solution)/shard_map/ppermute | solution.py:189
  56.2 47.3 %collective-permute-start.15 = (bf16[256,2560]{1,0:T(8,128)(2,1)}, bf16[256,2560]{1,0:T(8,128)(2,1)S(1)}, u32[]{:S(2)}, u32[]{:S(2)}) collective-permute-start(bf16[256,2560]{1,0:T(8,128)(2,1)} %get-tuple-element.8), channel_id=1, source_target_pairs={{0,16},{16,0},{32,48},{48,32},{64,80},{80,64},{96,112},{112,96},{1... | collective-permute-start | bytes 3932168 | tf_op jit(solution)/shard_map/ppermute | solution.py:267
  81.2 16.5 %collective-permute-start.13 = (bf16[320,1024]{1,0:T(8,128)(2,1)S(1)}, bf16[320,1024]{1,0:T(8,128)(2,1)S(1)}, u32[]{:S(2)}, u32[]{:S(2)}) collective-permute-start(bf16[320,1024]{1,0:T(8,128)(2,1)S(1)} %slice.46), channel_id=1, source_target_pairs={{0,64},{16,80},{32,96},{48,112},{64,128},{80,144},{96,160},{112,17... | collective-permute-start | bytes 1966088 | tf_op jit(solution)/shard_map/ppermute | solution.py:190
  84.2 16.0 %collective-permute-start.14 = (bf16[320,1024]{1,0:T(8,128)(2,1)S(1)}, bf16[320,1024]{1,0:T(8,128)(2,1)S(1)}, u32[]{:S(2)}, u32[]{:S(2)}) collective-permute-start(bf16[320,1024]{1,0:T(8,128)(2,1)S(1)} %slice.47), channel_id=1, source_target_pairs={{0,192},{16,208},{32,224},{48,240},{64,0},{80,16},{96,32},{112,48}... | collective-permute-start | bytes 1966088 | tf_op jit(solution)/shard_map/ppermute | solution.py:191
  108.7 21.7 %copy-start.11 = (s32[8]{0:T(128)S(1)}, s32[8]{0:T(128)}, u32[]{:S(2)}) copy-start(s32[8]{0:T(128)} %constant.81.clone) | copy-start | bytes 100
  108.7 21.7 %collective-permute-start.16 = (f32[256,1024]{1,0:T(8,128)}, f32[256,1024]{1,0:T(8,128)}, u32[]{:S(2)}, u32[]{:S(2)}) collective-permute-start(f32[256,1024]{1,0:T(8,128)} %fusion.6), channel_id=1, source_target_pairs={{0,16},{16,0},{32,48},{48,32},{64,80},{80,64},{96,112},{112,96},{1... | collective-permute-start | bytes 3145736 | tf_op jit(solution)/shard_map/ppermute | solution.py:270
  123.4 1.7 copy-start
  125.1 35.1 %all-to-all-start = ((bf16[16,128,256]{2,1,0:T(8,128)(2,1)}), bf16[16,128,256]{2,1,0:T(8,128)(2,1)S(1)}, u32[]{:S(2)}, u32[]{:S(2)}) async-start(bf16[16,128,256]{2,1,0:T(8,128)(2,1)} %pack.2), calls=%async_computation | async-start | bytes 2097152 | tf_op jit(solution)/shard_map/all_to_all | solution.py:257
  135.2 8.3 %collective-permute-start.17 = (bf16[256,512]{1,0:T(8,128)(2,1)S(1)}, bf16[256,512]{1,0:T(8,128)(2,1)S(1)}, u32[]{:S(2)}, u32[]{:S(2)}) collective-permute-start(bf16[256,512]{1,0:T(8,128)(2,1)S(1)} %get-tuple-element.14), channel_id=1, source_target_pairs={{0,1},{1,0},{2,3},{3,2},{4,5},{5,4},{6,7},{7,6},{8,9},{9,8},{10,11... | collective-permute-start | bytes 786440 | tf_op jit(solution)/shard_map/ppermute | solution.py:273
  143.5 1.9 copy-start.1

commit v4 on v3

--- a/solution.py
+++ b/solution.py
@@ -23,6 +23,7 @@
     return [(s, (s + step * XL) % (Z * XL)) for s in range(Z * XL)]
 
 
+SPLIT_FLOPS = 400_000_000_000
 CORE_SWAP = [(p, p ^ 1) for p in range(Y * XH * CORE)]
 XL_SWAP = [(s, s ^ 1) for s in range(Z * XL)]
 REGROUP_A = [(4 * y + a, 4 * y + b) for y in range(Y) for a, b in ((0, 2), (2, 3), (3, 1), (1, 0))]
@@ -238,7 +239,7 @@
         ),
         out_shape=[shape, shape],
         cost_estimate=pl.CostEstimate(
-            flops=0, bytes_accessed=4 * rows * depth, transcendentals=0
+            flops=SPLIT_FLOPS, bytes_accessed=4 * rows * depth, transcendentals=0
         ),
         name="split_text",
     )(jnp.stack([y, core]), *pieces, *pieces)
@@ -260,7 +261,7 @@
     offsets, pieces = ring_z(context[0])
     chunk = gather_weights(jnp.concatenate([key_weight, value_weight], axis=1), x_hi, core)
     packed = pack([queries[0], self_keys[0], self_values[0]], parts)
-    qkv = to_heads(hold(packed, chunk, *pieces[-4:]))
+    qkv = to_heads(hold(packed, *pieces[-4:-2]))
     weights = ring_y(chunk)
     text_rows = context.shape[1]
     mine, theirs = split_text(pieces, y, core)

time: 203 us -> 197 us (0.970)
  local copies, waits for them, and re-layouts: 17.9 us -> 13.6 us
    all_to_all x2, waiting for transfers between devices: 12.7 us -> 19.4 us  [to_heads(): heads = lax.all_to_all(packed, 'seq', split_axis=0, concat_axis=0)]
    ppermute x1, waiting for transfers between devices: 23.8 us -> 17.4 us  [ring_y(): before = lax.ppermute(chunk, 'prompt', y_shift(1))]
    unnamed x29 -> x19, local copies, waits for them, and re-layouts: 9.78 us -> 7.45 us
    ppermute x1, starting transfers between devices: 0.53 us -> 2.75 us  [ring_y(): far_bottom = lax.ppermute(after[half:], 'prompt', y_shift(-1))]
  transfers between devices with their start and end apart: 20 -> 20, of which waited for: 8 -> 7; matrix products, arithmetic and copies ran while one was open for 14% -> 13% of each run, Pallas kernels for 12% -> 13%
where the time goes in v4:
time: 197 us; the launch traced here: 195 us
  waiting for transfers between devices  60.5 us (31%)
  starting transfers between devices  39.3 us (20%)
  blocking collectives  34.3 us (17%)
  Pallas kernels  33.1 us (17%)
  local copies, waits for them, and re-layouts  13.6 us (7%)
  matrix products  9.57 us (5%)
  other arithmetic  3.99 us (2%)
    all_to_all x1, blocking collectives, body(): lax.all_to_all(attended.reshape(parts, -1, width), 'seq', split_axis=0, c...  34.3 us
    all_to_all x2, waiting for transfers between devices, to_heads(): heads = lax.all_to_all(packed, 'seq', split_axis=0, concat_axis=0)  19.4 us
    ppermute x1, waiting for transfers between devices, ring_y(): before = lax.ppermute(chunk, 'prompt', y_shift(1))  17.4 us
    pallas_call x1, Pallas kernels, self_attend(): pl.pallas_call(self_kernel, grid=(rows // block,), in_specs=[pl.BlockSpec...  16.3 us
    ppermute x1, waiting for transfers between devices, ring_y(): far_top = lax.ppermute(before[:half], 'prompt', y_shift(1))  10.6 us
    ppermute x3, starting transfers between devices, ring_z(): down = lax.ppermute(down, 'seq', z_shift(-1))  10.4 us
    all_to_all x2, starting transfers between devices, to_heads(): heads = lax.all_to_all(packed, 'seq', split_axis=0, concat_axis=0)  9.66 us
    ppermute x3, waiting for transfers between devices, ring_z(): up = lax.ppermute(up, 'seq', z_shift(1))  7.71 us
  transfers between devices with their start and end apart: 20, of which 7 were waited for; matrix products, arithmetic and copies ran while one was open for 13% of the time, Pallas kernels for 13%

profile of v4, /device:TPU:8, one launch (start us, length us, event | category | flops | bytes accessed | tf_op | source)
XLA Modules:
  0.0 195.3 jit_solution(14261012986798236683)
XLA Ops:
  0.0 1.9 collective-permute-start
  1.9 3.9 %collective-permute-start.1 = (bf16[32,5120]{1,0:T(8,128)(2,1)}, bf16[32,5120]{1,0:T(8,128)(2,1)S(1)}, u32[]{:S(2)}, u32[]{:S(2)}) collective-permute-start(bf16[32,5120]{1,0:T(8,128)(2,1)} %bitcast.28), channel_id=1, source_target_pairs={{0,14},{1,15},{2,0},{3,1},{4,2},{5,3},{6,4},{7,5},{8,6},{9,7},{10,... | collective-permute-start | bytes 983048 | tf_op jit(solution)/shard_map/ppermute | solution.py:202
  6.9 1.6 collective-permute-start.8
  10.3 3.4 %collective-permute-done.refs_1_.refs_10_ = bf16[32,5120]{1,0:T(8,128)(2,1)S(1)} collective-permute-done((bf16[32,5120]{1,0:T(8,128)(2,1)}, bf16[32,5120]{1,0:T(8,128)(2,1)S(1)}, u32[]{:S(2)}, u32[]{:S(2)}) %collective-permute-start) | collective-permute-done | bytes 327712 | tf_op jit(solution)/shard_map/ppermute | solution.py:201
  13.8 3.2 %collective-permute-start.3 = (bf16[32,5120]{1,0:T(8,128)(2,1)S(1)}, bf16[32,5120]{1,0:T(8,128)(2,1)}, u32[]{:S(2)}, u32[]{:S(2)}) collective-permute-start(bf16[32,5120]{1,0:T(8,128)(2,1)S(1)} %collective-permute-done.1.refs_2_.refs_11_), channel_id=1, source_target_pairs={{0,14},{1,15},{2,0},{3,1},{4,2},{5,3},{6,4},{7,5},{8,6},{9,7},{10,... | collective-permute-start | bytes 983048 | tf_op jit(solution)/shard_map/ppermute | solution.py:202
  17.8 4.3 %collective-permute-start.10 = (bf16[320,1024]{1,0:T(8,128)(2,1)S(1)}, bf16[320,1024]{1,0:T(8,128)(2,1)S(1)}, u32[]{:S(2)}, u32[]{:S(2)}) collective-permute-start(bf16[320,1024]{1,0:T(8,128)(2,1)S(1)} %constant_dynamic-update-slice_fusion), channel_id=1, source_target_pairs={{0,32},{32,48},{48,16},{16,0},{64,96},{96,112},{112,80},{80,64},{1... | collective-permute-start | bytes 1966088 | tf_op jit(solution)/shard_map/ppermute | solution.py:175
  22.1 1.9 collective-permute-done.2.refs_3_.refs_12_
  24.0 3.2 %collective-permute-start.5 = (bf16[32,5120]{1,0:T(8,128)(2,1)}, bf16[32,5120]{1,0:T(8,128)(2,1)S(1)}, u32[]{:S(2)}, u32[]{:S(2)}) collective-permute-start(bf16[32,5120]{1,0:T(8,128)(2,1)} %collective-permute-done.3.refs_4_.refs_13_), channel_id=1, source_target_pairs={{0,14},{1,15},{2,0},{3,1},{4,2},{5,3},{6,4},{7,5},{8,6},{9,7},{10,... | collective-permute-start | bytes 983048 | tf_op jit(solution)/shard_map/ppermute | solution.py:202
  27.2 3.1 %pack.3.refs_0_ = bf16[16,128,768]{2,1,0:T(8,128)(2,1)} custom-call(bf16[128,4096]{1,0:T(8,128)(2,1)} %bitcast.24, bf16[128,4096]{1,0:T(8,128)(2,1)} %bitcast.25, bf16[128,4096]{1,0:T(8,128)(2,1)} %bitcast.26), custom_call_target="tpu_custom_call" | custom-call | bytes 6291456 | tf_op jit(solution)/shard_map/pack/pallas_call | solution.py:46
  31.0 2.4 %collective-permute-done.4.refs_5_.refs_14_ = bf16[32,5120]{1,0:T(8,128)(2,1)S(1)} collective-permute-done((bf16[32,5120]{1,0:T(8,128)(2,1)}, bf16[32,5120]{1,0:T(8,128)(2,1)S(1)}, u32[]{:S(2)}, u32[]{:S(2)}) %collective-permute-start.4) | collective-permute-done | bytes 327712 | tf_op jit(solution)/shard_map/ppermute | solution.py:201
  33.5 3.3 %collective-permute-start.7 = (bf16[16,5120]{1,0:T(8,128)(2,1)S(1)}, bf16[16,5120]{1,0:T(8,128)(2,1)S(1)}, u32[]{:S(2)}, u32[]{:S(2)}) collective-permute-start(bf16[16,5120]{1,0:T(8,128)(2,1)S(1)} %slice.33), channel_id=1, source_target_pairs={{0,14},{1,15},{2,0},{3,1},{4,2},{5,3},{6,4},{7,5},{8,6},{9,7},{10,... | collective-permute-start | bytes 491528 | tf_op jit(solution)/shard_map/ppermute | solution.py:206
  36.9 2.1 %constant_dynamic-update-slice_fusion.7 = (bf16[2560,1024]{1,0:T(8,128)(2,1)}, bf16[640,1024]{1,0:T(8,128)(2,1)}) fusion(bf16[320,1024]{1,0:T(8,128)(2,1)S(1)} %broadcast_select_fusion, bf16[320,1024]{1,0:T(8,128)(2,1)S(1)} %collective-permute-done.10, pred[]{:T(512)S(6)} %eq.13, pred[]{:T(512)S(6)} %eq.12), kind=kLoop, calls=%fused_computation.15 | loop fusion | flops 7208959 | bytes 3932162
  39.5 1.6 collective-permute-start.12
  42.2 6.0 %all-to-all-start.1 = ((bf16[16,128,768]{2,1,0:T(8,128)(2,1)}), bf16[16,128,768]{2,1,0:T(8,128)(2,1)}, u32[]{:S(2)}, u32[]{:S(2)}) async-start(bf16[16,128,768]{2,1,0:T(8,128)(2,1)} %hold.1), calls=%async_computation.1 | async-start | bytes 6291456 | tf_op jit(solution)/shard_map/all_to_all | solution.py:258
  49.6 4.9 %split_text.1 = (bf16[256,2560]{1,0:T(8,128)(2,1)}, bf16[256,2560]{1,0:T(8,128)(2,1)}) custom-call(s32[2]{0:T(128)} %pad_add_fusion.where_ref, bf16[32,5120]{1,0:T(8,128)(2,1)} %bitcast.29, bf16[32,5120]{1,0:T(8,128)(2,1)} %copy-done.3, bf16[32,5120]{1,0:T(8,128)(2,1)} %copy-done.4, bf16[32,5120]{1,0:T(8,128)(2,1)} %collective-permute-done.2.refs_3_.refs_12_, ...), custom_call_target="tpu_custom_call" | custom-call | flops 399999991808 | bytes 5242880 | tf_op jit(solution)/shard_map/split_text/pallas_call | solution.py:232
  54.6 17.4 %collective-permute-done.12 = bf16[640,1024]{1,0:T(8,128)(2,1)} collective-permute-done((bf16[640,1024]{1,0:T(8,128)(2,1)}, bf16[640,1024]{1,0:T(8,128)(2,1)}, u32[]{:S(2)}, u32[]{:S(2)}) %collective-permute-start.12) | collective-permute-done | bytes 1310752 | tf_op jit(solution)/shard_map/ppermute | solution.py:189
  73.7 1.1 slice.35
  74.8 2.7 %collective-permute-start.14 = (bf16[320,1024]{1,0:T(8,128)(2,1)S(1)}, bf16[320,1024]{1,0:T(8,128)(2,1)S(1)}, u32[]{:S(2)}, u32[]{:S(2)}) collective-permute-start(bf16[320,1024]{1,0:T(8,128)(2,1)S(1)} %slice.35), channel_id=1, source_target_pairs={{0,192},{16,208},{32,224},{48,240},{64,0},{80,16},{96,32},{112,48}... | collective-permute-start | bytes 1966088 | tf_op jit(solution)/shard_map/ppermute | solution.py:192
  77.5 2.5 %constant_dynamic-update-slice_fusion.6 = bf16[2560,1024]{1,0:T(8,128)(2,1)} fusion(bf16[2560,1024]{1,0:T(8,128)(2,1)} %get-tuple-element.9, bf16[640,1024]{1,0:T(8,128)(2,1)} %collective-permute-done.11), kind=kLoop, calls=%fused_computation.14 | loop fusion | bytes 2621440
  80.0 10.6 %collective-permute-done.13 = bf16[320,1024]{1,0:T(8,128)(2,1)S(1)} collective-permute-done((bf16[320,1024]{1,0:T(8,128)(2,1)S(1)}, bf16[320,1024]{1,0:T(8,128)(2,1)S(1)}, u32[]{:S(2)}, u32[]{:S(2)}) %collective-permute-start.13) | collective-permute-done | bytes 655392 | tf_op jit(solution)/shard_map/ppermute | solution.py:191
  92.4 2.5 %constant_dynamic-update-slice_fusion.3 = bf16[2560,1024]{1,0:T(8,128)(2,1)} fusion(bf16[2560,1024]{1,0:T(8,128)(2,1)} %constant_dynamic-update-slice_fusion.4, bf16[640,1024]{1,0:T(8,128)(2,1)} %collective-permute-done.12), kind=kLoop, calls=%fused_computation.11 | loop fusion | bytes 2621440 | tf_op jit(solution)/shard_map/concatenate | solution.py:193
  94.9 5.1 %fusion.6 = f32[256,1024]{1,0:T(8,128)} fusion(bf16[256,2560]{1,0:T(8,128)(2,1)S(1)} %collective-permute-done.15, bf16[2560,1024]{1,0:T(8,128)(2,1)} %constant_dynamic-update-slice_fusion.3), kind=kOutput, calls=%fused_computation.28 | convolution fusion | flops 1342177280 | bytes 7602176 | tf_op jit(solution)/shard_map/dot_general | solution.py:269
  100.0 2.1 %pack.2 = bf16[16,128,256]{2,1,0:T(8,128)(2,1)} custom-call(bf16[128,4096]{1,0:T(8,128)(2,1)} %bitcast.23), custom_call_target="tpu_custom_call" | custom-call | bytes 2097152 | tf_op jit(solution)/shard_map/pack/pallas_call | solution.py:46
  102.1 19.4 %all-to-all-done.1 = bf16[16,128,768]{2,1,0:T(8,128)(2,1)} async-done(((bf16[16,128,768]{2,1,0:T(8,128)(2,1)}), bf16[16,128,768]{2,1,0:T(8,128)(2,1)}, u32[]{:S(2)}, u32[]{:S(2)}) %all-to-all-start.1) | async-done | bytes 3145760 | tf_op jit(solution)/shard_map/all_to_all | solution.py:258
  121.5 3.7 %all-to-all-start = ((bf16[16,128,256]{2,1,0:T(8,128)(2,1)}), bf16[16,128,256]{2,1,0:T(8,128)(2,1)S(1)}, u32[]{:S(2)}, u32[]{:S(2)}) async-start(bf16[16,128,256]{2,1,0:T(8,128)(2,1)} %pack.2), calls=%async_computation | async-start | bytes 2097152 | tf_op jit(solution)/shard_map/all_to_all | solution.py:258
  125.2 4.4 %fusion = bf16[256,1024]{1,0:T(8,128)(2,1)S(1)} fusion(f32[256,1024]{1,0:T(8,128)S(1)} %collective-permute-done.16, bf16[256,2560]{1,0:T(8,128)(2,1)} %get-tuple-element.7, bf16[2560,1024]{1,0:T(8,128)(2,1)} %constant_dynamic-update-slice_fusion.3), kind=kOutput, calls=%fused_computation.4 | convolution fusion | flops 1342701568 | bytes 8126464 | tf_op jit(solution)/shard_map/dot_general | solution.py:270
  129.7 1.9 collective-permute-start.17
  132.5 5.4 %collective-permute-done.17 = bf16[256,512]{1,0:T(8,128)(2,1)S(1)} collective-permute-done((bf16[256,512]{1,0:T(8,128)(2,1)S(1)}, bf16[256,512]{1,0:T(8,128)(2,1)S(1)}, u32[]{:S(2)}, u32[]{:S(2)}) %collective-permute-start.17) | collective-permute-done | bytes 262176 | tf_op jit(solution)/shard_map/ppermute | solution.py:274
  137.9 16.3 %self_attend.1.self_ref = bf16[2048,256]{1,0:T(8,128)(2,1)S(1)} custom-call(bf16[2048,768]{1,0:T(8,128)(2,1)} %bitcast.11.q_ref.k_ref.v_ref, bf16[2048,768]{1,0:T(8,128)(2,1)} %bitcast.11.q_ref.k_ref.v_ref, bf16[2048,768]{1,0:T(8,128)(2,1)} %bitcast.11.q_ref.k_ref.v_ref), custom_call_target="tpu_custom_call" | custom-call | flops 4294967296 | bytes 4194304 | tf_op jit(solution)/shard_map/self_attend/pallas_call | solution.py:129
  154.2 4.5 %cross_attend.1 = bf16[2048,256]{1,0:T(8,128)(2,1)S(1)} custom-call(f32[1,512]{1,0:T(1,128)S(1)} %select_n.67.bias_ref, bf16[2048,256]{1,0:T(8,128)(2,1)S(1)} %bitcast.21, bf16[512,512]{1,0:T(8,128)(2,1)S(1)} %pad_maximum_fusion.2.tk_ref.tv_ref, bf16[512,512]{1,0:T(8,128)(2,1)S(1)} %pad_maximum_fusion.2.tk_ref.tv_ref, bf16[2048,256]{1,0:T(8,128)(2,1)S(1)} %self_attend.1.self_ref), custom_call_target="tpu_custom_call" | custom-call | flops 1073741824 | bytes 3145728 | tf_op jit(solution)/shard_map/cross_attend/pallas_call | solution.py:153
  158.6 34.3 %all_to_all.15.in_ref = bf16[16,128,256]{2,1,0:T(8,128)(2,1)} all-to-all(bf16[16,128,256]{2,1,0:T(8,128)(2,1)S(1)} %bitcast.22), channel_id=1, replica_groups=mesh['prompt'=16,'seq'=16] {'seq'}, dimensions={0} | all-to-all | bytes 2097152 | tf_op jit(solution)/shard_map/all_to_all | solution.py:284
  193.0 2.3 %unpack.1 = bf16[128,4096]{1,0:T(8,128)(2,1)} custom-call(bf16[16,128,256]{2,1,0:T(8,128)(2,1)} %all_to_all.15.in_ref), custom_call_target="tpu_custom_call" | custom-call | tf_op jit(solution)/shard_map/unpack/pallas_call | solution.py:84
  (57 shorter events, 11.3 us)
Async XLA Ops:
  0.0 13.8 %collective-permute-start = (bf16[32,5120]{1,0:T(8,128)(2,1)}, bf16[32,5120]{1,0:T(8,128)(2,1)S(1)}, u32[]{:S(2)}, u32[]{:S(2)}) collective-permute-start(bf16[32,5120]{1,0:T(8,128)(2,1)} %bitcast.27), channel_id=1, source_target_pairs={{0,2},{1,3},{2,4},{3,5},{4,6},{5,7},{6,8},{7,9},{8,10},{9,11},{10,... | collective-permute-start | bytes 983048 | tf_op jit(solution)/shard_map/ppermute | solution.py:201
  1.9 11.9 %collective-permute-start.1 = (bf16[32,5120]{1,0:T(8,128)(2,1)}, bf16[32,5120]{1,0:T(8,128)(2,1)S(1)}, u32[]{:S(2)}, u32[]{:S(2)}) collective-permute-start(bf16[32,5120]{1,0:T(8,128)(2,1)} %bitcast.28), channel_id=1, source_target_pairs={{0,14},{1,15},{2,0},{3,1},{4,2},{5,3},{6,4},{7,5},{8,6},{9,7},{10,... | collective-permute-start | bytes 983048 | tf_op jit(solution)/shard_map/ppermute | solution.py:202
  6.9 10.1 %collective-permute-start.8 = (bf16[320,512]{1,0:T(8,128)(2,1)S(1)}, bf16[320,512]{1,0:T(8,128)(2,1)S(1)}, u32[]{:S(2)}, u32[]{:S(2)}) collective-permute-start(bf16[320,512]{1,0:T(8,128)(2,1)S(1)} %pad_maximum_fusion.3), channel_id=1, source_target_pairs={{0,1},{1,0},{2,3},{3,2},{4,5},{5,4},{6,7},{7,6},{8,9},{9,8},{10,11... | collective-permute-start | bytes 983048 | tf_op jit(solution)/shard_map/ppermute | solution.py:174
  13.8 16.6 %copy-start.3 = (bf16[32,5120]{1,0:T(8,128)(2,1)}, bf16[32,5120]{1,0:T(8,128)(2,1)S(1)}, u32[]{:S(2)}) copy-start(bf16[32,5120]{1,0:T(8,128)(2,1)S(1)} %collective-permute-done.refs_1_.refs_10_) | copy-start | bytes 983044
  13.8 10.2 %collective-permute-start.2 = (bf16[32,5120]{1,0:T(8,128)(2,1)S(1)}, bf16[32,5120]{1,0:T(8,128)(2,1)}, u32[]{:S(2)}, u32[]{:S(2)}) collective-permute-start(bf16[32,5120]{1,0:T(8,128)(2,1)S(1)} %collective-permute-done.refs_1_.refs_10_), channel_id=1, source_target_pairs={{0,2},{1,3},{2,4},{3,5},{4,6},{5,7},{6,8},{7,9},{8,10},{9,11},{10,... | collective-permute-start | bytes 983048 | tf_op jit(solution)/shard_map/ppermute | solution.py:201
  13.8 16.6 %copy-start.4 = (bf16[32,5120]{1,0:T(8,128)(2,1)}, bf16[32,5120]{1,0:T(8,128)(2,1)S(1)}, u32[]{:S(2)}) copy-start(bf16[32,5120]{1,0:T(8,128)(2,1)S(1)} %collective-permute-done.1.refs_2_.refs_11_) | copy-start | bytes 983044
  13.8 10.2 %collective-permute-start.3 = (bf16[32,5120]{1,0:T(8,128)(2,1)S(1)}, bf16[32,5120]{1,0:T(8,128)(2,1)}, u32[]{:S(2)}, u32[]{:S(2)}) collective-permute-start(bf16[32,5120]{1,0:T(8,128)(2,1)S(1)} %collective-permute-done.1.refs_2_.refs_11_), channel_id=1, source_target_pairs={{0,14},{1,15},{2,0},{3,1},{4,2},{5,3},{6,4},{7,5},{8,6},{9,7},{10,... | collective-permute-start | bytes 983048 | tf_op jit(solution)/shard_map/ppermute | solution.py:202
  17.1 19.8 %collective-permute-start.9 = (bf16[320,1024]{1,0:T(8,128)(2,1)S(1)}, bf16[320,1024]{1,0:T(8,128)(2,1)S(1)}, u32[]{:S(2)}, u32[]{:S(2)}) collective-permute-start(bf16[320,1024]{1,0:T(8,128)(2,1)S(1)} %constant_dynamic-update-slice_fusion), channel_id=1, source_target_pairs={{16,32},{32,16},{80,96},{96,80},{144,160},{160,144},{208,224},{224... | collective-permute-start | bytes 1966088 | tf_op jit(solution)/shard_map/ppermute | solution.py:176
  17.8 19.1 %collective-permute-start.10 = (bf16[320,1024]{1,0:T(8,128)(2,1)S(1)}, bf16[320,1024]{1,0:T(8,128)(2,1)S(1)}, u32[]{:S(2)}, u32[]{:S(2)}) collective-permute-start(bf16[320,1024]{1,0:T(8,128)(2,1)S(1)} %constant_dynamic-update-slice_fusion), channel_id=1, source_target_pairs={{0,32},{32,48},{48,16},{16,0},{64,96},{96,112},{112,80},{80,64},{1... | collective-permute-start | bytes 1966088 | tf_op jit(solution)/shard_map/ppermute | solution.py:175
  24.0 9.4 %collective-permute-start.4 = (bf16[32,5120]{1,0:T(8,128)(2,1)}, bf16[32,5120]{1,0:T(8,128)(2,1)S(1)}, u32[]{:S(2)}, u32[]{:S(2)}) collective-permute-start(bf16[32,5120]{1,0:T(8,128)(2,1)} %collective-permute-done.2.refs_3_.refs_12_), channel_id=1, source_target_pairs={{0,2},{1,3},{2,4},{3,5},{4,6},{5,7},{6,8},{7,9},{8,10},{9,11},{10,... | collective-permute-start | bytes 983048 | tf_op jit(solution)/shard_map/ppermute | solution.py:201
  24.0 9.5 %collective-permute-start.5 = (bf16[32,5120]{1,0:T(8,128)(2,1)}, bf16[32,5120]{1,0:T(8,128)(2,1)S(1)}, u32[]{:S(2)}, u32[]{:S(2)}) collective-permute-start(bf16[32,5120]{1,0:T(8,128)(2,1)} %collective-permute-done.3.refs_4_.refs_13_), channel_id=1, source_target_pairs={{0,14},{1,15},{2,0},{3,1},{4,2},{5,3},{6,4},{7,5},{8,6},{9,7},{10,... | collective-permute-start | bytes 983048 | tf_op jit(solution)/shard_map/ppermute | solution.py:202
  33.4 7.7 %copy-start = (bf16[32,5120]{1,0:T(8,128)(2,1)}, bf16[32,5120]{1,0:T(8,128)(2,1)S(1)}, u32[]{:S(2)}) copy-start(bf16[32,5120]{1,0:T(8,128)(2,1)S(1)} %collective-permute-done.4.refs_5_.refs_14_) | copy-start | bytes 983044
  33.4 14.9 %collective-permute-start.6 = (bf16[16,5120]{1,0:T(8,128)(2,1)S(1)}, bf16[16,5120]{1,0:T(8,128)(2,1)S(1)}, u32[]{:S(2)}, u32[]{:S(2)}) collective-permute-start(bf16[16,5120]{1,0:T(8,128)(2,1)S(1)} %slice.32), channel_id=1, source_target_pairs={{0,2},{1,3},{2,4},{3,5},{4,6},{5,7},{6,8},{7,9},{8,10},{9,11},{10,... | collective-permute-start | bytes 491528 | tf_op jit(solution)/shard_map/ppermute | solution.py:205
  33.5 8.2 %copy-start.1 = (bf16[32,5120]{1,0:T(8,128)(2,1)}, bf16[32,5120]{1,0:T(8,128)(2,1)S(1)}, u32[]{:S(2)}) copy-start(bf16[32,5120]{1,0:T(8,128)(2,1)S(1)} %collective-permute-done.5.refs_6_.refs_15_) | copy-start | bytes 983044
  33.5 14.7 %collective-permute-start.7 = (bf16[16,5120]{1,0:T(8,128)(2,1)S(1)}, bf16[16,5120]{1,0:T(8,128)(2,1)S(1)}, u32[]{:S(2)}, u32[]{:S(2)}) collective-permute-start(bf16[16,5120]{1,0:T(8,128)(2,1)S(1)} %slice.33), channel_id=1, source_target_pairs={{0,14},{1,15},{2,0},{3,1},{4,2},{5,3},{6,4},{7,5},{8,6},{9,7},{10,... | collective-permute-start | bytes 491528 | tf_op jit(solution)/shard_map/ppermute | solution.py:206
  39.0 34.6 %collective-permute-start.11 = (bf16[640,1024]{1,0:T(8,128)(2,1)}, bf16[640,1024]{1,0:T(8,128)(2,1)}, u32[]{:S(2)}, u32[]{:S(2)}) collective-permute-start(bf16[640,1024]{1,0:T(8,128)(2,1)} %get-tuple-element.10), channel_id=1, source_target_pairs={{0,192},{16,208},{32,224},{48,240},{64,0},{80,16},{96,32},{112,48}... | collective-permute-start | bytes 3932168 | tf_op jit(solution)/shard_map/ppermute | solution.py:190
  39.5 32.5 %collective-permute-start.12 = (bf16[640,1024]{1,0:T(8,128)(2,1)}, bf16[640,1024]{1,0:T(8,128)(2,1)}, u32[]{:S(2)}, u32[]{:S(2)}) collective-permute-start(bf16[640,1024]{1,0:T(8,128)(2,1)} %get-tuple-element.10), channel_id=1, source_target_pairs={{0,64},{16,80},{32,96},{48,112},{64,128},{80,144},{96,160},{112,17... | collective-permute-start | bytes 3932168 | tf_op jit(solution)/shard_map/ppermute | solution.py:189
  42.2 79.2 %all-to-all-start.1 = ((bf16[16,128,768]{2,1,0:T(8,128)(2,1)}), bf16[16,128,768]{2,1,0:T(8,128)(2,1)}, u32[]{:S(2)}, u32[]{:S(2)}) async-start(bf16[16,128,768]{2,1,0:T(8,128)(2,1)} %hold.1), calls=%async_computation.1 | async-start | bytes 6291456 | tf_op jit(solution)/shard_map/all_to_all | solution.py:258
  48.3 0.7 copy-start.5
  48.9 0.7 copy-start.6
  54.5 40.4 %collective-permute-start.15 = (bf16[256,2560]{1,0:T(8,128)(2,1)}, bf16[256,2560]{1,0:T(8,128)(2,1)S(1)}, u32[]{:S(2)}, u32[]{:S(2)}) collective-permute-start(bf16[256,2560]{1,0:T(8,128)(2,1)} %get-tuple-element.8), channel_id=1, source_target_pairs={{0,16},{16,0},{32,48},{48,32},{64,80},{80,64},{96,112},{112,96},{1... | collective-permute-start | bytes 3932168 | tf_op jit(solution)/shard_map/ppermute | solution.py:268
  73.1 17.5 %collective-permute-start.13 = (bf16[320,1024]{1,0:T(8,128)(2,1)S(1)}, bf16[320,1024]{1,0:T(8,128)(2,1)S(1)}, u32[]{:S(2)}, u32[]{:S(2)}) collective-permute-start(bf16[320,1024]{1,0:T(8,128)(2,1)S(1)} %slice.34), channel_id=1, source_target_pairs={{0,64},{16,80},{32,96},{48,112},{64,128},{80,144},{96,160},{112,17... | collective-permute-start | bytes 1966088 | tf_op jit(solution)/shard_map/ppermute | solution.py:191
  74.8 16.7 %collective-permute-start.14 = (bf16[320,1024]{1,0:T(8,128)(2,1)S(1)}, bf16[320,1024]{1,0:T(8,128)(2,1)S(1)}, u32[]{:S(2)}, u32[]{:S(2)}) collective-permute-start(bf16[320,1024]{1,0:T(8,128)(2,1)S(1)} %slice.35), channel_id=1, source_target_pairs={{0,192},{16,208},{32,224},{48,240},{64,0},{80,16},{96,32},{112,48}... | collective-permute-start | bytes 1966088 | tf_op jit(solution)/shard_map/ppermute | solution.py:192
  100.0 25.1 %copy-start.2 = (s32[8]{0:T(128)S(1)}, s32[8]{0:T(128)}, u32[]{:S(2)}) copy-start(s32[8]{0:T(128)} %constant.81.clone) | copy-start | bytes 100
  100.0 25.2 %collective-permute-start.16 = (f32[256,1024]{1,0:T(8,128)}, f32[256,1024]{1,0:T(8,128)S(1)}, u32[]{:S(2)}, u32[]{:S(2)}) collective-permute-start(f32[256,1024]{1,0:T(8,128)} %fusion.6), channel_id=1, source_target_pairs={{0,16},{16,0},{32,48},{48,32},{64,80},{80,64},{96,112},{112,96},{1... | collective-permute-start | bytes 3145736 | tf_op jit(solution)/shard_map/ppermute | solution.py:271
  121.5 32.7 %all-to-all-start = ((bf16[16,128,256]{2,1,0:T(8,128)(2,1)}), bf16[16,128,256]{2,1,0:T(8,128)(2,1)S(1)}, u32[]{:S(2)}, u32[]{:S(2)}) async-start(bf16[16,128,256]{2,1,0:T(8,128)(2,1)} %pack.2), calls=%async_computation | async-start | bytes 2097152 | tf_op jit(solution)/shard_map/all_to_all | solution.py:258
  129.7 8.2 %collective-permute-start.17 = (bf16[256,512]{1,0:T(8,128)(2,1)S(1)}, bf16[256,512]{1,0:T(8,128)(2,1)S(1)}, u32[]{:S(2)}, u32[]{:S(2)}) collective-permute-start(bf16[256,512]{1,0:T(8,128)(2,1)S(1)} %get-tuple-element.14), channel_id=1, source_target_pairs={{0,1},{1,0},{2,3},{3,2},{4,5},{5,4},{6,7},{7,6},{8,9},{9,8},{10,11... | collective-permute-start | bytes 786440 | tf_op jit(solution)/shard_map/ppermute | solution.py:274

commit v5 on v4

--- a/solution.py
+++ b/solution.py
@@ -105,26 +105,33 @@
 
 
 def self_kernel(q_ref, k_ref, v_ref, out_ref):
-    for head in range(q_ref.shape[1] // HD):
-        cols = slice(head * HD, (head + 1) * HD)
-        out_ref[:, cols] = softmax_mix(
-            q_ref[:, cols], k_ref[:, cols], v_ref[:, cols], None
-        ).astype(jnp.bfloat16)
+    rows = math.gcd(q_ref.shape[0], 256)
+    for start in range(0, q_ref.shape[0], rows):
+        for head in range(q_ref.shape[1] // HD):
+            cols = slice(head * HD, (head + 1) * HD)
+            out_ref[start : start + rows, cols] = softmax_mix(
+                q_ref[start : start + rows, cols], k_ref[:, cols], v_ref[:, cols], None
+            ).astype(jnp.bfloat16)
 
 
 def cross_kernel(bias_ref, cq_ref, tk_ref, tv_ref, self_ref, out_ref):
-    for head in range(cq_ref.shape[1] // HD):
-        cols = slice(head * HD, (head + 1) * HD)
-        cross_out = softmax_mix(cq_ref[:, cols], tk_ref[:, cols], tv_ref[:, cols], bias_ref[...])
-        out_ref[:, cols] = (
-            self_ref[:, cols].astype(jnp.float32)
-            + cross_out.astype(jnp.bfloat16).astype(jnp.float32)
-        ).astype(jnp.bfloat16)
+    rows = math.gcd(cq_ref.shape[0], 512)
+    for start in range(0, cq_ref.shape[0], rows):
+        here = slice(start, start + rows)
+        for head in range(cq_ref.shape[1] // HD):
+            cols = slice(head * HD, (head + 1) * HD)
+            cross_out = softmax_mix(
+                cq_ref[here, cols], tk_ref[:, cols], tv_ref[:, cols], bias_ref[...]
+            )
+            out_ref[here, cols] = (
+                self_ref[here, cols].astype(jnp.float32)
+                + cross_out.astype(jnp.bfloat16).astype(jnp.float32)
+            ).astype(jnp.bfloat16)
 
 
 def self_attend(qkv, width):
     rows = qkv.shape[0]
-    block = math.gcd(rows, 256)
+    block = math.gcd(rows, 1024)
     pairs = rows * width * rows
     return pl.pallas_call(
         self_kernel,
@@ -136,7 +143,7 @@
         ],
         out_specs=pl.BlockSpec((block, width), lambda i: (i, 0)),
         out_shape=jax.ShapeDtypeStruct((rows, width), jnp.bfloat16),
-        compiler_params=pltpu.CompilerParams(vmem_limit_bytes=32 << 20),
+        compiler_params=pltpu.CompilerParams(vmem_limit_bytes=40 << 20),
         cost_estimate=pl.CostEstimate(
             flops=4 * pairs, bytes_accessed=8 * rows * width, transcendentals=pairs // HD
         ),
@@ -147,7 +154,7 @@
 def cross_attend(bias, cq, text, self_out):
     rows, width = cq.shape
     slots = text.shape[0]
-    block = math.gcd(rows, 512)
+    block = math.gcd(rows, 1024)
     pairs = rows * width * slots
     row_spec = pl.BlockSpec((block, width), lambda i: (i, 0))
     return pl.pallas_call(
@@ -170,9 +177,9 @@
     )(bias, cq, text, text, self_out)
 
 
-def gather_weights(weights, x_hi, core):
+def gather_weights(weights, x_hi, core, *until):
     wide = jnp.concatenate([weights, lax.ppermute(weights, "seq", XL_SWAP)], axis=1)
-    first = lax.ppermute(wide, "prompt", REGROUP_A)
+    first = hold(lax.ppermute(wide, "prompt", REGROUP_A), *until)
     second = lax.ppermute(wide, "prompt", REGROUP_B)
     same = x_hi == core
     keep = jnp.where(same, wide, second)
@@ -185,12 +192,27 @@
 
 
 def ring_y(chunk):
-    half = chunk.shape[0] // 2
+    half = chunk.shape[1] // 2
     before = lax.ppermute(chunk, "prompt", y_shift(1))
     after = lax.ppermute(chunk, "prompt", y_shift(-1))
-    far_top = lax.ppermute(before[:half], "prompt", y_shift(1))
-    far_bottom = lax.ppermute(after[half:], "prompt", y_shift(-1))
-    return jnp.concatenate([chunk, after, far_top, far_bottom, before], axis=0)
+    far_left = lax.ppermute(before[:, :half], "prompt", y_shift(1))
+    far_right = lax.ppermute(after[:, half:], "prompt", y_shift(-1))
+    return (chunk, after, before), (far_left, far_right)
+
+
+def project(text, near, far):
+    deep, columns = near[0].shape
+    chunks = [text[:, k * deep : (k + 1) * deep] for k in range(Y)]
+
+    def dot(rows, weights):
+        return jnp.dot(rows, weights, preferred_element_type=jnp.float32)
+
+    sums = dot(chunks[0], near[0]) + dot(chunks[1], near[1]) + dot(chunks[3], near[2])
+    sums = lax.optimization_barrier(sums)
+    return [
+        sums[:, : columns // 2] + dot(chunks[2], far[0]),
+        sums[:, columns // 2 :] + dot(chunks[2], far[1]),
+    ]
 
 
 def ring_z(block):
@@ -259,27 +281,29 @@
         return heads.reshape(-1, packed.shape[2])
 
     offsets, pieces = ring_z(context[0])
-    chunk = gather_weights(jnp.concatenate([key_weight, value_weight], axis=1), x_hi, core)
+    both = jnp.concatenate([key_weight, value_weight], axis=1)
+    chunk = gather_weights(both, x_hi, core, *pieces[-2:])
     packed = pack([queries[0], self_keys[0], self_values[0]], parts)
     qkv = to_heads(hold(packed, *pieces[-4:-2]))
-    weights = ring_y(chunk)
+    near, far = ring_y(chunk)
     text_rows = context.shape[1]
     mine, theirs = split_text(pieces, y, core)
     other = lax.ppermute(theirs, "prompt", CORE_SWAP)
-    other_part = jnp.dot(other, weights, preferred_element_type=jnp.float32)
-    own_part = jnp.dot(mine, weights, preferred_element_type=jnp.float32)
-    summed = (own_part + lax.ppermute(other_part, "prompt", CORE_SWAP)).astype(jnp.bfloat16)
-    own_columns, their_columns = summed[:, : 2 * width], summed[:, 2 * width :]
-    text_kv = jnp.concatenate(
-        [own_columns, lax.ppermute(their_columns, "seq", XL_SWAP)], axis=0
-    )
+    other_parts = project(other, near, far)
+    own_parts = lax.optimization_barrier(project(mine, near, far))
+    own_columns, their_columns = [
+        (own + lax.ppermute(part, "prompt", CORE_SWAP)).astype(jnp.bfloat16)
+        for own, part in zip(own_parts, other_parts)
+    ]
+    swapped = lax.ppermute(their_columns, "seq", XL_SWAP)
     source_z = (z + jnp.array(offsets, jnp.int32)) % Z
     source_seq = jnp.stack([source_z * 2 + x_lo, source_z * 2 + 1 - x_lo]).reshape(-1, 1)
     slot = (source_seq * text_rows + jnp.arange(text_rows, dtype=jnp.int32)[None, :]).reshape(1, -1)
     bias = jnp.where(slot < lengths[0], 0.0, -jnp.inf).astype(jnp.float32)
 
-    cq = to_heads(pack([cross_queries[0]], parts))
+    cq = to_heads(hold(pack([cross_queries[0]], parts), own_columns, their_columns))
     self_out = self_attend(qkv, width)
+    text_kv = jnp.concatenate([own_columns, hold(swapped, self_out)], axis=0)
     attended = cross_attend(bias, cq, text_kv, self_out)
     back = lax.all_to_all(
         attended.reshape(parts, -1, width), "seq", split_axis=0, concat_axis=0

time: 197 us -> 185 us (0.939)
  waiting for transfers between devices: 60.5 us -> 51.6 us
  matrix products: 9.57 us -> 12.9 us
  Pallas kernels: 33.1 us -> 30.1 us
  local copies, waits for them, and re-layouts: 13.6 us -> 10.7 us
  blocking collectives: 34.3 us -> 31.6 us
    ppermute x1, waiting for transfers between devices: 0.01 us -> 20.3 us  [ring_y(): after = lax.ppermute(chunk, 'prompt', y_shift(-1))]
    ppermute x1, waiting for transfers between devices: 17.4 us -> 0.01 us  [ring_y(): before = lax.ppermute(chunk, 'prompt', y_shift(1))]
    ppermute x5 -> x6, waiting for transfers between devices: 15.9 us -> 0.26 us  [the longest x2 0.25 us: body(): lax.ppermute(part, 'prompt', CORE_SWAP)]
    all_to_all x2, waiting for transfers between devices: 19.4 us -> 23.5 us  [to_heads(): heads = lax.all_to_all(packed, 'seq', split_axis=0, concat_axis=0)]
    unnamed x19 -> x22, local copies, waits for them, and re-layouts: 7.45 us -> 3.42 us
    slice x2 -> x7, local copies, waits for them, and re-layouts: 1.18 us -> 4.85 us  [hold(): marks = [mark[:16, :HD] for mark in until]]
    dot_general x2 -> x10, matrix products: 9.57 us -> 12.9 us  [dot(): return jnp.dot(rows, weights, preferred_element_type=jnp.float32)]
    select_n x0 -> x1, other arithmetic: none -> 2.89 us  [gather_weights(): jnp.where(core == 0, jnp.where(same, jnp.concatenate([keep, first]), jnp....]
  transfers between devices with their start and end apart: 20 -> 21, of which waited for: 7 -> 8; matrix products, arithmetic and copies ran while one was open for 13% -> 15% of each run, Pallas kernels for 13% -> 13%
where the time goes in v5:
time: 185 us; the launch traced here: 183 us
  waiting for transfers between devices  51.6 us (28%)
  starting transfers between devices  39.4 us (21%)
  blocking collectives  31.6 us (17%)
  Pallas kernels  30.1 us (16%)
  matrix products  12.9 us (7%)
  local copies, waits for them, and re-layouts  10.7 us (6%)
  other arithmetic  5.88 us (3%)
    all_to_all x1, blocking collectives, body(): lax.all_to_all(attended.reshape(parts, -1, width), 'seq', split_axis=0, c...  31.6 us
    all_to_all x2, waiting for transfers between devices, to_heads(): heads = lax.all_to_all(packed, 'seq', split_axis=0, concat_axis=0)  23.5 us
    ppermute x1, waiting for transfers between devices, ring_y(): after = lax.ppermute(chunk, 'prompt', y_shift(-1))  20.3 us
    pallas_call x1, Pallas kernels, self_attend(): pl.pallas_call(self_kernel, grid=(rows // block,), in_specs=[pl.BlockSpec...  14.3 us
    dot_general x10, matrix products, dot(): return jnp.dot(rows, weights, preferred_element_type=jnp.float32)  12.9 us
    ppermute x3, starting transfers between devices, ring_z(): down = lax.ppermute(down, 'seq', z_shift(-1))  10.4 us
    all_to_all x2, starting transfers between devices, to_heads(): heads = lax.all_to_all(packed, 'seq', split_axis=0, concat_axis=0)  9.83 us
    ppermute x3, waiting for transfers between devices, ring_z(): up = lax.ppermute(up, 'seq', z_shift(1))  7.5 us
  transfers between devices with their start and end apart: 21, of which 8 were waited for; matrix products, arithmetic and copies ran while one was open for 15% of the time, Pallas kernels for 13%

profile of v5, /device:TPU:8, one launch (start us, length us, event | category | flops | bytes accessed | tf_op | source)
XLA Modules:
  0.0 183.3 jit_solution(1203377731905152117)
XLA Ops:
  0.0 1.9 %collective-permute-start = (bf16[32,5120]{1,0:T(8,128)(2,1)}, bf16[32,5120]{1,0:T(8,128)(2,1)S(1)}, u32[]{:S(2)}, u32[]{:S(2)}) collective-permute-start(bf16[32,5120]{1,0:T(8,128)(2,1)} %bitcast.33), channel_id=1, source_target_pairs={{0,2},{1,3},{2,4},{3,5},{4,6},{5,7},{6,8},{7,9},{8,10},{9,11},{10,... | collective-permute-start | bytes 983048 | tf_op jit(solution)/shard_map/ppermute | solution.py:223
  1.9 3.9 %collective-permute-start.1 = (bf16[32,5120]{1,0:T(8,128)(2,1)}, bf16[32,5120]{1,0:T(8,128)(2,1)S(1)}, u32[]{:S(2)}, u32[]{:S(2)}) collective-permute-start(bf16[32,5120]{1,0:T(8,128)(2,1)} %bitcast.34), channel_id=1, source_target_pairs={{0,14},{1,15},{2,0},{3,1},{4,2},{5,3},{6,4},{7,5},{8,6},{9,7},{10,... | collective-permute-start | bytes 983048 | tf_op jit(solution)/shard_map/ppermute | solution.py:224
  6.9 1.6 collective-permute-start.8
  10.3 3.4 %collective-permute-done.refs_1_.refs_10_ = bf16[32,5120]{1,0:T(8,128)(2,1)S(1)} collective-permute-done((bf16[32,5120]{1,0:T(8,128)(2,1)}, bf16[32,5120]{1,0:T(8,128)(2,1)S(1)}, u32[]{:S(2)}, u32[]{:S(2)}) %collective-permute-start) | collective-permute-done | bytes 327712 | tf_op jit(solution)/shard_map/ppermute | solution.py:223
  13.8 3.2 %collective-permute-start.3 = (bf16[32,5120]{1,0:T(8,128)(2,1)S(1)}, bf16[32,5120]{1,0:T(8,128)(2,1)}, u32[]{:S(2)}, u32[]{:S(2)}) collective-permute-start(bf16[32,5120]{1,0:T(8,128)(2,1)S(1)} %collective-permute-done.1.refs_2_.refs_11_), channel_id=1, source_target_pairs={{0,14},{1,15},{2,0},{3,1},{4,2},{5,3},{6,4},{7,5},{8,6},{9,7},{10,... | collective-permute-start | bytes 983048 | tf_op jit(solution)/shard_map/ppermute | solution.py:224
  17.8 4.3 %collective-permute-start.10 = (bf16[320,1024]{1,0:T(8,128)(2,1)S(1)}, bf16[320,1024]{1,0:T(8,128)(2,1)S(1)}, u32[]{:S(2)}, u32[]{:S(2)}) collective-permute-start(bf16[320,1024]{1,0:T(8,128)(2,1)S(1)} %constant_dynamic-update-slice_fusion), channel_id=1, source_target_pairs={{0,32},{32,48},{48,16},{16,0},{64,96},{96,112},{112,80},{80,64},{1... | collective-permute-start | bytes 1966088 | tf_op jit(solution)/shard_map/ppermute | solution.py:182
  22.1 1.8 collective-permute-done.2.refs_3_.refs_12_
  23.9 3.2 %collective-permute-start.5 = (bf16[32,5120]{1,0:T(8,128)(2,1)}, bf16[32,5120]{1,0:T(8,128)(2,1)S(1)}, u32[]{:S(2)}, u32[]{:S(2)}) collective-permute-start(bf16[32,5120]{1,0:T(8,128)(2,1)} %collective-permute-done.3.refs_4_.refs_13_), channel_id=1, source_target_pairs={{0,14},{1,15},{2,0},{3,1},{4,2},{5,3},{6,4},{7,5},{8,6},{9,7},{10,... | collective-permute-start | bytes 983048 | tf_op jit(solution)/shard_map/ppermute | solution.py:224
  27.1 3.1 %pack.3.refs_0_ = bf16[16,128,768]{2,1,0:T(8,128)(2,1)} custom-call(bf16[128,4096]{1,0:T(8,128)(2,1)} %bitcast.30, bf16[128,4096]{1,0:T(8,128)(2,1)} %bitcast.31, bf16[128,4096]{1,0:T(8,128)(2,1)} %bitcast.32), custom_call_target="tpu_custom_call" | custom-call | bytes 6291456 | tf_op jit(solution)/shard_map/pack/pallas_call | solution.py:46
  30.9 2.3 %collective-permute-done.4.refs_5_.refs_14_ = bf16[32,5120]{1,0:T(8,128)(2,1)S(1)} collective-permute-done((bf16[32,5120]{1,0:T(8,128)(2,1)S(1)}, bf16[32,5120]{1,0:T(8,128)(2,1)S(1)}, u32[]{:S(2)}, u32[]{:S(2)}) %collective-permute-start.4) | collective-permute-done | bytes 327712 | tf_op jit(solution)/shard_map/ppermute | solution.py:223
  33.3 3.3 %collective-permute-start.7 = (bf16[16,5120]{1,0:T(8,128)(2,1)S(1)}, bf16[16,5120]{1,0:T(8,128)(2,1)}, u32[]{:S(2)}, u32[]{:S(2)}) collective-permute-start(bf16[16,5120]{1,0:T(8,128)(2,1)S(1)} %slice.93), channel_id=1, source_target_pairs={{0,14},{1,15},{2,0},{3,1},{4,2},{5,3},{6,4},{7,5},{8,6},{9,7},{10,... | collective-permute-start | bytes 491528 | tf_op jit(solution)/shard_map/ppermute | solution.py:228
  37.8 5.9 %all-to-all-start.1 = ((bf16[16,128,768]{2,1,0:T(8,128)(2,1)}), bf16[16,128,768]{2,1,0:T(8,128)(2,1)}, u32[]{:S(2)}, u32[]{:S(2)}) async-start(bf16[16,128,768]{2,1,0:T(8,128)(2,1)} %hold.6), calls=%async_computation.1 | async-start | bytes 6291456 | tf_op jit(solution)/shard_map/all_to_all | solution.py:280
  46.6 2.9 %select_select_fusion = bf16[640,1024]{1,0:T(8,128)(2,1)} fusion(bf16[320,1024]{1,0:T(8,128)(2,1)S(1)} %broadcast_select_fusion, bf16[320,1024]{1,0:T(8,128)(2,1)} %hold.4, pred[]{:T(512)S(6)} %eq.13, pred[]{:T(512)S(6)} %eq.12), kind=kLoop, calls=%fused_computation.6 | loop fusion | flops 7208960 | bytes 2621442 | tf_op jit(solution)/shard_map/jit(_where)/select_n | solution.py:186
  49.4 1.6 collective-permute-start.12
  51.5 4.9 %split_text.1 = (bf16[256,2560]{1,0:T(8,128)(2,1)}, bf16[256,2560]{1,0:T(8,128)(2,1)}) custom-call(s32[2]{0:T(128)} %pad_add_fusion.where_ref, bf16[32,5120]{1,0:T(8,128)(2,1)} %bitcast.35, bf16[32,5120]{1,0:T(8,128)(2,1)} %copy-done.7, bf16[32,5120]{1,0:T(8,128)(2,1)} %copy-done.8, bf16[32,5120]{1,0:T(8,128)(2,1)} %copy-done.9, ...), custom_call_target="tpu_custom_call" | custom-call | flops 399999991808 | bytes 5242880 | tf_op jit(solution)/shard_map/split_text/pallas_call | solution.py:254
  56.4 2.1 %pack.2.refs_0_ = bf16[16,128,256]{2,1,0:T(8,128)(2,1)} custom-call(bf16[128,4096]{1,0:T(8,128)(2,1)} %bitcast.29), custom_call_target="tpu_custom_call" | custom-call | bytes 2097152 | tf_op jit(solution)/shard_map/pack/pallas_call | solution.py:46
  58.5 20.3 %collective-permute-done.11 = bf16[640,1024]{1,0:T(8,128)(2,1)} collective-permute-done((bf16[640,1024]{1,0:T(8,128)(2,1)}, bf16[640,1024]{1,0:T(8,128)(2,1)}, u32[]{:S(2)}, u32[]{:S(2)}) %collective-permute-start.11) | collective-permute-done | bytes 1310752 | tf_op jit(solution)/shard_map/ppermute | solution.py:197
  81.8 1.7 collective-permute-start.13
  83.4 1.9 %fusion.2 = f32[256,1024]{1,0:T(8,128)S(1)} fusion(bf16[640,1024]{1,0:T(8,128)(2,1)} %collective-permute-done.12, bf16[256,2560]{1,0:T(8,128)(2,1)S(1)} %collective-permute-done.15), kind=kOutput, calls=%fused_computation.15 | convolution fusion | flops 335544320 | bytes 2686976 | tf_op jit(solution)/shard_map/dot_general | solution.py:208
  85.3 1.9 %fusion.4 = f32[256,1024]{1,0:T(8,128)S(1)} fusion(bf16[640,1024]{1,0:T(8,128)(2,1)} %collective-permute-done.11, bf16[256,2560]{1,0:T(8,128)(2,1)S(1)} %collective-permute-done.15), kind=kOutput, calls=%fused_computation.17 | convolution fusion | flops 335544320 | bytes 2686976 | tf_op jit(solution)/shard_map/dot_general | solution.py:208
  87.2 2.0 %fusion = f32[256,1024]{1,0:T(8,128)S(1)} fusion(f32[256,1024]{1,0:T(8,128)S(1)} %fusion.2, f32[256,1024]{1,0:T(8,128)S(1)} %fusion.4, bf16[640,1024]{1,0:T(8,128)(2,1)} %select_select_fusion, bf16[256,2560]{1,0:T(8,128)(2,1)S(1)} %collective-permute-done.15), kind=kOutput, calls=%fused_computation.1 | convolution fusion | flops 336068608 | bytes 4784128 | tf_op jit(solution)/shard_map/dot_general | solution.py:208
  89.2 1.9 %fusion.9 = f32[256,1024]{1,0:T(8,128)S(1)} fusion(bf16[640,1024]{1,0:T(8,128)(2,1)} %collective-permute-done.11, bf16[256,2560]{1,0:T(8,128)(2,1)S(1)} %copy-done.1), kind=kOutput, calls=%fused_computation.23 | convolution fusion | flops 335544320 | bytes 2686976 | tf_op jit(solution)/shard_map/dot_general | solution.py:208
  91.1 1.9 %fusion.7 = f32[256,1024]{1,0:T(8,128)S(1)} fusion(bf16[640,1024]{1,0:T(8,128)(2,1)} %collective-permute-done.12, bf16[256,2560]{1,0:T(8,128)(2,1)S(1)} %copy-done.1), kind=kOutput, calls=%fused_computation.21 | convolution fusion | flops 335544320 | bytes 2686976 | tf_op jit(solution)/shard_map/dot_general | solution.py:208
  93.0 1.9 %fusion.1 = f32[256,1024]{1,0:T(8,128)S(1)} fusion(f32[256,1024]{1,0:T(8,128)S(1)} %fusion.7, f32[256,1024]{1,0:T(8,128)S(1)} %fusion.9, bf16[640,1024]{1,0:T(8,128)(2,1)} %select_select_fusion, bf16[256,2560]{1,0:T(8,128)(2,1)S(1)} %copy-done.1), kind=kOutput, calls=%fused_computation.3 | convolution fusion | flops 336068608 | bytes 4784128 | tf_op jit(solution)/shard_map/dot_general | solution.py:208
  98.8 15.2 %all-to-all-done.1 = bf16[16,128,768]{2,1,0:T(8,128)(2,1)} async-done(((bf16[16,128,768]{2,1,0:T(8,128)(2,1)}), bf16[16,128,768]{2,1,0:T(8,128)(2,1)}, u32[]{:S(2)}, u32[]{:S(2)}) %all-to-all-start.1) | async-done | bytes 3145760 | tf_op jit(solution)/shard_map/all_to_all | solution.py:280
  114.0 3.9 %all-to-all-start = ((bf16[16,128,256]{2,1,0:T(8,128)(2,1)}), bf16[16,128,256]{2,1,0:T(8,128)(2,1)S(1)}, u32[]{:S(2)}, u32[]{:S(2)}) async-start(bf16[16,128,256]{2,1,0:T(8,128)(2,1)} %hold.5), calls=%async_computation | async-start | bytes 2097152 | tf_op jit(solution)/shard_map/all_to_all | solution.py:280
  118.9 2.1 %collective-permute-start.18 = (bf16[256,512]{1,0:T(8,128)(2,1)S(1)}, bf16[256,512]{1,0:T(8,128)(2,1)S(1)}, u32[]{:S(2)}, u32[]{:S(2)}) collective-permute-start(bf16[256,512]{1,0:T(8,128)(2,1)S(1)} %add_convert_fusion), channel_id=1, source_target_pairs={{0,1},{1,0},{2,3},{3,2},{4,5},{5,4},{6,7},{7,6},{8,9},{9,8},{10,11... | collective-permute-start | bytes 786440 | tf_op jit(solution)/shard_map/ppermute | solution.py:298
  121.0 14.3 %self_attend.1.self_ref = bf16[2048,256]{1,0:T(8,128)(2,1)S(1)} custom-call(bf16[2048,768]{1,0:T(8,128)(2,1)} %bitcast.11.q_ref.k_ref.v_ref, bf16[2048,768]{1,0:T(8,128)(2,1)} %bitcast.11.q_ref.k_ref.v_ref, bf16[2048,768]{1,0:T(8,128)(2,1)} %bitcast.11.q_ref.k_ref.v_ref), custom_call_target="tpu_custom_call" | custom-call | flops 4294967296 | bytes 4194304 | tf_op jit(solution)/shard_map/self_attend/pallas_call | solution.py:136
  137.6 8.3 %all-to-all-done = bf16[16,128,256]{2,1,0:T(8,128)(2,1)S(1)} async-done(((bf16[16,128,256]{2,1,0:T(8,128)(2,1)}), bf16[16,128,256]{2,1,0:T(8,128)(2,1)S(1)}, u32[]{:S(2)}, u32[]{:S(2)}) %all-to-all-start) | async-done | bytes 1048608 | tf_op jit(solution)/shard_map/all_to_all | solution.py:280
  145.9 3.5 %cross_attend.1 = bf16[2048,256]{1,0:T(8,128)(2,1)S(1)} custom-call(f32[1,512]{1,0:T(1,128)S(1)} %select_n.67.bias_ref, bf16[2048,256]{1,0:T(8,128)(2,1)S(1)} %bitcast.27, bf16[512,512]{1,0:T(8,128)(2,1)S(1)} %pad_maximum_fusion.2.tk_ref.tv_ref, bf16[512,512]{1,0:T(8,128)(2,1)S(1)} %pad_maximum_fusion.2.tk_ref.tv_ref, bf16[2048,256]{1,0:T(8,128)(2,1)S(1)} %self_attend.1.self_ref), custom_call_target="tpu_custom_call" | custom-call | flops 1073741824 | bytes 3145728 | tf_op jit(solution)/shard_map/cross_attend/pallas_call | solution.py:160
  149.4 31.6 %all_to_all.15.in_ref = bf16[16,128,256]{2,1,0:T(8,128)(2,1)} all-to-all(bf16[16,128,256]{2,1,0:T(8,128)(2,1)S(1)} %bitcast.28), channel_id=1, replica_groups=mesh['prompt'=16,'seq'=16] {'seq'}, dimensions={0} | all-to-all | bytes 2097152 | tf_op jit(solution)/shard_map/all_to_all | solution.py:308
  181.0 2.3 %unpack.1 = bf16[128,4096]{1,0:T(8,128)(2,1)} custom-call(bf16[16,128,256]{2,1,0:T(8,128)(2,1)} %all_to_all.15.in_ref), custom_call_target="tpu_custom_call" | custom-call | tf_op jit(solution)/shard_map/unpack/pallas_call | solution.py:84
  (78 shorter events, 18.2 us)
Async XLA Ops:
  0.0 13.8 %collective-permute-start = (bf16[32,5120]{1,0:T(8,128)(2,1)}, bf16[32,5120]{1,0:T(8,128)(2,1)S(1)}, u32[]{:S(2)}, u32[]{:S(2)}) collective-permute-start(bf16[32,5120]{1,0:T(8,128)(2,1)} %bitcast.33), channel_id=1, source_target_pairs={{0,2},{1,3},{2,4},{3,5},{4,6},{5,7},{6,8},{7,9},{8,10},{9,11},{10,... | collective-permute-start | bytes 983048 | tf_op jit(solution)/shard_map/ppermute | solution.py:223
  1.9 11.9 %collective-permute-start.1 = (bf16[32,5120]{1,0:T(8,128)(2,1)}, bf16[32,5120]{1,0:T(8,128)(2,1)S(1)}, u32[]{:S(2)}, u32[]{:S(2)}) collective-permute-start(bf16[32,5120]{1,0:T(8,128)(2,1)} %bitcast.34), channel_id=1, source_target_pairs={{0,14},{1,15},{2,0},{3,1},{4,2},{5,3},{6,4},{7,5},{8,6},{9,7},{10,... | collective-permute-start | bytes 983048 | tf_op jit(solution)/shard_map/ppermute | solution.py:224
  6.9 10.1 %collective-permute-start.8 = (bf16[320,512]{1,0:T(8,128)(2,1)S(1)}, bf16[320,512]{1,0:T(8,128)(2,1)S(1)}, u32[]{:S(2)}, u32[]{:S(2)}) collective-permute-start(bf16[320,512]{1,0:T(8,128)(2,1)S(1)} %pad_maximum_fusion.3), channel_id=1, source_target_pairs={{0,1},{1,0},{2,3},{3,2},{4,5},{5,4},{6,7},{7,6},{8,9},{9,8},{10,11... | collective-permute-start | bytes 983048 | tf_op jit(solution)/shard_map/ppermute | solution.py:181
  13.8 10.1 %copy-start.7 = (bf16[32,5120]{1,0:T(8,128)(2,1)}, bf16[32,5120]{1,0:T(8,128)(2,1)S(1)}, u32[]{:S(2)}) copy-start(bf16[32,5120]{1,0:T(8,128)(2,1)S(1)} %collective-permute-done.refs_1_.refs_10_) | copy-start | bytes 983044
  13.8 10.1 %collective-permute-start.2 = (bf16[32,5120]{1,0:T(8,128)(2,1)S(1)}, bf16[32,5120]{1,0:T(8,128)(2,1)S(1)}, u32[]{:S(2)}, u32[]{:S(2)}) collective-permute-start(bf16[32,5120]{1,0:T(8,128)(2,1)S(1)} %collective-permute-done.refs_1_.refs_10_), channel_id=1, source_target_pairs={{0,2},{1,3},{2,4},{3,5},{4,6},{5,7},{6,8},{7,9},{8,10},{9,11},{10,... | collective-permute-start | bytes 983048 | tf_op jit(solution)/shard_map/ppermute | solution.py:223
  13.8 16.5 %copy-start.8 = (bf16[32,5120]{1,0:T(8,128)(2,1)}, bf16[32,5120]{1,0:T(8,128)(2,1)S(1)}, u32[]{:S(2)}) copy-start(bf16[32,5120]{1,0:T(8,128)(2,1)S(1)} %collective-permute-done.1.refs_2_.refs_11_) | copy-start | bytes 983044
  13.8 10.1 %collective-permute-start.3 = (bf16[32,5120]{1,0:T(8,128)(2,1)S(1)}, bf16[32,5120]{1,0:T(8,128)(2,1)}, u32[]{:S(2)}, u32[]{:S(2)}) collective-permute-start(bf16[32,5120]{1,0:T(8,128)(2,1)S(1)} %collective-permute-done.1.refs_2_.refs_11_), channel_id=1, source_target_pairs={{0,14},{1,15},{2,0},{3,1},{4,2},{5,3},{6,4},{7,5},{8,6},{9,7},{10,... | collective-permute-start | bytes 983048 | tf_op jit(solution)/shard_map/ppermute | solution.py:224
  17.1 26.7 %collective-permute-start.9 = (bf16[320,1024]{1,0:T(8,128)(2,1)S(1)}, bf16[320,1024]{1,0:T(8,128)(2,1)S(1)}, u32[]{:S(2)}, u32[]{:S(2)}) collective-permute-start(bf16[320,1024]{1,0:T(8,128)(2,1)S(1)} %constant_dynamic-update-slice_fusion), channel_id=1, source_target_pairs={{16,32},{32,16},{80,96},{96,80},{144,160},{160,144},{208,224},{224... | collective-permute-start | bytes 1966088 | tf_op jit(solution)/shard_map/ppermute | solution.py:183
  17.8 27.9 %collective-permute-start.10 = (bf16[320,1024]{1,0:T(8,128)(2,1)S(1)}, bf16[320,1024]{1,0:T(8,128)(2,1)S(1)}, u32[]{:S(2)}, u32[]{:S(2)}) collective-permute-start(bf16[320,1024]{1,0:T(8,128)(2,1)S(1)} %constant_dynamic-update-slice_fusion), channel_id=1, source_target_pairs={{0,32},{32,48},{48,16},{16,0},{64,96},{96,112},{112,80},{80,64},{1... | collective-permute-start | bytes 1966088 | tf_op jit(solution)/shard_map/ppermute | solution.py:182
  23.9 6.4 %copy-start.9 = (bf16[32,5120]{1,0:T(8,128)(2,1)}, bf16[32,5120]{1,0:T(8,128)(2,1)S(1)}, u32[]{:S(2)}) copy-start(bf16[32,5120]{1,0:T(8,128)(2,1)S(1)} %collective-permute-done.2.refs_3_.refs_12_) | copy-start | bytes 983044
  23.9 9.3 %collective-permute-start.4 = (bf16[32,5120]{1,0:T(8,128)(2,1)S(1)}, bf16[32,5120]{1,0:T(8,128)(2,1)S(1)}, u32[]{:S(2)}, u32[]{:S(2)}) collective-permute-start(bf16[32,5120]{1,0:T(8,128)(2,1)S(1)} %collective-permute-done.2.refs_3_.refs_12_), channel_id=1, source_target_pairs={{0,2},{1,3},{2,4},{3,5},{4,6},{5,7},{6,8},{7,9},{8,10},{9,11},{10,... | collective-permute-start | bytes 983048 | tf_op jit(solution)/shard_map/ppermute | solution.py:223
  23.9 9.3 %collective-permute-start.5 = (bf16[32,5120]{1,0:T(8,128)(2,1)}, bf16[32,5120]{1,0:T(8,128)(2,1)S(1)}, u32[]{:S(2)}, u32[]{:S(2)}) collective-permute-start(bf16[32,5120]{1,0:T(8,128)(2,1)} %collective-permute-done.3.refs_4_.refs_13_), channel_id=1, source_target_pairs={{0,14},{1,15},{2,0},{3,1},{4,2},{5,3},{6,4},{7,5},{8,6},{9,7},{10,... | collective-permute-start | bytes 983048 | tf_op jit(solution)/shard_map/ppermute | solution.py:224
  33.1 4.6 %copy-start.3 = (bf16[32,5120]{1,0:T(8,128)(2,1)}, bf16[32,5120]{1,0:T(8,128)(2,1)S(1)}, u32[]{:S(2)}) copy-start(bf16[32,5120]{1,0:T(8,128)(2,1)S(1)} %collective-permute-done.4.refs_5_.refs_14_) | copy-start | bytes 983044
  33.2 10.6 %collective-permute-start.6 = (bf16[16,5120]{1,0:T(8,128)(2,1)S(1)}, bf16[16,5120]{1,0:T(8,128)(2,1)S(1)}, u32[]{:S(2)}, u32[]{:S(2)}) collective-permute-start(bf16[16,5120]{1,0:T(8,128)(2,1)S(1)} %slice.92), channel_id=1, source_target_pairs={{0,2},{1,3},{2,4},{3,5},{4,6},{5,7},{6,8},{7,9},{8,10},{9,11},{10,... | collective-permute-start | bytes 491528 | tf_op jit(solution)/shard_map/ppermute | solution.py:227
  33.3 4.5 %copy-start.4 = (bf16[32,5120]{1,0:T(8,128)(2,1)}, bf16[32,5120]{1,0:T(8,128)(2,1)S(1)}, u32[]{:S(2)}) copy-start(bf16[32,5120]{1,0:T(8,128)(2,1)S(1)} %collective-permute-done.5.refs_6_.refs_15_) | copy-start | bytes 983044
  33.3 11.2 %collective-permute-start.7 = (bf16[16,5120]{1,0:T(8,128)(2,1)S(1)}, bf16[16,5120]{1,0:T(8,128)(2,1)}, u32[]{:S(2)}, u32[]{:S(2)}) collective-permute-start(bf16[16,5120]{1,0:T(8,128)(2,1)S(1)} %slice.93), channel_id=1, source_target_pairs={{0,14},{1,15},{2,0},{3,1},{4,2},{5,3},{6,4},{7,5},{8,6},{9,7},{10,... | collective-permute-start | bytes 491528 | tf_op jit(solution)/shard_map/ppermute | solution.py:228
  37.8 76.2 %all-to-all-start.1 = ((bf16[16,128,768]{2,1,0:T(8,128)(2,1)}), bf16[16,128,768]{2,1,0:T(8,128)(2,1)}, u32[]{:S(2)}, u32[]{:S(2)}) async-start(bf16[16,128,768]{2,1,0:T(8,128)(2,1)} %hold.6), calls=%async_computation.1 | async-start | bytes 6291456 | tf_op jit(solution)/shard_map/all_to_all | solution.py:280
  43.8 7.7 %copy-start.6 = (bf16[16,5120]{1,0:T(8,128)(2,1)}, bf16[16,5120]{1,0:T(8,128)(2,1)S(1)}, u32[]{:S(2)}) copy-start(bf16[16,5120]{1,0:T(8,128)(2,1)S(1)} %collective-permute-done.6.refs_7_.refs_16_) | copy-start | bytes 491524
  45.7 0.8 copy-start
  49.4 31.2 %collective-permute-start.12 = (bf16[640,1024]{1,0:T(8,128)(2,1)}, bf16[640,1024]{1,0:T(8,128)(2,1)}, u32[]{:S(2)}, u32[]{:S(2)}) collective-permute-start(bf16[640,1024]{1,0:T(8,128)(2,1)} %select_select_fusion), channel_id=1, source_target_pairs={{0,64},{16,80},{32,96},{48,112},{64,128},{80,144},{96,160},{112,17... | collective-permute-start | bytes 3932168 | tf_op jit(solution)/shard_map/ppermute | solution.py:196
  51.0 27.8 %collective-permute-start.11 = (bf16[640,1024]{1,0:T(8,128)(2,1)}, bf16[640,1024]{1,0:T(8,128)(2,1)}, u32[]{:S(2)}, u32[]{:S(2)}) collective-permute-start(bf16[640,1024]{1,0:T(8,128)(2,1)} %select_select_fusion), channel_id=1, source_target_pairs={{0,192},{16,208},{32,224},{48,240},{64,0},{80,16},{96,32},{112,48}... | collective-permute-start | bytes 3932168 | tf_op jit(solution)/shard_map/ppermute | solution.py:197
  56.3 27.1 %collective-permute-start.15 = (bf16[256,2560]{1,0:T(8,128)(2,1)}, bf16[256,2560]{1,0:T(8,128)(2,1)S(1)}, u32[]{:S(2)}, u32[]{:S(2)}) collective-permute-start(bf16[256,2560]{1,0:T(8,128)(2,1)} %get-tuple-element.11), channel_id=1, source_target_pairs={{0,16},{16,0},{32,48},{48,32},{64,80},{80,64},{96,112},{112,96},{1... | collective-permute-start | bytes 3932168 | tf_op jit(solution)/shard_map/ppermute | solution.py:291
  79.9 15.0 %collective-permute-start.14 = (bf16[640,512]{1,0:T(8,128)(2,1)S(1)}, bf16[640,512]{1,0:T(8,128)(2,1)S(1)}, u32[]{:S(2)}, u32[]{:S(2)}) collective-permute-start(bf16[640,512]{1,0:T(8,128)(2,1)S(1)} %slice.99), channel_id=1, source_target_pairs={{0,192},{16,208},{32,224},{48,240},{64,0},{80,16},{96,32},{112,48}... | collective-permute-start | bytes 1966088 | tf_op jit(solution)/shard_map/ppermute | solution.py:199
  81.8 13.7 %collective-permute-start.13 = (bf16[640,512]{1,0:T(8,128)(2,1)S(1)}, bf16[640,512]{1,0:T(8,128)(2,1)S(1)}, u32[]{:S(2)}, u32[]{:S(2)}) collective-permute-start(bf16[640,512]{1,0:T(8,128)(2,1)S(1)} %slice.97), channel_id=1, source_target_pairs={{0,64},{16,80},{32,96},{48,112},{64,128},{80,144},{96,160},{112,17... | collective-permute-start | bytes 1966088 | tf_op jit(solution)/shard_map/ppermute | solution.py:198
  87.2 2.0 %copy-start.1 = (bf16[256,2560]{1,0:T(8,128)(2,1)S(1)}, bf16[256,2560]{1,0:T(8,128)(2,1)}, u32[]{:S(2)}) copy-start(bf16[256,2560]{1,0:T(8,128)(2,1)} %get-tuple-element.9) | copy-start | bytes 3932164
  95.3 2.0 %collective-permute-start.17 = (f32[256,512]{1,0:T(8,128)S(1)}, f32[256,512]{1,0:T(8,128)S(1)}, u32[]{:S(2)}, u32[]{:S(2)}) collective-permute-start(f32[256,512]{1,0:T(8,128)S(1)} %slice_add_fusion), channel_id=1, source_target_pairs={{0,16},{16,0},{32,48},{48,32},{64,80},{80,64},{96,112},{112,96},{1... | collective-permute-start | bytes 1572872 | tf_op jit(solution)/shard_map/ppermute | solution.py:295
  95.8 2.3 %collective-permute-start.16 = (f32[256,512]{1,0:T(8,128)S(1)}, f32[256,512]{1,0:T(8,128)S(1)}, u32[]{:S(2)}, u32[]{:S(2)}) collective-permute-start(f32[256,512]{1,0:T(8,128)S(1)} %slice_add_fusion.1), channel_id=1, source_target_pairs={{0,16},{16,0},{32,48},{48,32},{64,80},{80,64},{96,112},{112,96},{1... | collective-permute-start | bytes 1572872 | tf_op jit(solution)/shard_map/ppermute | solution.py:295
  98.8 19.2 %copy-start.5 = (s32[8]{0:T(128)S(1)}, s32[8]{0:T(128)}, u32[]{:S(2)}) copy-start(s32[8]{0:T(128)} %constant.81.clone) | copy-start | bytes 100
  114.0 31.9 %all-to-all-start = ((bf16[16,128,256]{2,1,0:T(8,128)(2,1)}), bf16[16,128,256]{2,1,0:T(8,128)(2,1)S(1)}, u32[]{:S(2)}, u32[]{:S(2)}) async-start(bf16[16,128,256]{2,1,0:T(8,128)(2,1)} %hold.5), calls=%async_computation | async-start | bytes 2097152 | tf_op jit(solution)/shard_map/all_to_all | solution.py:280
  118.9 17.1 %collective-permute-start.18 = (bf16[256,512]{1,0:T(8,128)(2,1)S(1)}, bf16[256,512]{1,0:T(8,128)(2,1)S(1)}, u32[]{:S(2)}, u32[]{:S(2)}) collective-permute-start(bf16[256,512]{1,0:T(8,128)(2,1)S(1)} %add_convert_fusion), channel_id=1, source_target_pairs={{0,1},{1,0},{2,3},{3,2},{4,5},{5,4},{6,7},{7,6},{8,9},{9,8},{10,11... | collective-permute-start | bytes 786440 | tf_op jit(solution)/shard_map/ppermute | solution.py:298
  135.9 0.7 copy-start.2

commit v6 on v5

--- a/solution.py
+++ b/solution.py
@@ -26,8 +26,7 @@
 SPLIT_FLOPS = 400_000_000_000
 CORE_SWAP = [(p, p ^ 1) for p in range(Y * XH * CORE)]
 XL_SWAP = [(s, s ^ 1) for s in range(Z * XL)]
-REGROUP_A = [(4 * y + a, 4 * y + b) for y in range(Y) for a, b in ((0, 2), (2, 3), (3, 1), (1, 0))]
-REGROUP_B = [(4 * y + a, 4 * y + b) for y in range(Y) for a, b in ((1, 2), (2, 1))]
+XH_SWAP = [(p, p ^ 2) for p in range(Y * XH * CORE)]
 
 
 def pack_kernel(width, parts, *refs):
@@ -177,18 +176,10 @@
     )(bias, cq, text, text, self_out)
 
 
-def gather_weights(weights, x_hi, core, *until):
+def gather_weights(weights, early, *until):
     wide = jnp.concatenate([weights, lax.ppermute(weights, "seq", XL_SWAP)], axis=1)
-    first = hold(lax.ppermute(wide, "prompt", REGROUP_A), *until)
-    second = lax.ppermute(wide, "prompt", REGROUP_B)
-    same = x_hi == core
-    keep = jnp.where(same, wide, second)
-    chunk = jnp.where(
-        core == 0,
-        jnp.where(same, jnp.concatenate([keep, first]), jnp.concatenate([first, keep])),
-        jnp.where(same, jnp.concatenate([first, keep]), jnp.concatenate([keep, first])),
-    )
-    return chunk
+    other = lax.ppermute(hold(wide, early), "prompt", XH_SWAP)
+    return jnp.concatenate([wide, hold(other, *until)], axis=0)
 
 
 def ring_y(chunk):
@@ -230,33 +221,40 @@
 
 
 def split_kernel(count, where_ref, *refs):
-    del where_ref
-    for half in range(CORE):
-        place = 0
-        for ref in refs[half * count : (half + 1) * count]:
-            refs[CORE * count + half][place : place + ref.shape[0], :] = ref[...]
-            place += ref.shape[0]
-
-
-def split_text(pieces, y, core):
+    outs = refs[count:]
+    wide = refs[0].shape[1] // (XH * CORE)
+    for x_hi in range(XH):
+        for core in range(CORE):
+
+            @pl.when((where_ref[1] == x_hi) & (where_ref[2] == core))
+            def _():
+                place = 0
+                for ref in refs[:count]:
+                    rows = slice(place, place + ref.shape[0])
+                    for flip, out in enumerate(outs):
+                        for k in range(XH):
+                            chunk = (x_hi ^ k) * CORE + (core ^ flip)
+                            out[rows, k * wide : (k + 1) * wide] = ref[
+                                :, chunk * wide : (chunk + 1) * wide
+                            ]
+                    place += ref.shape[0]
+
+
+def split_text(pieces, y, x_hi, core):
     depth = pieces[0].shape[1]
     rows = sum(piece.shape[0] for piece in pieces)
-    wide = depth // (Y * CORE)
-
-    def chunk(flip):
-        def place(k, where):
-            return 0, ((where[0] + k) % Y) * CORE + (where[1] + flip) % CORE
-
-        return [pl.BlockSpec((piece.shape[0], wide), place) for piece in pieces]
-
-    shape = jax.ShapeDtypeStruct((rows, Y * wide), jnp.bfloat16)
-    spec = pl.BlockSpec((rows, wide), lambda k, where: (0, k))
+    wide = depth // Y
+    shape = jax.ShapeDtypeStruct((rows, depth // CORE), jnp.bfloat16)
+    spec = pl.BlockSpec((rows, wide // CORE), lambda k, where: (0, k))
     return pl.pallas_call(
         functools.partial(split_kernel, len(pieces)),
         grid_spec=pltpu.PrefetchScalarGridSpec(
             num_scalar_prefetch=1,
             grid=(Y,),
-            in_specs=chunk(0) + chunk(1),
+            in_specs=[
+                pl.BlockSpec((piece.shape[0], wide), lambda k, where: (0, (where[0] + k) % Y))
+                for piece in pieces
+            ],
             out_specs=[spec, spec],
         ),
         out_shape=[shape, shape],
@@ -264,7 +262,7 @@
             flops=SPLIT_FLOPS, bytes_accessed=4 * rows * depth, transcendentals=0
         ),
         name="split_text",
-    )(jnp.stack([y, core]), *pieces, *pieces)
+    )(jnp.stack([y, x_hi, core]), *pieces)
 
 
 def body(
@@ -282,12 +280,12 @@
 
     offsets, pieces = ring_z(context[0])
     both = jnp.concatenate([key_weight, value_weight], axis=1)
-    chunk = gather_weights(both, x_hi, core, *pieces[-2:])
     packed = pack([queries[0], self_keys[0], self_values[0]], parts)
-    qkv = to_heads(hold(packed, *pieces[-4:-2]))
+    chunk = gather_weights(both, packed[0], *pieces[-2:])
+    qkv = to_heads(hold(packed, pieces[-3]))
     near, far = ring_y(chunk)
     text_rows = context.shape[1]
-    mine, theirs = split_text(pieces, y, core)
+    mine, theirs = split_text(pieces, y, x_hi, core)
     other = lax.ppermute(theirs, "prompt", CORE_SWAP)
     other_parts = project(other, near, far)
     own_parts = lax.optimization_barrier(project(mine, near, far))

time: 185 us -> 182 us (0.984)
  matrix products: 12.9 us -> 10.3 us
    ppermute x3, waiting for transfers between devices: 7.5 us -> 0.01 us  [ring_z(): up = lax.ppermute(up, 'seq', z_shift(1))]
    ppermute x3, waiting for transfers between devices: 0.01 us -> 7.18 us  [ring_z(): down = lax.ppermute(down, 'seq', z_shift(-1))]
    ppermute x1, waiting for transfers between devices: 0.01 us -> 3.01 us  [ring_y(): far_left = lax.ppermute(before[:, :half], 'prompt', y_shift(1))]
    select_n x2 -> x0, other arithmetic: 2.96 us -> none  [the longest x1 2.89 us: gather_weights(): jnp.where(core == 0, jnp.where(same, jnp.concatenate([keep, first]), jnp....]
    ppermute x3, starting transfers between devices: 10.4 us -> 13.1 us  [ring_z(): down = lax.ppermute(down, 'seq', z_shift(-1))]
    dot_general x10, matrix products: 12.9 us -> 10.3 us  [dot(): return jnp.dot(rows, weights, preferred_element_type=jnp.float32)]
    concatenate x0 -> x1, other arithmetic: none -> 2.26 us  [gather_weights(): return jnp.concatenate([wide, hold(other, *until)], axis=0)]
    ppermute x2 -> x1, starting transfers between devices: 5.03 us -> 3.02 us  [gather_weights(): other = lax.ppermute(hold(wide, early), 'prompt', XH_SWAP)]
  transfers between devices with their start and end apart: 21 -> 20, of which waited for: 8 -> 9; matrix products, arithmetic and copies ran while one was open for 15% -> 13% of each run, Pallas kernels for 13% -> 14%
where the time goes in v6:
time: 182 us
  waiting for transfers between devices  53 us (29%)
  starting transfers between devices  38.9 us (21%)
  blocking collectives  32.4 us (18%)
  Pallas kernels  30.5 us (17%)
  matrix products  10.3 us (6%)
  local copies, waits for them, and re-layouts  10.2 us (6%)
  other arithmetic  5.16 us (3%)
    all_to_all x1, blocking collectives, body(): lax.all_to_all(attended.reshape(parts, -1, width), 'seq', split_axis=0, c...  32.4 us
    all_to_all x2, waiting for transfers between devices, to_heads(): heads = lax.all_to_all(packed, 'seq', split_axis=0, concat_axis=0)  24 us
    ppermute x1, waiting for transfers between devices, ring_y(): after = lax.ppermute(chunk, 'prompt', y_shift(-1))  18.6 us
    pallas_call x1, Pallas kernels, self_attend(): pl.pallas_call(self_kernel, grid=(rows // block,), in_specs=[pl.BlockSpec...  14.3 us
    ppermute x3, starting transfers between devices, ring_z(): down = lax.ppermute(down, 'seq', z_shift(-1))  13.1 us
    dot_general x10, matrix products, dot(): return jnp.dot(rows, weights, preferred_element_type=jnp.float32)  10.3 us
    all_to_all x2, starting transfers between devices, to_heads(): heads = lax.all_to_all(packed, 'seq', split_axis=0, concat_axis=0)  10.1 us
    ppermute x3, waiting for transfers between devices, ring_z(): down = lax.ppermute(down, 'seq', z_shift(-1))  7.18 us
  transfers between devices with their start and end apart: 20, of which 9 were waited for; matrix products, arithmetic and copies ran while one was open for 13% of the time, Pallas kernels for 14%

profile of v6, /device:TPU:8, one launch (start us, length us, event | category | flops | bytes accessed | tf_op | source)
XLA Modules:
  0.0 181.5 jit_solution(8851022307365140560)
XLA Ops:
  0.0 5.9 %collective-permute-start.1 = (bf16[32,5120]{1,0:T(8,128)(2,1)}, bf16[32,5120]{1,0:T(8,128)(2,1)S(1)}, u32[]{:S(2)}, u32[]{:S(2)}) collective-permute-start(bf16[32,5120]{1,0:T(8,128)(2,1)} %bitcast.34), channel_id=1, source_target_pairs={{0,14},{1,15},{2,0},{3,1},{4,2},{5,3},{6,4},{7,5},{8,6},{9,7},{10,... | collective-permute-start | bytes 983048 | tf_op jit(solution)/shard_map/ppermute | solution.py:215
  5.9 1.0 pad_maximum_fusion.2
  6.9 1.6 collective-permute-start.8
  8.5 3.1 %pack.3.refs_0_ = bf16[16,128,768]{2,1,0:T(8,128)(2,1)} custom-call(bf16[128,4096]{1,0:T(8,128)(2,1)} %bitcast.31, bf16[128,4096]{1,0:T(8,128)(2,1)} %bitcast.32, bf16[128,4096]{1,0:T(8,128)(2,1)} %bitcast.33), custom_call_target="tpu_custom_call" | custom-call | bytes 6291456 | tf_op jit(solution)/shard_map/pack/pallas_call | solution.py:45
  13.1 3.6 %collective-permute-start.3 = (bf16[32,5120]{1,0:T(8,128)(2,1)S(1)}, bf16[32,5120]{1,0:T(8,128)(2,1)S(1)}, u32[]{:S(2)}, u32[]{:S(2)}) collective-permute-start(bf16[32,5120]{1,0:T(8,128)(2,1)S(1)} %collective-permute-done.1.refs_2_), channel_id=1, source_target_pairs={{0,14},{1,15},{2,0},{3,1},{4,2},{5,3},{6,4},{7,5},{8,6},{9,7},{10,... | collective-permute-start | bytes 983048 | tf_op jit(solution)/shard_map/ppermute | solution.py:215
  18.4 3.0 %collective-permute-start.9 = (bf16[320,1024]{1,0:T(8,128)(2,1)}, bf16[320,1024]{1,0:T(8,128)(2,1)S(1)}, u32[]{:S(2)}, u32[]{:S(2)}) collective-permute-start(bf16[320,1024]{1,0:T(8,128)(2,1)} %hold.5), channel_id=1, source_target_pairs={{0,32},{16,48},{32,0},{48,16},{64,96},{80,112},{96,64},{112,80},{1... | collective-permute-start | bytes 1966088 | tf_op jit(solution)/shard_map/ppermute | solution.py:181
  21.4 1.4 collective-permute-done.3.refs_4_
  22.8 3.7 %collective-permute-start.5 = (bf16[32,5120]{1,0:T(8,128)(2,1)S(1)}, bf16[32,5120]{1,0:T(8,128)(2,1)S(1)}, u32[]{:S(2)}, u32[]{:S(2)}) collective-permute-start(bf16[32,5120]{1,0:T(8,128)(2,1)S(1)} %collective-permute-done.3.refs_4_), channel_id=1, source_target_pairs={{0,14},{1,15},{2,0},{3,1},{4,2},{5,3},{6,4},{7,5},{8,6},{9,7},{10,... | collective-permute-start | bytes 983048 | tf_op jit(solution)/shard_map/ppermute | solution.py:215
  26.5 5.2 %collective-permute-done.5.refs_6_ = bf16[32,5120]{1,0:T(8,128)(2,1)S(1)} collective-permute-done((bf16[32,5120]{1,0:T(8,128)(2,1)S(1)}, bf16[32,5120]{1,0:T(8,128)(2,1)S(1)}, u32[]{:S(2)}, u32[]{:S(2)}) %collective-permute-start.5) | collective-permute-done | bytes 327712 | tf_op jit(solution)/shard_map/ppermute | solution.py:215
  31.7 3.8 %collective-permute-start.7 = (bf16[16,5120]{1,0:T(8,128)(2,1)S(1)}, bf16[16,5120]{1,0:T(8,128)(2,1)S(1)}, u32[]{:S(2)}, u32[]{:S(2)}) collective-permute-start(bf16[16,5120]{1,0:T(8,128)(2,1)S(1)} %slice.97), channel_id=1, source_target_pairs={{0,14},{1,15},{2,0},{3,1},{4,2},{5,3},{6,4},{7,5},{8,6},{9,7},{10,... | collective-permute-start | bytes 491528 | tf_op jit(solution)/shard_map/ppermute | solution.py:219
  36.8 5.5 %all-to-all-start.1 = ((bf16[16,128,768]{2,1,0:T(8,128)(2,1)}), bf16[16,128,768]{2,1,0:T(8,128)(2,1)}, u32[]{:S(2)}, u32[]{:S(2)}) async-start(bf16[16,128,768]{2,1,0:T(8,128)(2,1)} %hold.8), calls=%async_computation.1 | async-start | bytes 6291456 | tf_op jit(solution)/shard_map/all_to_all | solution.py:278
  44.5 2.3 %pad_maximum_fusion = bf16[640,1024]{1,0:T(8,128)(2,1)} fusion(bf16[320,1024]{1,0:T(8,128)(2,1)} %hold.6, bf16[320,1024]{1,0:T(8,128)(2,1)S(1)} %constant_dynamic-update-slice_fusion), kind=kLoop, calls=%fused_computation.4 | loop fusion | flops 2621440 | bytes 2621440 | tf_op jit(solution)/shard_map/concatenate | solution.py:182
  47.2 1.6 collective-permute-start.11
  48.8 5.2 %split_text.1 = (bf16[256,2560]{1,0:T(8,128)(2,1)}, bf16[256,2560]{1,0:T(8,128)(2,1)}) custom-call(s32[3]{0:T(128)} %pad_add_fusion.where_ref, bf16[32,5120]{1,0:T(8,128)(2,1)} %bitcast.36, bf16[32,5120]{1,0:T(8,128)(2,1)} %copy-done.14, bf16[32,5120]{1,0:T(8,128)(2,1)} %copy-done.13, bf16[32,5120]{1,0:T(8,128)(2,1)} %collective-permute-done.2.refs_3_, ...), custom_call_target="tpu_custom_call" | custom-call | flops 399999991808 | bytes 5242880 | tf_op jit(solution)/shard_map/split_text/pallas_call | solution.py:249
  54.0 2.1 %pack.2.refs_0_ = bf16[16,128,256]{2,1,0:T(8,128)(2,1)} custom-call(bf16[128,4096]{1,0:T(8,128)(2,1)} %bitcast.30), custom_call_target="tpu_custom_call" | custom-call | bytes 2097152 | tf_op jit(solution)/shard_map/pack/pallas_call | solution.py:45
  56.1 18.6 %collective-permute-done.10 = bf16[640,1024]{1,0:T(8,128)(2,1)} collective-permute-done((bf16[640,1024]{1,0:T(8,128)(2,1)}, bf16[640,1024]{1,0:T(8,128)(2,1)}, u32[]{:S(2)}, u32[]{:S(2)}) %collective-permute-start.10) | collective-permute-done | bytes 1310752 | tf_op jit(solution)/shard_map/ppermute | solution.py:188
  74.7 1.1 slice.105
  76.2 1.1 slice.103
  77.4 2.0 %collective-permute-start.12 = (bf16[640,512]{1,0:T(8,128)(2,1)S(1)}, bf16[640,512]{1,0:T(8,128)(2,1)S(1)}, u32[]{:S(2)}, u32[]{:S(2)}) collective-permute-start(bf16[640,512]{1,0:T(8,128)(2,1)S(1)} %slice.103), channel_id=1, source_target_pairs={{0,64},{16,80},{32,96},{48,112},{64,128},{80,144},{96,160},{112,17... | collective-permute-start | bytes 1966088 | tf_op jit(solution)/shard_map/ppermute | solution.py:189
  79.3 1.9 %fusion.9 = f32[256,1024]{1,0:T(8,128)S(1)} fusion(bf16[640,1024]{1,0:T(8,128)(2,1)} %collective-permute-done.10, bf16[256,2560]{1,0:T(8,128)(2,1)S(1)} %copy-done.4), kind=kOutput, calls=%fused_computation.20 | convolution fusion | flops 335544320 | bytes 2686976 | tf_op jit(solution)/shard_map/dot_general | solution.py:199
  81.2 2.0 %fusion.7 = f32[256,1024]{1,0:T(8,128)S(1)} fusion(bf16[640,1024]{1,0:T(8,128)(2,1)} %collective-permute-done.11, bf16[256,2560]{1,0:T(8,128)(2,1)S(1)} %copy-done.4), kind=kOutput, calls=%fused_computation.18 | convolution fusion | flops 335544320 | bytes 2686976 | tf_op jit(solution)/shard_map/dot_general | solution.py:199
  83.9 1.9 %fusion.4 = f32[256,1024]{1,0:T(8,128)S(1)} fusion(bf16[640,1024]{1,0:T(8,128)(2,1)} %collective-permute-done.10, bf16[256,2560]{1,0:T(8,128)(2,1)S(1)} %collective-permute-done.14), kind=kOutput, calls=%fused_computation.14 | convolution fusion | flops 335544320 | bytes 2686976 | tf_op jit(solution)/shard_map/dot_general | solution.py:199
  85.8 1.9 %fusion.2 = f32[256,1024]{1,0:T(8,128)S(1)} fusion(bf16[640,1024]{1,0:T(8,128)(2,1)} %collective-permute-done.11, bf16[256,2560]{1,0:T(8,128)(2,1)S(1)} %collective-permute-done.14), kind=kOutput, calls=%fused_computation.12 | convolution fusion | flops 335544320 | bytes 2686976 | tf_op jit(solution)/shard_map/dot_general | solution.py:199
  88.3 3.0 %collective-permute-done.12 = bf16[640,512]{1,0:T(8,128)(2,1)S(1)} collective-permute-done((bf16[640,512]{1,0:T(8,128)(2,1)S(1)}, bf16[640,512]{1,0:T(8,128)(2,1)S(1)}, u32[]{:S(2)}, u32[]{:S(2)}) %collective-permute-start.12) | collective-permute-done | bytes 655392 | tf_op jit(solution)/shard_map/ppermute | solution.py:189
  95.1 16.8 %all-to-all-done.1 = bf16[16,128,768]{2,1,0:T(8,128)(2,1)} async-done(((bf16[16,128,768]{2,1,0:T(8,128)(2,1)}), bf16[16,128,768]{2,1,0:T(8,128)(2,1)}, u32[]{:S(2)}, u32[]{:S(2)}) %all-to-all-start.1) | async-done | bytes 3145760 | tf_op jit(solution)/shard_map/all_to_all | solution.py:278
  111.9 4.5 %all-to-all-start = ((bf16[16,128,256]{2,1,0:T(8,128)(2,1)}), bf16[16,128,256]{2,1,0:T(8,128)(2,1)S(1)}, u32[]{:S(2)}, u32[]{:S(2)}) async-start(bf16[16,128,256]{2,1,0:T(8,128)(2,1)} %hold.7), calls=%async_computation | async-start | bytes 2097152 | tf_op jit(solution)/shard_map/all_to_all | solution.py:278
  117.4 2.2 %collective-permute-start.17 = (bf16[256,512]{1,0:T(8,128)(2,1)S(1)}, bf16[256,512]{1,0:T(8,128)(2,1)S(1)}, u32[]{:S(2)}, u32[]{:S(2)}) collective-permute-start(bf16[256,512]{1,0:T(8,128)(2,1)S(1)} %add_convert_fusion), channel_id=1, source_target_pairs={{0,1},{1,0},{2,3},{3,2},{4,5},{5,4},{6,7},{7,6},{8,9},{9,8},{10,11... | collective-permute-start | bytes 786440 | tf_op jit(solution)/shard_map/ppermute | solution.py:296
  119.5 14.3 %self_attend.1.self_ref = bf16[2048,256]{1,0:T(8,128)(2,1)S(1)} custom-call(bf16[2048,768]{1,0:T(8,128)(2,1)} %bitcast.13.q_ref.k_ref.v_ref, bf16[2048,768]{1,0:T(8,128)(2,1)} %bitcast.13.q_ref.k_ref.v_ref, bf16[2048,768]{1,0:T(8,128)(2,1)} %bitcast.13.q_ref.k_ref.v_ref), custom_call_target="tpu_custom_call" | custom-call | flops 4294967296 | bytes 4194304 | tf_op jit(solution)/shard_map/self_attend/pallas_call | solution.py:135
  136.2 7.2 %all-to-all-done = bf16[16,128,256]{2,1,0:T(8,128)(2,1)S(1)} async-done(((bf16[16,128,256]{2,1,0:T(8,128)(2,1)}), bf16[16,128,256]{2,1,0:T(8,128)(2,1)S(1)}, u32[]{:S(2)}, u32[]{:S(2)}) %all-to-all-start) | async-done | bytes 1048608 | tf_op jit(solution)/shard_map/all_to_all | solution.py:278
  143.4 3.5 %cross_attend.1 = bf16[2048,256]{1,0:T(8,128)(2,1)S(1)} custom-call(f32[1,512]{1,0:T(1,128)S(1)} %select_n.41.bias_ref, bf16[2048,256]{1,0:T(8,128)(2,1)S(1)} %bitcast.28, bf16[512,512]{1,0:T(8,128)(2,1)S(1)} %pad_maximum_fusion.1.tk_ref.tv_ref, bf16[512,512]{1,0:T(8,128)(2,1)S(1)} %pad_maximum_fusion.1.tk_ref.tv_ref, bf16[2048,256]{1,0:T(8,128)(2,1)S(1)} %self_attend.1.self_ref), custom_call_target="tpu_custom_call" | custom-call | flops 1073741824 | bytes 3145728 | tf_op jit(solution)/shard_map/cross_attend/pallas_call | solution.py:159
  146.9 32.4 %all_to_all.15.in_ref = bf16[16,128,256]{2,1,0:T(8,128)(2,1)} all-to-all(bf16[16,128,256]{2,1,0:T(8,128)(2,1)S(1)} %bitcast.29), channel_id=1, replica_groups=mesh['prompt'=16,'seq'=16] {'seq'}, dimensions={0} | all-to-all | bytes 2097152 | tf_op jit(solution)/shard_map/all_to_all | solution.py:306
  179.2 2.3 %unpack.1 = bf16[128,4096]{1,0:T(8,128)(2,1)} custom-call(bf16[16,128,256]{2,1,0:T(8,128)(2,1)} %all_to_all.15.in_ref), custom_call_target="tpu_custom_call" | custom-call | tf_op jit(solution)/shard_map/unpack/pallas_call | solution.py:83
  (90 shorter events, 14.9 us)
Async XLA Ops:
  0.0 13.1 %collective-permute-start.1 = (bf16[32,5120]{1,0:T(8,128)(2,1)}, bf16[32,5120]{1,0:T(8,128)(2,1)S(1)}, u32[]{:S(2)}, u32[]{:S(2)}) collective-permute-start(bf16[32,5120]{1,0:T(8,128)(2,1)} %bitcast.34), channel_id=1, source_target_pairs={{0,14},{1,15},{2,0},{3,1},{4,2},{5,3},{6,4},{7,5},{8,6},{9,7},{10,... | collective-permute-start | bytes 983048 | tf_op jit(solution)/shard_map/ppermute | solution.py:215
  5.9 10.9 %collective-permute-start = (bf16[32,5120]{1,0:T(8,128)(2,1)}, bf16[32,5120]{1,0:T(8,128)(2,1)S(1)}, u32[]{:S(2)}, u32[]{:S(2)}) collective-permute-start(bf16[32,5120]{1,0:T(8,128)(2,1)} %bitcast.35), channel_id=1, source_target_pairs={{0,2},{1,3},{2,4},{3,5},{4,6},{5,7},{6,8},{7,9},{8,10},{9,11},{10,... | collective-permute-start | bytes 983048 | tf_op jit(solution)/shard_map/ppermute | solution.py:214
  6.9 10.6 %collective-permute-start.8 = (bf16[320,512]{1,0:T(8,128)(2,1)S(1)}, bf16[320,512]{1,0:T(8,128)(2,1)S(1)}, u32[]{:S(2)}, u32[]{:S(2)}) collective-permute-start(bf16[320,512]{1,0:T(8,128)(2,1)S(1)} %pad_maximum_fusion.2), channel_id=1, source_target_pairs={{0,1},{1,0},{2,3},{3,2},{4,5},{5,4},{6,7},{7,6},{8,9},{9,8},{10,11... | collective-permute-start | bytes 983048 | tf_op jit(solution)/shard_map/ppermute | solution.py:180
  8.5 3.1 %copy-start.6 = (bf16[320,256]{1,0:T(8,128)(2,1)S(1)}, bf16[320,256]{1,0:T(8,128)(2,1)}, u32[]{:S(2)}) copy-start(bf16[320,256]{1,0:T(8,128)(2,1)} %param.14) | copy-start | bytes 491524
  8.5 8.3 %copy-start.7 = (bf16[320,256]{1,0:T(8,128)(2,1)S(1)}, bf16[320,256]{1,0:T(8,128)(2,1)}, u32[]{:S(2)}) copy-start(bf16[320,256]{1,0:T(8,128)(2,1)} %param.15) | copy-start | bytes 491524
  13.1 5.2 %copy-start.13 = (bf16[32,5120]{1,0:T(8,128)(2,1)}, bf16[32,5120]{1,0:T(8,128)(2,1)S(1)}, u32[]{:S(2)}) copy-start(bf16[32,5120]{1,0:T(8,128)(2,1)S(1)} %collective-permute-done.1.refs_2_) | copy-start | bytes 983044
  13.1 9.7 %collective-permute-start.3 = (bf16[32,5120]{1,0:T(8,128)(2,1)S(1)}, bf16[32,5120]{1,0:T(8,128)(2,1)S(1)}, u32[]{:S(2)}, u32[]{:S(2)}) collective-permute-start(bf16[32,5120]{1,0:T(8,128)(2,1)S(1)} %collective-permute-done.1.refs_2_), channel_id=1, source_target_pairs={{0,14},{1,15},{2,0},{3,1},{4,2},{5,3},{6,4},{7,5},{8,6},{9,7},{10,... | collective-permute-start | bytes 983048 | tf_op jit(solution)/shard_map/ppermute | solution.py:215
  16.7 9.8 %collective-permute-start.2 = (bf16[32,5120]{1,0:T(8,128)(2,1)S(1)}, bf16[32,5120]{1,0:T(8,128)(2,1)}, u32[]{:S(2)}, u32[]{:S(2)}) collective-permute-start(bf16[32,5120]{1,0:T(8,128)(2,1)S(1)} %collective-permute-done.refs_1_), channel_id=1, source_target_pairs={{0,2},{1,3},{2,4},{3,5},{4,6},{5,7},{6,8},{7,9},{8,10},{9,11},{10,... | collective-permute-start | bytes 983048 | tf_op jit(solution)/shard_map/ppermute | solution.py:214
  17.5 27.0 %copy-start = (bf16[320,1024]{1,0:T(8,128)(2,1)}, bf16[320,1024]{1,0:T(8,128)(2,1)S(1)}, u32[]{:S(2)}) copy-start(bf16[320,1024]{1,0:T(8,128)(2,1)S(1)} %constant_dynamic-update-slice_fusion) | copy-start | bytes 1966084
  18.4 25.3 %collective-permute-start.9 = (bf16[320,1024]{1,0:T(8,128)(2,1)}, bf16[320,1024]{1,0:T(8,128)(2,1)S(1)}, u32[]{:S(2)}, u32[]{:S(2)}) collective-permute-start(bf16[320,1024]{1,0:T(8,128)(2,1)} %hold.5), channel_id=1, source_target_pairs={{0,32},{16,48},{32,0},{48,16},{64,96},{80,112},{96,64},{112,80},{1... | collective-permute-start | bytes 1966088 | tf_op jit(solution)/shard_map/ppermute | solution.py:181
  22.8 8.9 %copy-start.15 = (bf16[32,5120]{1,0:T(8,128)(2,1)}, bf16[32,5120]{1,0:T(8,128)(2,1)S(1)}, u32[]{:S(2)}) copy-start(bf16[32,5120]{1,0:T(8,128)(2,1)S(1)} %collective-permute-done.3.refs_4_) | copy-start | bytes 983044
  22.8 8.9 %collective-permute-start.5 = (bf16[32,5120]{1,0:T(8,128)(2,1)S(1)}, bf16[32,5120]{1,0:T(8,128)(2,1)S(1)}, u32[]{:S(2)}, u32[]{:S(2)}) collective-permute-start(bf16[32,5120]{1,0:T(8,128)(2,1)S(1)} %collective-permute-done.3.refs_4_), channel_id=1, source_target_pairs={{0,14},{1,15},{2,0},{3,1},{4,2},{5,3},{6,4},{7,5},{8,6},{9,7},{10,... | collective-permute-start | bytes 983048 | tf_op jit(solution)/shard_map/ppermute | solution.py:215
  26.5 9.0 %collective-permute-start.4 = (bf16[32,5120]{1,0:T(8,128)(2,1)}, bf16[32,5120]{1,0:T(8,128)(2,1)S(1)}, u32[]{:S(2)}, u32[]{:S(2)}) collective-permute-start(bf16[32,5120]{1,0:T(8,128)(2,1)} %collective-permute-done.2.refs_3_), channel_id=1, source_target_pairs={{0,2},{1,3},{2,4},{3,5},{4,6},{5,7},{6,8},{7,9},{8,10},{9,11},{10,... | collective-permute-start | bytes 983048 | tf_op jit(solution)/shard_map/ppermute | solution.py:214
  31.7 5.1 %copy-start.8 = (bf16[32,5120]{1,0:T(8,128)(2,1)}, bf16[32,5120]{1,0:T(8,128)(2,1)S(1)}, u32[]{:S(2)}) copy-start(bf16[32,5120]{1,0:T(8,128)(2,1)S(1)} %collective-permute-done.5.refs_6_) | copy-start | bytes 983044
  31.7 10.7 %collective-permute-start.7 = (bf16[16,5120]{1,0:T(8,128)(2,1)S(1)}, bf16[16,5120]{1,0:T(8,128)(2,1)S(1)}, u32[]{:S(2)}, u32[]{:S(2)}) collective-permute-start(bf16[16,5120]{1,0:T(8,128)(2,1)S(1)} %slice.97), channel_id=1, source_target_pairs={{0,14},{1,15},{2,0},{3,1},{4,2},{5,3},{6,4},{7,5},{8,6},{9,7},{10,... | collective-permute-start | bytes 491528 | tf_op jit(solution)/shard_map/ppermute | solution.py:219
  35.5 7.5 %collective-permute-start.6 = (bf16[16,5120]{1,0:T(8,128)(2,1)S(1)}, bf16[16,5120]{1,0:T(8,128)(2,1)S(1)}, u32[]{:S(2)}, u32[]{:S(2)}) collective-permute-start(bf16[16,5120]{1,0:T(8,128)(2,1)S(1)} %slice.96), channel_id=1, source_target_pairs={{0,2},{1,3},{2,4},{3,5},{4,6},{5,7},{6,8},{7,9},{8,10},{9,11},{10,... | collective-permute-start | bytes 491528 | tf_op jit(solution)/shard_map/ppermute | solution.py:218
  36.8 75.0 %all-to-all-start.1 = ((bf16[16,128,768]{2,1,0:T(8,128)(2,1)}), bf16[16,128,768]{2,1,0:T(8,128)(2,1)}, u32[]{:S(2)}, u32[]{:S(2)}) async-start(bf16[16,128,768]{2,1,0:T(8,128)(2,1)} %hold.8), calls=%async_computation.1 | async-start | bytes 6291456 | tf_op jit(solution)/shard_map/all_to_all | solution.py:278
  42.4 6.4 %copy-start.11 = (bf16[16,5120]{1,0:T(8,128)(2,1)}, bf16[16,5120]{1,0:T(8,128)(2,1)S(1)}, u32[]{:S(2)}) copy-start(bf16[16,5120]{1,0:T(8,128)(2,1)S(1)} %collective-permute-done.7.refs_8_) | copy-start | bytes 491524
  43.0 5.8 %copy-start.12 = (bf16[16,5120]{1,0:T(8,128)(2,1)}, bf16[16,5120]{1,0:T(8,128)(2,1)S(1)}, u32[]{:S(2)}) copy-start(bf16[16,5120]{1,0:T(8,128)(2,1)S(1)} %collective-permute-done.6.refs_7_) | copy-start | bytes 491524
  46.7 27.9 %collective-permute-start.10 = (bf16[640,1024]{1,0:T(8,128)(2,1)}, bf16[640,1024]{1,0:T(8,128)(2,1)}, u32[]{:S(2)}, u32[]{:S(2)}) collective-permute-start(bf16[640,1024]{1,0:T(8,128)(2,1)} %pad_maximum_fusion), channel_id=1, source_target_pairs={{0,192},{16,208},{32,224},{48,240},{64,0},{80,16},{96,32},{112,48}... | collective-permute-start | bytes 3932168 | tf_op jit(solution)/shard_map/ppermute | solution.py:188
  47.2 29.0 %collective-permute-start.11 = (bf16[640,1024]{1,0:T(8,128)(2,1)}, bf16[640,1024]{1,0:T(8,128)(2,1)}, u32[]{:S(2)}, u32[]{:S(2)}) collective-permute-start(bf16[640,1024]{1,0:T(8,128)(2,1)} %pad_maximum_fusion), channel_id=1, source_target_pairs={{0,64},{16,80},{32,96},{48,112},{64,128},{80,144},{96,160},{112,17... | collective-permute-start | bytes 3932168 | tf_op jit(solution)/shard_map/ppermute | solution.py:187
  54.0 29.9 %collective-permute-start.14 = (bf16[256,2560]{1,0:T(8,128)(2,1)}, bf16[256,2560]{1,0:T(8,128)(2,1)S(1)}, u32[]{:S(2)}, u32[]{:S(2)}) collective-permute-start(bf16[256,2560]{1,0:T(8,128)(2,1)} %get-tuple-element.11), channel_id=1, source_target_pairs={{0,16},{16,0},{32,48},{48,32},{64,80},{80,64},{96,112},{112,96},{1... | collective-permute-start | bytes 3932168 | tf_op jit(solution)/shard_map/ppermute | solution.py:289
  56.1 23.2 %copy-start.4 = (bf16[256,2560]{1,0:T(8,128)(2,1)S(1)}, bf16[256,2560]{1,0:T(8,128)(2,1)}, u32[]{:S(2)}) copy-start(bf16[256,2560]{1,0:T(8,128)(2,1)} %get-tuple-element.9) | copy-start | bytes 3932164
  75.8 15.9 %collective-permute-start.13 = (bf16[640,512]{1,0:T(8,128)(2,1)S(1)}, bf16[640,512]{1,0:T(8,128)(2,1)S(1)}, u32[]{:S(2)}, u32[]{:S(2)}) collective-permute-start(bf16[640,512]{1,0:T(8,128)(2,1)S(1)} %slice.105), channel_id=1, source_target_pairs={{0,192},{16,208},{32,224},{48,240},{64,0},{80,16},{96,32},{112,48}... | collective-permute-start | bytes 1966088 | tf_op jit(solution)/shard_map/ppermute | solution.py:190
  77.4 13.9 %collective-permute-start.12 = (bf16[640,512]{1,0:T(8,128)(2,1)S(1)}, bf16[640,512]{1,0:T(8,128)(2,1)S(1)}, u32[]{:S(2)}, u32[]{:S(2)}) collective-permute-start(bf16[640,512]{1,0:T(8,128)(2,1)S(1)} %slice.103), channel_id=1, source_target_pairs={{0,64},{16,80},{32,96},{48,112},{64,128},{80,144},{96,160},{112,17... | collective-permute-start | bytes 1966088 | tf_op jit(solution)/shard_map/ppermute | solution.py:189
  81.2 2.0 %copy-start.1 = (bf16[320,1024]{1,0:T(8,128)(2,1)S(1)}, bf16[320,1024]{1,0:T(8,128)(2,1)}, u32[]{:S(2)}) copy-start(bf16[320,1024]{1,0:T(8,128)(2,1)} %copy-done) | copy-start | bytes 1966084
  81.2 2.0 %copy-start.3 = (bf16[320,1024]{1,0:T(8,128)(2,1)S(1)}, bf16[320,1024]{1,0:T(8,128)(2,1)}, u32[]{:S(2)}) copy-start(bf16[320,1024]{1,0:T(8,128)(2,1)} %hold.6) | copy-start | bytes 1966084
  91.7 2.0 %collective-permute-start.15 = (f32[256,512]{1,0:T(8,128)S(1)}, f32[256,512]{1,0:T(8,128)S(1)}, u32[]{:S(2)}, u32[]{:S(2)}) collective-permute-start(f32[256,512]{1,0:T(8,128)S(1)} %slice_add_fusion.1), channel_id=1, source_target_pairs={{0,16},{16,0},{32,48},{48,32},{64,80},{80,64},{96,112},{112,96},{1... | collective-permute-start | bytes 1572872 | tf_op jit(solution)/shard_map/ppermute | solution.py:293
  92.2 2.3 %collective-permute-start.16 = (f32[256,512]{1,0:T(8,128)S(1)}, f32[256,512]{1,0:T(8,128)S(1)}, u32[]{:S(2)}, u32[]{:S(2)}) collective-permute-start(f32[256,512]{1,0:T(8,128)S(1)} %slice_add_fusion), channel_id=1, source_target_pairs={{0,16},{16,0},{32,48},{48,32},{64,80},{80,64},{96,112},{112,96},{1... | collective-permute-start | bytes 1572872 | tf_op jit(solution)/shard_map/ppermute | solution.py:293
  95.1 22.0 %copy-start.10 = (s32[8]{0:T(128)S(1)}, s32[8]{0:T(128)}, u32[]{:S(2)}) copy-start(s32[8]{0:T(128)} %constant.80.clone) | copy-start | bytes 100
  111.9 31.5 %all-to-all-start = ((bf16[16,128,256]{2,1,0:T(8,128)(2,1)}), bf16[16,128,256]{2,1,0:T(8,128)(2,1)S(1)}, u32[]{:S(2)}, u32[]{:S(2)}) async-start(bf16[16,128,256]{2,1,0:T(8,128)(2,1)} %hold.7), calls=%async_computation | async-start | bytes 2097152 | tf_op jit(solution)/shard_map/all_to_all | solution.py:278
  117.4 17.1 %collective-permute-start.17 = (bf16[256,512]{1,0:T(8,128)(2,1)S(1)}, bf16[256,512]{1,0:T(8,128)(2,1)S(1)}, u32[]{:S(2)}, u32[]{:S(2)}) collective-permute-start(bf16[256,512]{1,0:T(8,128)(2,1)S(1)} %add_convert_fusion), channel_id=1, source_target_pairs={{0,1},{1,0},{2,3},{3,2},{4,5},{5,4},{6,7},{7,6},{8,9},{9,8},{10,11... | collective-permute-start | bytes 786440 | tf_op jit(solution)/shard_map/ppermute | solution.py:296
  (4 other events, 4.5 us)

commit v7 on v6

--- a/solution.py
+++ b/solution.py
@@ -60,7 +60,7 @@
 
 
 def hold(array, *until):
-    marks = [mark[:16, :HD] for mark in until]
+    marks = [mark[:16, :HD] if mark.shape[0] > 16 else mark for mark in until]
     return pl.pallas_call(
         hold_kernel,
         in_specs=[pl.BlockSpec(memory_space=pl.ANY)] * (1 + len(marks)),
@@ -79,7 +79,7 @@
 
 def unpack(blocks):
     parts, rows, width = blocks.shape
-    block = math.gcd(rows, 128)
+    block = math.gcd(rows, 64)
     return pl.pallas_call(
         unpack_kernel,
         grid=(rows // block,),
@@ -178,7 +178,7 @@
 
 def gather_weights(weights, early, *until):
     wide = jnp.concatenate([weights, lax.ppermute(weights, "seq", XL_SWAP)], axis=1)
-    other = lax.ppermute(hold(wide, early), "prompt", XH_SWAP)
+    other = lax.ppermute(hold(wide, *early), "prompt", XH_SWAP)
     return jnp.concatenate([wide, hold(other, *until)], axis=0)
 
 
@@ -217,7 +217,7 @@
         pieces += [up, down]
     pieces.append(lax.ppermute(up[:half], "seq", z_shift(1)))
     pieces.append(lax.ppermute(down[half:], "seq", z_shift(-1)))
-    return offsets + [Z // 2], pieces
+    return offsets + [Z // 2], pieces, down[half:]
 
 
 def split_kernel(count, where_ref, *refs):
@@ -240,7 +240,7 @@
                     place += ref.shape[0]
 
 
-def split_text(pieces, y, x_hi, core):
+def split_text(pieces, where):
     depth = pieces[0].shape[1]
     rows = sum(piece.shape[0] for piece in pieces)
     wide = depth // Y
@@ -262,7 +262,7 @@
             flops=SPLIT_FLOPS, bytes_accessed=4 * rows * depth, transcendentals=0
         ),
         name="split_text",
-    )(jnp.stack([y, x_hi, core]), *pieces)
+    )(where, *pieces)
 
 
 def body(
@@ -278,14 +278,15 @@
         heads = lax.all_to_all(packed, "seq", split_axis=0, concat_axis=0)
         return heads.reshape(-1, packed.shape[2])
 
-    offsets, pieces = ring_z(context[0])
+    offsets, pieces, sent = ring_z(context[0])
     both = jnp.concatenate([key_weight, value_weight], axis=1)
     packed = pack([queries[0], self_keys[0], self_values[0]], parts)
-    chunk = gather_weights(both, packed[0], *pieces[-2:])
-    qkv = to_heads(hold(packed, pieces[-3]))
+    where = jnp.stack([y, x_hi, core])
+    chunk = gather_weights(both, (packed[0], where), *pieces[-2:])
+    qkv = to_heads(hold(packed, sent))
     near, far = ring_y(chunk)
     text_rows = context.shape[1]
-    mine, theirs = split_text(pieces, y, x_hi, core)
+    mine, theirs = split_text(pieces, where)
     other = lax.ppermute(theirs, "prompt", CORE_SWAP)
     other_parts = project(other, near, far)
     own_parts = lax.optimization_barrier(project(mine, near, far))

time: 182 us -> 181 us (level)
    ppermute x1, waiting for transfers between devices: 0.01 us -> 2.76 us  [ring_z(): pieces.append(lax.ppermute(up[:half], 'seq', z_shift(1)))]
    ppermute x1, waiting for transfers between devices: 3.01 us -> 1.06 us  [ring_y(): far_left = lax.ppermute(before[:, :half], 'prompt', y_shift(1))]
    slice x7 -> x4, local copies, waits for them, and re-layouts: 4.29 us -> 2.37 us  [hold(): marks = [mark[:16, :HD] if mark.shape[0] > 16 else mark for mark in until]]
    all_to_all x2, waiting for transfers between devices: 24 us -> 25.8 us  [to_heads(): heads = lax.all_to_all(packed, 'seq', split_axis=0, concat_axis=0)]
where the time goes in v7:
time: 181 us; the launch traced here: 180 us
  waiting for transfers between devices  54.7 us (30%)
  starting transfers between devices  37.3 us (21%)
  blocking collectives  31.6 us (17%)
  Pallas kernels  30.3 us (17%)
  matrix products  10.3 us (6%)
  local copies, waits for them, and re-layouts  9.61 us (5%)
  other arithmetic  5.25 us (3%)
    all_to_all x1, blocking collectives, body(): lax.all_to_all(attended.reshape(parts, -1, width), 'seq', split_axis=0, c...  31.6 us
    all_to_all x2, waiting for transfers between devices, to_heads(): heads = lax.all_to_all(packed, 'seq', split_axis=0, concat_axis=0)  25.8 us
    ppermute x1, waiting for transfers between devices, ring_y(): after = lax.ppermute(chunk, 'prompt', y_shift(-1))  18.6 us
    pallas_call x1, Pallas kernels, self_attend(): pl.pallas_call(self_kernel, grid=(rows // block,), in_specs=[pl.BlockSpec...  14.3 us
    ppermute x3, starting transfers between devices, ring_z(): down = lax.ppermute(down, 'seq', z_shift(-1))  12.9 us
    dot_general x10, matrix products, dot(): return jnp.dot(rows, weights, preferred_element_type=jnp.float32)  10.3 us
    all_to_all x2, starting transfers between devices, to_heads(): heads = lax.all_to_all(packed, 'seq', split_axis=0, concat_axis=0)  8.87 us
    ppermute x3, waiting for transfers between devices, ring_z(): down = lax.ppermute(down, 'seq', z_shift(-1))  6.23 us
  transfers between devices with their start and end apart: 20, of which 9 were waited for; matrix products, arithmetic and copies ran while one was open for 13% of the time, Pallas kernels for 14%

profile of v7, /device:TPU:8, one launch (start us, length us, event | category | flops | bytes accessed | tf_op | source)
XLA Modules:
  0.0 180.2 jit_solution(7838763309304157877)
XLA Ops:
  0.0 5.9 %collective-permute-start.1 = (bf16[32,5120]{1,0:T(8,128)(2,1)}, bf16[32,5120]{1,0:T(8,128)(2,1)S(1)}, u32[]{:S(2)}, u32[]{:S(2)}) collective-permute-start(bf16[32,5120]{1,0:T(8,128)(2,1)} %bitcast.34), channel_id=1, source_target_pairs={{0,14},{1,15},{2,0},{3,1},{4,2},{5,3},{6,4},{7,5},{8,6},{9,7},{10,... | collective-permute-start | bytes 983048 | tf_op jit(solution)/shard_map/ppermute | solution.py:215
  6.9 1.6 collective-permute-start.8
  9.4 3.1 %pack.3.refs_0_ = bf16[16,128,768]{2,1,0:T(8,128)(2,1)} custom-call(bf16[128,4096]{1,0:T(8,128)(2,1)} %bitcast.31, bf16[128,4096]{1,0:T(8,128)(2,1)} %bitcast.32, bf16[128,4096]{1,0:T(8,128)(2,1)} %bitcast.33), custom_call_target="tpu_custom_call" | custom-call | bytes 6291456 | tf_op jit(solution)/shard_map/pack/pallas_call | solution.py:45
  13.6 3.3 %collective-permute-start.3 = (bf16[32,5120]{1,0:T(8,128)(2,1)S(1)}, bf16[32,5120]{1,0:T(8,128)(2,1)S(1)}, u32[]{:S(2)}, u32[]{:S(2)}) collective-permute-start(bf16[32,5120]{1,0:T(8,128)(2,1)S(1)} %collective-permute-done.1.refs_2_), channel_id=1, source_target_pairs={{0,14},{1,15},{2,0},{3,1},{4,2},{5,3},{6,4},{7,5},{8,6},{9,7},{10,... | collective-permute-start | bytes 983048 | tf_op jit(solution)/shard_map/ppermute | solution.py:215
  19.1 2.9 %collective-permute-start.9 = (bf16[320,1024]{1,0:T(8,128)(2,1)}, bf16[320,1024]{1,0:T(8,128)(2,1)S(1)}, u32[]{:S(2)}, u32[]{:S(2)}) collective-permute-start(bf16[320,1024]{1,0:T(8,128)(2,1)} %hold.5), channel_id=1, source_target_pairs={{0,32},{16,48},{32,0},{48,16},{64,96},{80,112},{96,64},{112,80},{1... | collective-permute-start | bytes 1966088 | tf_op jit(solution)/shard_map/ppermute | solution.py:181
  22.0 1.0 collective-permute-done.3.refs_4_
  23.0 3.7 %collective-permute-start.5 = (bf16[32,5120]{1,0:T(8,128)(2,1)S(1)}, bf16[32,5120]{1,0:T(8,128)(2,1)S(1)}, u32[]{:S(2)}, u32[]{:S(2)}) collective-permute-start(bf16[32,5120]{1,0:T(8,128)(2,1)S(1)} %collective-permute-done.3.refs_4_), channel_id=1, source_target_pairs={{0,14},{1,15},{2,0},{3,1},{4,2},{5,3},{6,4},{7,5},{8,6},{9,7},{10,... | collective-permute-start | bytes 983048 | tf_op jit(solution)/shard_map/ppermute | solution.py:215
  26.7 5.2 %collective-permute-done.5.refs_6_ = bf16[32,5120]{1,0:T(8,128)(2,1)S(1)} collective-permute-done((bf16[32,5120]{1,0:T(8,128)(2,1)S(1)}, bf16[32,5120]{1,0:T(8,128)(2,1)S(1)}, u32[]{:S(2)}, u32[]{:S(2)}) %collective-permute-start.5) | collective-permute-done | bytes 327712 | tf_op jit(solution)/shard_map/ppermute | solution.py:215
  31.9 3.8 %collective-permute-start.7 = (bf16[16,5120]{1,0:T(8,128)(2,1)S(1)}, bf16[16,5120]{1,0:T(8,128)(2,1)S(1)}, u32[]{:S(2)}, u32[]{:S(2)}) collective-permute-start(bf16[16,5120]{1,0:T(8,128)(2,1)S(1)} %slice.86.refs_1_), channel_id=1, source_target_pairs={{0,14},{1,15},{2,0},{3,1},{4,2},{5,3},{6,4},{7,5},{8,6},{9,7},{10,... | collective-permute-start | bytes 491528 | tf_op jit(solution)/shard_map/ppermute | solution.py:219
  36.4 4.8 %all-to-all-start.1 = ((bf16[16,128,768]{2,1,0:T(8,128)(2,1)}), bf16[16,128,768]{2,1,0:T(8,128)(2,1)}, u32[]{:S(2)}, u32[]{:S(2)}) async-start(bf16[16,128,768]{2,1,0:T(8,128)(2,1)} %hold.8), calls=%async_computation.1 | async-start | bytes 6291456 | tf_op jit(solution)/shard_map/all_to_all | solution.py:278
  41.3 2.8 %collective-permute-done.6.refs_7_.refs_1_ = bf16[16,5120]{1,0:T(8,128)(2,1)S(1)} collective-permute-done((bf16[16,5120]{1,0:T(8,128)(2,1)S(1)}, bf16[16,5120]{1,0:T(8,128)(2,1)S(1)}, u32[]{:S(2)}, u32[]{:S(2)}) %collective-permute-start.6) | collective-permute-done | bytes 163872 | tf_op jit(solution)/shard_map/ppermute | solution.py:218
  44.7 2.3 %pad_maximum_fusion = bf16[640,1024]{1,0:T(8,128)(2,1)} fusion(bf16[320,1024]{1,0:T(8,128)(2,1)} %hold.6, bf16[320,1024]{1,0:T(8,128)(2,1)S(1)} %constant_dynamic-update-slice_fusion), kind=kLoop, calls=%fused_computation.4 | loop fusion | flops 2621440 | bytes 2621440 | tf_op jit(solution)/shard_map/concatenate | solution.py:182
  47.4 1.6 collective-permute-start.11
  49.0 5.2 %split_text.1 = (bf16[256,2560]{1,0:T(8,128)(2,1)}, bf16[256,2560]{1,0:T(8,128)(2,1)}) custom-call(s32[3]{0:T(128)} %pad_add_fusion.where_ref.refs_2_, bf16[32,5120]{1,0:T(8,128)(2,1)} %bitcast.36, bf16[32,5120]{1,0:T(8,128)(2,1)} %copy-done.14, bf16[32,5120]{1,0:T(8,128)(2,1)} %copy-done.13, bf16[32,5120]{1,0:T(8,128)(2,1)} %collective-permute-done.2.refs_3_, ...), custom_call_target="tpu_custom_call" | custom-call | flops 399999991808 | bytes 5242880 | tf_op jit(solution)/shard_map/split_text/pallas_call | solution.py:249
  54.2 2.1 %pack.2.refs_0_ = bf16[16,128,256]{2,1,0:T(8,128)(2,1)} custom-call(bf16[128,4096]{1,0:T(8,128)(2,1)} %bitcast.30), custom_call_target="tpu_custom_call" | custom-call | bytes 2097152 | tf_op jit(solution)/shard_map/pack/pallas_call | solution.py:45
  56.3 18.6 %collective-permute-done.10 = bf16[640,1024]{1,0:T(8,128)(2,1)} collective-permute-done((bf16[640,1024]{1,0:T(8,128)(2,1)}, bf16[640,1024]{1,0:T(8,128)(2,1)}, u32[]{:S(2)}, u32[]{:S(2)}) %collective-permute-start.10) | collective-permute-done | bytes 1310752 | tf_op jit(solution)/shard_map/ppermute | solution.py:188
  74.9 1.1 slice.92
  76.1 1.1 slice.90
  77.3 2.3 %collective-permute-start.12 = (bf16[640,512]{1,0:T(8,128)(2,1)S(1)}, bf16[640,512]{1,0:T(8,128)(2,1)S(1)}, u32[]{:S(2)}, u32[]{:S(2)}) collective-permute-start(bf16[640,512]{1,0:T(8,128)(2,1)S(1)} %slice.90), channel_id=1, source_target_pairs={{0,64},{16,80},{32,96},{48,112},{64,128},{80,144},{96,160},{112,17... | collective-permute-start | bytes 1966088 | tf_op jit(solution)/shard_map/ppermute | solution.py:189
  79.5 1.9 %fusion.9 = f32[256,1024]{1,0:T(8,128)S(1)} fusion(bf16[640,1024]{1,0:T(8,128)(2,1)} %collective-permute-done.10, bf16[256,2560]{1,0:T(8,128)(2,1)S(1)} %copy-done.4), kind=kOutput, calls=%fused_computation.20 | convolution fusion | flops 335544320 | bytes 2686976 | tf_op jit(solution)/shard_map/dot_general | solution.py:199
  81.5 2.0 %fusion.7 = f32[256,1024]{1,0:T(8,128)S(1)} fusion(bf16[640,1024]{1,0:T(8,128)(2,1)} %collective-permute-done.11, bf16[256,2560]{1,0:T(8,128)(2,1)S(1)} %copy-done.4), kind=kOutput, calls=%fused_computation.18 | convolution fusion | flops 335544320 | bytes 2686976 | tf_op jit(solution)/shard_map/dot_general | solution.py:199
  84.1 1.9 %fusion.4 = f32[256,1024]{1,0:T(8,128)S(1)} fusion(bf16[640,1024]{1,0:T(8,128)(2,1)} %collective-permute-done.10, bf16[256,2560]{1,0:T(8,128)(2,1)S(1)} %collective-permute-done.14), kind=kOutput, calls=%fused_computation.14 | convolution fusion | flops 335544320 | bytes 2686976 | tf_op jit(solution)/shard_map/dot_general | solution.py:199
  86.0 1.9 %fusion.2 = f32[256,1024]{1,0:T(8,128)S(1)} fusion(bf16[640,1024]{1,0:T(8,128)(2,1)} %collective-permute-done.11, bf16[256,2560]{1,0:T(8,128)(2,1)S(1)} %collective-permute-done.14), kind=kOutput, calls=%fused_computation.12 | convolution fusion | flops 335544320 | bytes 2686976 | tf_op jit(solution)/shard_map/dot_general | solution.py:199
  88.5 1.1 collective-permute-done.12
  93.4 17.7 %all-to-all-done.1 = bf16[16,128,768]{2,1,0:T(8,128)(2,1)} async-done(((bf16[16,128,768]{2,1,0:T(8,128)(2,1)}), bf16[16,128,768]{2,1,0:T(8,128)(2,1)}, u32[]{:S(2)}, u32[]{:S(2)}) %all-to-all-start.1) | async-done | bytes 3145760 | tf_op jit(solution)/shard_map/all_to_all | solution.py:278
  111.1 4.1 %all-to-all-start = ((bf16[16,128,256]{2,1,0:T(8,128)(2,1)}), bf16[16,128,256]{2,1,0:T(8,128)(2,1)S(1)}, u32[]{:S(2)}, u32[]{:S(2)}) async-start(bf16[16,128,256]{2,1,0:T(8,128)(2,1)} %hold.7), calls=%async_computation | async-start | bytes 2097152 | tf_op jit(solution)/shard_map/all_to_all | solution.py:278
  116.1 2.2 %collective-permute-start.17 = (bf16[256,512]{1,0:T(8,128)(2,1)S(1)}, bf16[256,512]{1,0:T(8,128)(2,1)S(1)}, u32[]{:S(2)}, u32[]{:S(2)}) collective-permute-start(bf16[256,512]{1,0:T(8,128)(2,1)S(1)} %add_convert_fusion), channel_id=1, source_target_pairs={{0,1},{1,0},{2,3},{3,2},{4,5},{5,4},{6,7},{7,6},{8,9},{9,8},{10,11... | collective-permute-start | bytes 786440 | tf_op jit(solution)/shard_map/ppermute | solution.py:297
  118.3 14.3 %self_attend.1.self_ref = bf16[2048,256]{1,0:T(8,128)(2,1)S(1)} custom-call(bf16[2048,768]{1,0:T(8,128)(2,1)} %bitcast.13.q_ref.k_ref.v_ref, bf16[2048,768]{1,0:T(8,128)(2,1)} %bitcast.13.q_ref.k_ref.v_ref, bf16[2048,768]{1,0:T(8,128)(2,1)} %bitcast.13.q_ref.k_ref.v_ref), custom_call_target="tpu_custom_call" | custom-call | flops 4294967296 | bytes 4194304 | tf_op jit(solution)/shard_map/self_attend/pallas_call | solution.py:135
  134.9 8.1 %all-to-all-done = bf16[16,128,256]{2,1,0:T(8,128)(2,1)S(1)} async-done(((bf16[16,128,256]{2,1,0:T(8,128)(2,1)}), bf16[16,128,256]{2,1,0:T(8,128)(2,1)S(1)}, u32[]{:S(2)}, u32[]{:S(2)}) %all-to-all-start) | async-done | bytes 1048608 | tf_op jit(solution)/shard_map/all_to_all | solution.py:278
  143.0 3.5 %cross_attend.1 = bf16[2048,256]{1,0:T(8,128)(2,1)S(1)} custom-call(f32[1,512]{1,0:T(1,128)S(1)} %select_n.41.bias_ref, bf16[2048,256]{1,0:T(8,128)(2,1)S(1)} %bitcast.28, bf16[512,512]{1,0:T(8,128)(2,1)S(1)} %pad_maximum_fusion.1.tk_ref.tv_ref, bf16[512,512]{1,0:T(8,128)(2,1)S(1)} %pad_maximum_fusion.1.tk_ref.tv_ref, bf16[2048,256]{1,0:T(8,128)(2,1)S(1)} %self_attend.1.self_ref), custom_call_target="tpu_custom_call" | custom-call | flops 1073741824 | bytes 3145728 | tf_op jit(solution)/shard_map/cross_attend/pallas_call | solution.py:159
  146.5 31.6 %all_to_all.15.in_ref = bf16[16,128,256]{2,1,0:T(8,128)(2,1)} all-to-all(bf16[16,128,256]{2,1,0:T(8,128)(2,1)S(1)} %bitcast.29), channel_id=1, replica_groups=mesh['prompt'=16,'seq'=16] {'seq'}, dimensions={0} | all-to-all | bytes 2097152 | tf_op jit(solution)/shard_map/all_to_all | solution.py:307
  178.1 2.0 %unpack.1 = bf16[128,4096]{1,0:T(8,128)(2,1)} custom-call(bf16[16,128,256]{2,1,0:T(8,128)(2,1)} %all_to_all.15.in_ref), custom_call_target="tpu_custom_call" | custom-call | tf_op jit(solution)/shard_map/unpack/pallas_call | solution.py:83
  (87 shorter events, 14.6 us)
Async XLA Ops:
  0.0 13.5 %collective-permute-start.1 = (bf16[32,5120]{1,0:T(8,128)(2,1)}, bf16[32,5120]{1,0:T(8,128)(2,1)S(1)}, u32[]{:S(2)}, u32[]{:S(2)}) collective-permute-start(bf16[32,5120]{1,0:T(8,128)(2,1)} %bitcast.34), channel_id=1, source_target_pairs={{0,14},{1,15},{2,0},{3,1},{4,2},{5,3},{6,4},{7,5},{8,6},{9,7},{10,... | collective-permute-start | bytes 983048 | tf_op jit(solution)/shard_map/ppermute | solution.py:215
  5.9 11.0 %collective-permute-start = (bf16[32,5120]{1,0:T(8,128)(2,1)}, bf16[32,5120]{1,0:T(8,128)(2,1)S(1)}, u32[]{:S(2)}, u32[]{:S(2)}) collective-permute-start(bf16[32,5120]{1,0:T(8,128)(2,1)} %bitcast.35), channel_id=1, source_target_pairs={{0,2},{1,3},{2,4},{3,5},{4,6},{5,7},{6,8},{7,9},{8,10},{9,11},{10,... | collective-permute-start | bytes 983048 | tf_op jit(solution)/shard_map/ppermute | solution.py:214
  6.9 11.3 %collective-permute-start.8 = (bf16[320,512]{1,0:T(8,128)(2,1)S(1)}, bf16[320,512]{1,0:T(8,128)(2,1)S(1)}, u32[]{:S(2)}, u32[]{:S(2)}) collective-permute-start(bf16[320,512]{1,0:T(8,128)(2,1)S(1)} %pad_maximum_fusion.2), channel_id=1, source_target_pairs={{0,1},{1,0},{2,3},{3,2},{4,5},{5,4},{6,7},{7,6},{8,9},{9,8},{10,11... | collective-permute-start | bytes 983048 | tf_op jit(solution)/shard_map/ppermute | solution.py:180
  9.4 3.2 %copy-start.7 = (bf16[320,256]{1,0:T(8,128)(2,1)S(1)}, bf16[320,256]{1,0:T(8,128)(2,1)}, u32[]{:S(2)}) copy-start(bf16[320,256]{1,0:T(8,128)(2,1)} %param.15) | copy-start | bytes 491524
  13.5 5.5 %copy-start.13 = (bf16[32,5120]{1,0:T(8,128)(2,1)}, bf16[32,5120]{1,0:T(8,128)(2,1)S(1)}, u32[]{:S(2)}) copy-start(bf16[32,5120]{1,0:T(8,128)(2,1)S(1)} %collective-permute-done.1.refs_2_) | copy-start | bytes 983044
  13.6 9.4 %collective-permute-start.3 = (bf16[32,5120]{1,0:T(8,128)(2,1)S(1)}, bf16[32,5120]{1,0:T(8,128)(2,1)S(1)}, u32[]{:S(2)}, u32[]{:S(2)}) collective-permute-start(bf16[32,5120]{1,0:T(8,128)(2,1)S(1)} %collective-permute-done.1.refs_2_), channel_id=1, source_target_pairs={{0,14},{1,15},{2,0},{3,1},{4,2},{5,3},{6,4},{7,5},{8,6},{9,7},{10,... | collective-permute-start | bytes 983048 | tf_op jit(solution)/shard_map/ppermute | solution.py:215
  16.9 2.2 %copy-start.14 = (bf16[32,5120]{1,0:T(8,128)(2,1)}, bf16[32,5120]{1,0:T(8,128)(2,1)S(1)}, u32[]{:S(2)}) copy-start(bf16[32,5120]{1,0:T(8,128)(2,1)S(1)} %collective-permute-done.refs_1_) | copy-start | bytes 983044
  16.9 9.8 %collective-permute-start.2 = (bf16[32,5120]{1,0:T(8,128)(2,1)S(1)}, bf16[32,5120]{1,0:T(8,128)(2,1)}, u32[]{:S(2)}, u32[]{:S(2)}) collective-permute-start(bf16[32,5120]{1,0:T(8,128)(2,1)S(1)} %collective-permute-done.refs_1_), channel_id=1, source_target_pairs={{0,2},{1,3},{2,4},{3,5},{4,6},{5,7},{6,8},{7,9},{8,10},{9,11},{10,... | collective-permute-start | bytes 983048 | tf_op jit(solution)/shard_map/ppermute | solution.py:214
  18.2 26.5 %copy-start = (bf16[320,1024]{1,0:T(8,128)(2,1)}, bf16[320,1024]{1,0:T(8,128)(2,1)S(1)}, u32[]{:S(2)}) copy-start(bf16[320,1024]{1,0:T(8,128)(2,1)S(1)} %constant_dynamic-update-slice_fusion) | copy-start | bytes 1966084
  19.1 22.1 %collective-permute-start.9 = (bf16[320,1024]{1,0:T(8,128)(2,1)}, bf16[320,1024]{1,0:T(8,128)(2,1)S(1)}, u32[]{:S(2)}, u32[]{:S(2)}) collective-permute-start(bf16[320,1024]{1,0:T(8,128)(2,1)} %hold.5), channel_id=1, source_target_pairs={{0,32},{16,48},{32,0},{48,16},{64,96},{80,112},{96,64},{112,80},{1... | collective-permute-start | bytes 1966088 | tf_op jit(solution)/shard_map/ppermute | solution.py:181
  23.0 8.9 %copy-start.15 = (bf16[32,5120]{1,0:T(8,128)(2,1)}, bf16[32,5120]{1,0:T(8,128)(2,1)S(1)}, u32[]{:S(2)}) copy-start(bf16[32,5120]{1,0:T(8,128)(2,1)S(1)} %collective-permute-done.3.refs_4_) | copy-start | bytes 983044
  23.0 8.9 %collective-permute-start.5 = (bf16[32,5120]{1,0:T(8,128)(2,1)S(1)}, bf16[32,5120]{1,0:T(8,128)(2,1)S(1)}, u32[]{:S(2)}, u32[]{:S(2)}) collective-permute-start(bf16[32,5120]{1,0:T(8,128)(2,1)S(1)} %collective-permute-done.3.refs_4_), channel_id=1, source_target_pairs={{0,14},{1,15},{2,0},{3,1},{4,2},{5,3},{6,4},{7,5},{8,6},{9,7},{10,... | collective-permute-start | bytes 983048 | tf_op jit(solution)/shard_map/ppermute | solution.py:215
  26.7 9.0 %collective-permute-start.4 = (bf16[32,5120]{1,0:T(8,128)(2,1)}, bf16[32,5120]{1,0:T(8,128)(2,1)S(1)}, u32[]{:S(2)}, u32[]{:S(2)}) collective-permute-start(bf16[32,5120]{1,0:T(8,128)(2,1)} %collective-permute-done.2.refs_3_), channel_id=1, source_target_pairs={{0,2},{1,3},{2,4},{3,5},{4,6},{5,7},{6,8},{7,9},{8,10},{9,11},{10,... | collective-permute-start | bytes 983048 | tf_op jit(solution)/shard_map/ppermute | solution.py:214
  31.9 3.9 %copy-start.10 = (bf16[32,5120]{1,0:T(8,128)(2,1)}, bf16[32,5120]{1,0:T(8,128)(2,1)S(1)}, u32[]{:S(2)}) copy-start(bf16[32,5120]{1,0:T(8,128)(2,1)S(1)} %collective-permute-done.5.refs_6_) | copy-start | bytes 983044
  31.9 3.9 %copy-start.6 = (bf16[16,5120]{1,0:T(8,128)(2,1)}, bf16[16,5120]{1,0:T(8,128)(2,1)S(1)}, u32[]{:S(2)}) copy-start(bf16[16,5120]{1,0:T(8,128)(2,1)S(1)} %slice.86.refs_1_) | copy-start | bytes 491524
  31.9 9.3 %collective-permute-start.7 = (bf16[16,5120]{1,0:T(8,128)(2,1)S(1)}, bf16[16,5120]{1,0:T(8,128)(2,1)S(1)}, u32[]{:S(2)}, u32[]{:S(2)}) collective-permute-start(bf16[16,5120]{1,0:T(8,128)(2,1)S(1)} %slice.86.refs_1_), channel_id=1, source_target_pairs={{0,14},{1,15},{2,0},{3,1},{4,2},{5,3},{6,4},{7,5},{8,6},{9,7},{10,... | collective-permute-start | bytes 491528 | tf_op jit(solution)/shard_map/ppermute | solution.py:219
  35.7 8.3 %collective-permute-start.6 = (bf16[16,5120]{1,0:T(8,128)(2,1)S(1)}, bf16[16,5120]{1,0:T(8,128)(2,1)S(1)}, u32[]{:S(2)}, u32[]{:S(2)}) collective-permute-start(bf16[16,5120]{1,0:T(8,128)(2,1)S(1)} %slice.85), channel_id=1, source_target_pairs={{0,2},{1,3},{2,4},{3,5},{4,6},{5,7},{6,8},{7,9},{8,10},{9,11},{10,... | collective-permute-start | bytes 491528 | tf_op jit(solution)/shard_map/ppermute | solution.py:218
  36.4 74.6 %all-to-all-start.1 = ((bf16[16,128,768]{2,1,0:T(8,128)(2,1)}), bf16[16,128,768]{2,1,0:T(8,128)(2,1)}, u32[]{:S(2)}, u32[]{:S(2)}) async-start(bf16[16,128,768]{2,1,0:T(8,128)(2,1)} %hold.8), calls=%async_computation.1 | async-start | bytes 6291456 | tf_op jit(solution)/shard_map/all_to_all | solution.py:278
  41.2 2.8 %copy-start.2 = (bf16[320,1024]{1,0:T(8,128)(2,1)}, bf16[320,1024]{1,0:T(8,128)(2,1)S(1)}, u32[]{:S(2)}) copy-start(bf16[320,1024]{1,0:T(8,128)(2,1)S(1)} %collective-permute-done.9.refs_0_) | copy-start | bytes 1966084
  41.2 2.8 %copy-start.8 = (bf16[16,5120]{1,0:T(8,128)(2,1)}, bf16[16,5120]{1,0:T(8,128)(2,1)S(1)}, u32[]{:S(2)}) copy-start(bf16[16,5120]{1,0:T(8,128)(2,1)S(1)} %collective-permute-done.7.refs_8_.refs_2_) | copy-start | bytes 491524
  47.0 27.9 %collective-permute-start.10 = (bf16[640,1024]{1,0:T(8,128)(2,1)}, bf16[640,1024]{1,0:T(8,128)(2,1)}, u32[]{:S(2)}, u32[]{:S(2)}) collective-permute-start(bf16[640,1024]{1,0:T(8,128)(2,1)} %pad_maximum_fusion), channel_id=1, source_target_pairs={{0,192},{16,208},{32,224},{48,240},{64,0},{80,16},{96,32},{112,48}... | collective-permute-start | bytes 3932168 | tf_op jit(solution)/shard_map/ppermute | solution.py:188
  47.4 28.7 %collective-permute-start.11 = (bf16[640,1024]{1,0:T(8,128)(2,1)}, bf16[640,1024]{1,0:T(8,128)(2,1)}, u32[]{:S(2)}, u32[]{:S(2)}) collective-permute-start(bf16[640,1024]{1,0:T(8,128)(2,1)} %pad_maximum_fusion), channel_id=1, source_target_pairs={{0,64},{16,80},{32,96},{48,112},{64,128},{80,144},{96,160},{112,17... | collective-permute-start | bytes 3932168 | tf_op jit(solution)/shard_map/ppermute | solution.py:187
  54.2 29.9 %collective-permute-start.14 = (bf16[256,2560]{1,0:T(8,128)(2,1)}, bf16[256,2560]{1,0:T(8,128)(2,1)S(1)}, u32[]{:S(2)}, u32[]{:S(2)}) collective-permute-start(bf16[256,2560]{1,0:T(8,128)(2,1)} %get-tuple-element.11), channel_id=1, source_target_pairs={{0,16},{16,0},{32,48},{48,32},{64,80},{80,64},{96,112},{112,96},{1... | collective-permute-start | bytes 3932168 | tf_op jit(solution)/shard_map/ppermute | solution.py:290
  56.3 23.3 %copy-start.4 = (bf16[256,2560]{1,0:T(8,128)(2,1)S(1)}, bf16[256,2560]{1,0:T(8,128)(2,1)}, u32[]{:S(2)}) copy-start(bf16[256,2560]{1,0:T(8,128)(2,1)} %get-tuple-element.9) | copy-start | bytes 3932164
  76.0 14.0 %collective-permute-start.13 = (bf16[640,512]{1,0:T(8,128)(2,1)S(1)}, bf16[640,512]{1,0:T(8,128)(2,1)S(1)}, u32[]{:S(2)}, u32[]{:S(2)}) collective-permute-start(bf16[640,512]{1,0:T(8,128)(2,1)S(1)} %slice.92), channel_id=1, source_target_pairs={{0,192},{16,208},{32,224},{48,240},{64,0},{80,16},{96,32},{112,48}... | collective-permute-start | bytes 1966088 | tf_op jit(solution)/shard_map/ppermute | solution.py:190
  77.3 12.3 %collective-permute-start.12 = (bf16[640,512]{1,0:T(8,128)(2,1)S(1)}, bf16[640,512]{1,0:T(8,128)(2,1)S(1)}, u32[]{:S(2)}, u32[]{:S(2)}) collective-permute-start(bf16[640,512]{1,0:T(8,128)(2,1)S(1)} %slice.90), channel_id=1, source_target_pairs={{0,64},{16,80},{32,96},{48,112},{64,128},{80,144},{96,160},{112,17... | collective-permute-start | bytes 1966088 | tf_op jit(solution)/shard_map/ppermute | solution.py:189
  81.4 2.0 %copy-start.1 = (bf16[320,1024]{1,0:T(8,128)(2,1)S(1)}, bf16[320,1024]{1,0:T(8,128)(2,1)}, u32[]{:S(2)}) copy-start(bf16[320,1024]{1,0:T(8,128)(2,1)} %copy-done) | copy-start | bytes 1966084
  89.9 2.0 %collective-permute-start.15 = (f32[256,512]{1,0:T(8,128)S(1)}, f32[256,512]{1,0:T(8,128)S(1)}, u32[]{:S(2)}, u32[]{:S(2)}) collective-permute-start(f32[256,512]{1,0:T(8,128)S(1)} %slice_add_fusion.1), channel_id=1, source_target_pairs={{0,16},{16,0},{32,48},{48,32},{64,80},{80,64},{96,112},{112,96},{1... | collective-permute-start | bytes 1572872 | tf_op jit(solution)/shard_map/ppermute | solution.py:294
  90.4 2.3 %collective-permute-start.16 = (f32[256,512]{1,0:T(8,128)S(1)}, f32[256,512]{1,0:T(8,128)S(1)}, u32[]{:S(2)}, u32[]{:S(2)}) collective-permute-start(f32[256,512]{1,0:T(8,128)S(1)} %slice_add_fusion), channel_id=1, source_target_pairs={{0,16},{16,0},{32,48},{48,32},{64,80},{80,64},{96,112},{112,96},{1... | collective-permute-start | bytes 1572872 | tf_op jit(solution)/shard_map/ppermute | solution.py:294
  93.4 22.5 %copy-start.12 = (s32[8]{0:T(128)S(1)}, s32[8]{0:T(128)}, u32[]{:S(2)}) copy-start(s32[8]{0:T(128)} %constant.80.clone) | copy-start | bytes 100
  111.1 31.9 %all-to-all-start = ((bf16[16,128,256]{2,1,0:T(8,128)(2,1)}), bf16[16,128,256]{2,1,0:T(8,128)(2,1)S(1)}, u32[]{:S(2)}, u32[]{:S(2)}) async-start(bf16[16,128,256]{2,1,0:T(8,128)(2,1)} %hold.7), calls=%async_computation | async-start | bytes 2097152 | tf_op jit(solution)/shard_map/all_to_all | solution.py:278
  116.1 17.1 %collective-permute-start.17 = (bf16[256,512]{1,0:T(8,128)(2,1)S(1)}, bf16[256,512]{1,0:T(8,128)(2,1)S(1)}, u32[]{:S(2)}, u32[]{:S(2)}) collective-permute-start(bf16[256,512]{1,0:T(8,128)(2,1)S(1)} %add_convert_fusion), channel_id=1, source_target_pairs={{0,1},{1,0},{2,3},{3,2},{4,5},{5,4},{6,7},{7,6},{8,9},{9,8},{10,11... | collective-permute-start | bytes 786440 | tf_op jit(solution)/shard_map/ppermute | solution.py:297
  (4 other events, 4.1 us)

commit v8 on v7

--- a/solution.py
+++ b/solution.py
@@ -153,7 +153,7 @@
 def cross_attend(bias, cq, text, self_out):
     rows, width = cq.shape
     slots = text.shape[0]
-    block = math.gcd(rows, 1024)
+    block = math.gcd(rows, 2048)
     pairs = rows * width * slots
     row_spec = pl.BlockSpec((block, width), lambda i: (i, 0))
     return pl.pallas_call(

time: 181 us -> 181 us (level)
  no operation moved by 1% of the time
where the time goes in v8:
time: 181 us; the launch traced here: 180 us
  waiting for transfers between devices  54.7 us (30%)
  starting transfers between devices  37.3 us (21%)
  blocking collectives  31.6 us (17%)
  Pallas kernels  30 us (17%)
  matrix products  10.3 us (6%)
  local copies, waits for them, and re-layouts  9.61 us (5%)
  other arithmetic  5.25 us (3%)
    all_to_all x1, blocking collectives, body(): lax.all_to_all(attended.reshape(parts, -1, width), 'seq', split_axis=0, c...  31.6 us
    all_to_all x2, waiting for transfers between devices, to_heads(): heads = lax.all_to_all(packed, 'seq', split_axis=0, concat_axis=0)  25.8 us
    ppermute x1, waiting for transfers between devices, ring_y(): after = lax.ppermute(chunk, 'prompt', y_shift(-1))  18.6 us
    pallas_call x1, Pallas kernels, self_attend(): pl.pallas_call(self_kernel, grid=(rows // block,), in_specs=[pl.BlockSpec...  14.3 us
    ppermute x3, starting transfers between devices, ring_z(): down = lax.ppermute(down, 'seq', z_shift(-1))  12.9 us
    dot_general x10, matrix products, dot(): return jnp.dot(rows, weights, preferred_element_type=jnp.float32)  10.3 us
    all_to_all x2, starting transfers between devices, to_heads(): heads = lax.all_to_all(packed, 'seq', split_axis=0, concat_axis=0)  8.87 us
    ppermute x3, waiting for transfers between devices, ring_z(): down = lax.ppermute(down, 'seq', z_shift(-1))  6.23 us
  transfers between devices with their start and end apart: 20, of which 9 were waited for; matrix products, arithmetic and copies ran while one was open for 13% of the time, Pallas kernels for 14%

profile of v8, /device:TPU:8, one launch (start us, length us, event | category | flops | bytes accessed | tf_op | source)
XLA Modules:
  0.0 179.8 jit_solution(16434766757878773606)
XLA Ops:
  0.0 5.9 %collective-permute-start.1 = (bf16[32,5120]{1,0:T(8,128)(2,1)}, bf16[32,5120]{1,0:T(8,128)(2,1)S(1)}, u32[]{:S(2)}, u32[]{:S(2)}) collective-permute-start(bf16[32,5120]{1,0:T(8,128)(2,1)} %bitcast.34), channel_id=1, source_target_pairs={{0,14},{1,15},{2,0},{3,1},{4,2},{5,3},{6,4},{7,5},{8,6},{9,7},{10,... | collective-permute-start | bytes 983048 | tf_op jit(solution)/shard_map/ppermute | solution.py:215
  6.9 1.6 collective-permute-start.8
  9.4 3.1 %pack.3.refs_0_ = bf16[16,128,768]{2,1,0:T(8,128)(2,1)} custom-call(bf16[128,4096]{1,0:T(8,128)(2,1)} %bitcast.31, bf16[128,4096]{1,0:T(8,128)(2,1)} %bitcast.32, bf16[128,4096]{1,0:T(8,128)(2,1)} %bitcast.33), custom_call_target="tpu_custom_call" | custom-call | bytes 6291456 | tf_op jit(solution)/shard_map/pack/pallas_call | solution.py:45
  13.6 3.3 %collective-permute-start.3 = (bf16[32,5120]{1,0:T(8,128)(2,1)S(1)}, bf16[32,5120]{1,0:T(8,128)(2,1)S(1)}, u32[]{:S(2)}, u32[]{:S(2)}) collective-permute-start(bf16[32,5120]{1,0:T(8,128)(2,1)S(1)} %collective-permute-done.1.refs_2_), channel_id=1, source_target_pairs={{0,14},{1,15},{2,0},{3,1},{4,2},{5,3},{6,4},{7,5},{8,6},{9,7},{10,... | collective-permute-start | bytes 983048 | tf_op jit(solution)/shard_map/ppermute | solution.py:215
  19.1 2.9 %collective-permute-start.9 = (bf16[320,1024]{1,0:T(8,128)(2,1)}, bf16[320,1024]{1,0:T(8,128)(2,1)S(1)}, u32[]{:S(2)}, u32[]{:S(2)}) collective-permute-start(bf16[320,1024]{1,0:T(8,128)(2,1)} %hold.5), channel_id=1, source_target_pairs={{0,32},{16,48},{32,0},{48,16},{64,96},{80,112},{96,64},{112,80},{1... | collective-permute-start | bytes 1966088 | tf_op jit(solution)/shard_map/ppermute | solution.py:181
  22.0 1.0 collective-permute-done.3.refs_4_
  23.0 3.7 %collective-permute-start.5 = (bf16[32,5120]{1,0:T(8,128)(2,1)S(1)}, bf16[32,5120]{1,0:T(8,128)(2,1)S(1)}, u32[]{:S(2)}, u32[]{:S(2)}) collective-permute-start(bf16[32,5120]{1,0:T(8,128)(2,1)S(1)} %collective-permute-done.3.refs_4_), channel_id=1, source_target_pairs={{0,14},{1,15},{2,0},{3,1},{4,2},{5,3},{6,4},{7,5},{8,6},{9,7},{10,... | collective-permute-start | bytes 983048 | tf_op jit(solution)/shard_map/ppermute | solution.py:215
  26.7 5.2 %collective-permute-done.5.refs_6_ = bf16[32,5120]{1,0:T(8,128)(2,1)S(1)} collective-permute-done((bf16[32,5120]{1,0:T(8,128)(2,1)S(1)}, bf16[32,5120]{1,0:T(8,128)(2,1)S(1)}, u32[]{:S(2)}, u32[]{:S(2)}) %collective-permute-start.5) | collective-permute-done | bytes 327712 | tf_op jit(solution)/shard_map/ppermute | solution.py:215
  31.9 3.8 %collective-permute-start.7 = (bf16[16,5120]{1,0:T(8,128)(2,1)S(1)}, bf16[16,5120]{1,0:T(8,128)(2,1)S(1)}, u32[]{:S(2)}, u32[]{:S(2)}) collective-permute-start(bf16[16,5120]{1,0:T(8,128)(2,1)S(1)} %slice.86.refs_1_), channel_id=1, source_target_pairs={{0,14},{1,15},{2,0},{3,1},{4,2},{5,3},{6,4},{7,5},{8,6},{9,7},{10,... | collective-permute-start | bytes 491528 | tf_op jit(solution)/shard_map/ppermute | solution.py:219
  36.4 4.8 %all-to-all-start.1 = ((bf16[16,128,768]{2,1,0:T(8,128)(2,1)}), bf16[16,128,768]{2,1,0:T(8,128)(2,1)}, u32[]{:S(2)}, u32[]{:S(2)}) async-start(bf16[16,128,768]{2,1,0:T(8,128)(2,1)} %hold.8), calls=%async_computation.1 | async-start | bytes 6291456 | tf_op jit(solution)/shard_map/all_to_all | solution.py:278
  41.3 2.8 %collective-permute-done.6.refs_7_.refs_1_ = bf16[16,5120]{1,0:T(8,128)(2,1)S(1)} collective-permute-done((bf16[16,5120]{1,0:T(8,128)(2,1)S(1)}, bf16[16,5120]{1,0:T(8,128)(2,1)S(1)}, u32[]{:S(2)}, u32[]{:S(2)}) %collective-permute-start.6) | collective-permute-done | bytes 163872 | tf_op jit(solution)/shard_map/ppermute | solution.py:218
  44.7 2.3 %pad_maximum_fusion = bf16[640,1024]{1,0:T(8,128)(2,1)} fusion(bf16[320,1024]{1,0:T(8,128)(2,1)} %hold.6, bf16[320,1024]{1,0:T(8,128)(2,1)S(1)} %constant_dynamic-update-slice_fusion), kind=kLoop, calls=%fused_computation.4 | loop fusion | flops 2621440 | bytes 2621440 | tf_op jit(solution)/shard_map/concatenate | solution.py:182
  47.4 1.6 collective-permute-start.11
  49.0 5.2 %split_text.1 = (bf16[256,2560]{1,0:T(8,128)(2,1)}, bf16[256,2560]{1,0:T(8,128)(2,1)}) custom-call(s32[3]{0:T(128)} %pad_add_fusion.where_ref.refs_2_, bf16[32,5120]{1,0:T(8,128)(2,1)} %bitcast.36, bf16[32,5120]{1,0:T(8,128)(2,1)} %copy-done.14, bf16[32,5120]{1,0:T(8,128)(2,1)} %copy-done.13, bf16[32,5120]{1,0:T(8,128)(2,1)} %collective-permute-done.2.refs_3_, ...), custom_call_target="tpu_custom_call" | custom-call | flops 399999991808 | bytes 5242880 | tf_op jit(solution)/shard_map/split_text/pallas_call | solution.py:249
  54.2 2.1 %pack.2.refs_0_ = bf16[16,128,256]{2,1,0:T(8,128)(2,1)} custom-call(bf16[128,4096]{1,0:T(8,128)(2,1)} %bitcast.30), custom_call_target="tpu_custom_call" | custom-call | bytes 2097152 | tf_op jit(solution)/shard_map/pack/pallas_call | solution.py:45
  56.3 18.6 %collective-permute-done.10 = bf16[640,1024]{1,0:T(8,128)(2,1)} collective-permute-done((bf16[640,1024]{1,0:T(8,128)(2,1)}, bf16[640,1024]{1,0:T(8,128)(2,1)}, u32[]{:S(2)}, u32[]{:S(2)}) %collective-permute-start.10) | collective-permute-done | bytes 1310752 | tf_op jit(solution)/shard_map/ppermute | solution.py:188
  74.9 1.1 slice.92
  76.1 1.1 slice.90
  77.3 2.3 %collective-permute-start.12 = (bf16[640,512]{1,0:T(8,128)(2,1)S(1)}, bf16[640,512]{1,0:T(8,128)(2,1)S(1)}, u32[]{:S(2)}, u32[]{:S(2)}) collective-permute-start(bf16[640,512]{1,0:T(8,128)(2,1)S(1)} %slice.90), channel_id=1, source_target_pairs={{0,64},{16,80},{32,96},{48,112},{64,128},{80,144},{96,160},{112,17... | collective-permute-start | bytes 1966088 | tf_op jit(solution)/shard_map/ppermute | solution.py:189
  79.5 1.9 %fusion.9 = f32[256,1024]{1,0:T(8,128)S(1)} fusion(bf16[640,1024]{1,0:T(8,128)(2,1)} %collective-permute-done.10, bf16[256,2560]{1,0:T(8,128)(2,1)S(1)} %copy-done.4), kind=kOutput, calls=%fused_computation.20 | convolution fusion | flops 335544320 | bytes 2686976 | tf_op jit(solution)/shard_map/dot_general | solution.py:199
  81.5 2.0 %fusion.7 = f32[256,1024]{1,0:T(8,128)S(1)} fusion(bf16[640,1024]{1,0:T(8,128)(2,1)} %collective-permute-done.11, bf16[256,2560]{1,0:T(8,128)(2,1)S(1)} %copy-done.4), kind=kOutput, calls=%fused_computation.18 | convolution fusion | flops 335544320 | bytes 2686976 | tf_op jit(solution)/shard_map/dot_general | solution.py:199
  84.1 1.9 %fusion.4 = f32[256,1024]{1,0:T(8,128)S(1)} fusion(bf16[640,1024]{1,0:T(8,128)(2,1)} %collective-permute-done.10, bf16[256,2560]{1,0:T(8,128)(2,1)S(1)} %collective-permute-done.14), kind=kOutput, calls=%fused_computation.14 | convolution fusion | flops 335544320 | bytes 2686976 | tf_op jit(solution)/shard_map/dot_general | solution.py:199
  86.0 1.9 %fusion.2 = f32[256,1024]{1,0:T(8,128)S(1)} fusion(bf16[640,1024]{1,0:T(8,128)(2,1)} %collective-permute-done.11, bf16[256,2560]{1,0:T(8,128)(2,1)S(1)} %collective-permute-done.14), kind=kOutput, calls=%fused_computation.12 | convolution fusion | flops 335544320 | bytes 2686976 | tf_op jit(solution)/shard_map/dot_general | solution.py:199
  88.5 1.1 collective-permute-done.12
  93.4 17.7 %all-to-all-done.1 = bf16[16,128,768]{2,1,0:T(8,128)(2,1)} async-done(((bf16[16,128,768]{2,1,0:T(8,128)(2,1)}), bf16[16,128,768]{2,1,0:T(8,128)(2,1)}, u32[]{:S(2)}, u32[]{:S(2)}) %all-to-all-start.1) | async-done | bytes 3145760 | tf_op jit(solution)/shard_map/all_to_all | solution.py:278
  111.1 4.1 %all-to-all-start = ((bf16[16,128,256]{2,1,0:T(8,128)(2,1)}), bf16[16,128,256]{2,1,0:T(8,128)(2,1)S(1)}, u32[]{:S(2)}, u32[]{:S(2)}) async-start(bf16[16,128,256]{2,1,0:T(8,128)(2,1)} %hold.7), calls=%async_computation | async-start | bytes 2097152 | tf_op jit(solution)/shard_map/all_to_all | solution.py:278
  116.1 2.2 %collective-permute-start.17 = (bf16[256,512]{1,0:T(8,128)(2,1)S(1)}, bf16[256,512]{1,0:T(8,128)(2,1)S(1)}, u32[]{:S(2)}, u32[]{:S(2)}) collective-permute-start(bf16[256,512]{1,0:T(8,128)(2,1)S(1)} %add_convert_fusion), channel_id=1, source_target_pairs={{0,1},{1,0},{2,3},{3,2},{4,5},{5,4},{6,7},{7,6},{8,9},{9,8},{10,11... | collective-permute-start | bytes 786440 | tf_op jit(solution)/shard_map/ppermute | solution.py:297
  118.3 14.3 %self_attend.1.self_ref = bf16[2048,256]{1,0:T(8,128)(2,1)S(1)} custom-call(bf16[2048,768]{1,0:T(8,128)(2,1)} %bitcast.13.q_ref.k_ref.v_ref, bf16[2048,768]{1,0:T(8,128)(2,1)} %bitcast.13.q_ref.k_ref.v_ref, bf16[2048,768]{1,0:T(8,128)(2,1)} %bitcast.13.q_ref.k_ref.v_ref), custom_call_target="tpu_custom_call" | custom-call | flops 4294967296 | bytes 4194304 | tf_op jit(solution)/shard_map/self_attend/pallas_call | solution.py:135
  134.9 8.1 %all-to-all-done = bf16[16,128,256]{2,1,0:T(8,128)(2,1)S(1)} async-done(((bf16[16,128,256]{2,1,0:T(8,128)(2,1)}), bf16[16,128,256]{2,1,0:T(8,128)(2,1)S(1)}, u32[]{:S(2)}, u32[]{:S(2)}) %all-to-all-start) | async-done | bytes 1048608 | tf_op jit(solution)/shard_map/all_to_all | solution.py:278
  143.0 3.2 %cross_attend.1 = bf16[2048,256]{1,0:T(8,128)(2,1)S(1)} custom-call(f32[1,512]{1,0:T(1,128)S(1)} %select_n.41.bias_ref, bf16[2048,256]{1,0:T(8,128)(2,1)S(1)} %bitcast.28, bf16[512,512]{1,0:T(8,128)(2,1)S(1)} %pad_maximum_fusion.1.tk_ref.tv_ref, bf16[512,512]{1,0:T(8,128)(2,1)S(1)} %pad_maximum_fusion.1.tk_ref.tv_ref, bf16[2048,256]{1,0:T(8,128)(2,1)S(1)} %self_attend.1.self_ref), custom_call_target="tpu_custom_call" | custom-call | flops 1073741824 | bytes 3145728 | tf_op jit(solution)/shard_map/cross_attend/pallas_call | solution.py:159
  146.2 31.6 %all_to_all.15.in_ref = bf16[16,128,256]{2,1,0:T(8,128)(2,1)} all-to-all(bf16[16,128,256]{2,1,0:T(8,128)(2,1)S(1)} %bitcast.29), channel_id=1, replica_groups=mesh['prompt'=16,'seq'=16] {'seq'}, dimensions={0} | all-to-all | bytes 2097152 | tf_op jit(solution)/shard_map/all_to_all | solution.py:307
  177.8 2.0 %unpack.1 = bf16[128,4096]{1,0:T(8,128)(2,1)} custom-call(bf16[16,128,256]{2,1,0:T(8,128)(2,1)} %all_to_all.15.in_ref), custom_call_target="tpu_custom_call" | custom-call | tf_op jit(solution)/shard_map/unpack/pallas_call | solution.py:83
  (87 shorter events, 14.6 us)
Async XLA Ops:
  0.0 13.5 %collective-permute-start.1 = (bf16[32,5120]{1,0:T(8,128)(2,1)}, bf16[32,5120]{1,0:T(8,128)(2,1)S(1)}, u32[]{:S(2)}, u32[]{:S(2)}) collective-permute-start(bf16[32,5120]{1,0:T(8,128)(2,1)} %bitcast.34), channel_id=1, source_target_pairs={{0,14},{1,15},{2,0},{3,1},{4,2},{5,3},{6,4},{7,5},{8,6},{9,7},{10,... | collective-permute-start | bytes 983048 | tf_op jit(solution)/shard_map/ppermute | solution.py:215
  5.9 11.0 %collective-permute-start = (bf16[32,5120]{1,0:T(8,128)(2,1)}, bf16[32,5120]{1,0:T(8,128)(2,1)S(1)}, u32[]{:S(2)}, u32[]{:S(2)}) collective-permute-start(bf16[32,5120]{1,0:T(8,128)(2,1)} %bitcast.35), channel_id=1, source_target_pairs={{0,2},{1,3},{2,4},{3,5},{4,6},{5,7},{6,8},{7,9},{8,10},{9,11},{10,... | collective-permute-start | bytes 983048 | tf_op jit(solution)/shard_map/ppermute | solution.py:214
  6.9 11.3 %collective-permute-start.8 = (bf16[320,512]{1,0:T(8,128)(2,1)S(1)}, bf16[320,512]{1,0:T(8,128)(2,1)S(1)}, u32[]{:S(2)}, u32[]{:S(2)}) collective-permute-start(bf16[320,512]{1,0:T(8,128)(2,1)S(1)} %pad_maximum_fusion.2), channel_id=1, source_target_pairs={{0,1},{1,0},{2,3},{3,2},{4,5},{5,4},{6,7},{7,6},{8,9},{9,8},{10,11... | collective-permute-start | bytes 983048 | tf_op jit(solution)/shard_map/ppermute | solution.py:180
  9.4 3.2 %copy-start.7 = (bf16[320,256]{1,0:T(8,128)(2,1)S(1)}, bf16[320,256]{1,0:T(8,128)(2,1)}, u32[]{:S(2)}) copy-start(bf16[320,256]{1,0:T(8,128)(2,1)} %param.15) | copy-start | bytes 491524
  13.5 5.5 %copy-start.13 = (bf16[32,5120]{1,0:T(8,128)(2,1)}, bf16[32,5120]{1,0:T(8,128)(2,1)S(1)}, u32[]{:S(2)}) copy-start(bf16[32,5120]{1,0:T(8,128)(2,1)S(1)} %collective-permute-done.1.refs_2_) | copy-start | bytes 983044
  13.6 9.4 %collective-permute-start.3 = (bf16[32,5120]{1,0:T(8,128)(2,1)S(1)}, bf16[32,5120]{1,0:T(8,128)(2,1)S(1)}, u32[]{:S(2)}, u32[]{:S(2)}) collective-permute-start(bf16[32,5120]{1,0:T(8,128)(2,1)S(1)} %collective-permute-done.1.refs_2_), channel_id=1, source_target_pairs={{0,14},{1,15},{2,0},{3,1},{4,2},{5,3},{6,4},{7,5},{8,6},{9,7},{10,... | collective-permute-start | bytes 983048 | tf_op jit(solution)/shard_map/ppermute | solution.py:215
  16.9 2.2 %copy-start.14 = (bf16[32,5120]{1,0:T(8,128)(2,1)}, bf16[32,5120]{1,0:T(8,128)(2,1)S(1)}, u32[]{:S(2)}) copy-start(bf16[32,5120]{1,0:T(8,128)(2,1)S(1)} %collective-permute-done.refs_1_) | copy-start | bytes 983044
  16.9 9.8 %collective-permute-start.2 = (bf16[32,5120]{1,0:T(8,128)(2,1)S(1)}, bf16[32,5120]{1,0:T(8,128)(2,1)}, u32[]{:S(2)}, u32[]{:S(2)}) collective-permute-start(bf16[32,5120]{1,0:T(8,128)(2,1)S(1)} %collective-permute-done.refs_1_), channel_id=1, source_target_pairs={{0,2},{1,3},{2,4},{3,5},{4,6},{5,7},{6,8},{7,9},{8,10},{9,11},{10,... | collective-permute-start | bytes 983048 | tf_op jit(solution)/shard_map/ppermute | solution.py:214
  18.2 26.5 %copy-start = (bf16[320,1024]{1,0:T(8,128)(2,1)}, bf16[320,1024]{1,0:T(8,128)(2,1)S(1)}, u32[]{:S(2)}) copy-start(bf16[320,1024]{1,0:T(8,128)(2,1)S(1)} %constant_dynamic-update-slice_fusion) | copy-start | bytes 1966084
  19.1 22.1 %collective-permute-start.9 = (bf16[320,1024]{1,0:T(8,128)(2,1)}, bf16[320,1024]{1,0:T(8,128)(2,1)S(1)}, u32[]{:S(2)}, u32[]{:S(2)}) collective-permute-start(bf16[320,1024]{1,0:T(8,128)(2,1)} %hold.5), channel_id=1, source_target_pairs={{0,32},{16,48},{32,0},{48,16},{64,96},{80,112},{96,64},{112,80},{1... | collective-permute-start | bytes 1966088 | tf_op jit(solution)/shard_map/ppermute | solution.py:181
  23.0 8.9 %copy-start.15 = (bf16[32,5120]{1,0:T(8,128)(2,1)}, bf16[32,5120]{1,0:T(8,128)(2,1)S(1)}, u32[]{:S(2)}) copy-start(bf16[32,5120]{1,0:T(8,128)(2,1)S(1)} %collective-permute-done.3.refs_4_) | copy-start | bytes 983044
  23.0 8.9 %collective-permute-start.5 = (bf16[32,5120]{1,0:T(8,128)(2,1)S(1)}, bf16[32,5120]{1,0:T(8,128)(2,1)S(1)}, u32[]{:S(2)}, u32[]{:S(2)}) collective-permute-start(bf16[32,5120]{1,0:T(8,128)(2,1)S(1)} %collective-permute-done.3.refs_4_), channel_id=1, source_target_pairs={{0,14},{1,15},{2,0},{3,1},{4,2},{5,3},{6,4},{7,5},{8,6},{9,7},{10,... | collective-permute-start | bytes 983048 | tf_op jit(solution)/shard_map/ppermute | solution.py:215
  26.7 9.0 %collective-permute-start.4 = (bf16[32,5120]{1,0:T(8,128)(2,1)}, bf16[32,5120]{1,0:T(8,128)(2,1)S(1)}, u32[]{:S(2)}, u32[]{:S(2)}) collective-permute-start(bf16[32,5120]{1,0:T(8,128)(2,1)} %collective-permute-done.2.refs_3_), channel_id=1, source_target_pairs={{0,2},{1,3},{2,4},{3,5},{4,6},{5,7},{6,8},{7,9},{8,10},{9,11},{10,... | collective-permute-start | bytes 983048 | tf_op jit(solution)/shard_map/ppermute | solution.py:214
  31.9 3.9 %copy-start.10 = (bf16[32,5120]{1,0:T(8,128)(2,1)}, bf16[32,5120]{1,0:T(8,128)(2,1)S(1)}, u32[]{:S(2)}) copy-start(bf16[32,5120]{1,0:T(8,128)(2,1)S(1)} %collective-permute-done.5.refs_6_) | copy-start | bytes 983044
  31.9 3.9 %copy-start.6 = (bf16[16,5120]{1,0:T(8,128)(2,1)}, bf16[16,5120]{1,0:T(8,128)(2,1)S(1)}, u32[]{:S(2)}) copy-start(bf16[16,5120]{1,0:T(8,128)(2,1)S(1)} %slice.86.refs_1_) | copy-start | bytes 491524
  31.9 9.3 %collective-permute-start.7 = (bf16[16,5120]{1,0:T(8,128)(2,1)S(1)}, bf16[16,5120]{1,0:T(8,128)(2,1)S(1)}, u32[]{:S(2)}, u32[]{:S(2)}) collective-permute-start(bf16[16,5120]{1,0:T(8,128)(2,1)S(1)} %slice.86.refs_1_), channel_id=1, source_target_pairs={{0,14},{1,15},{2,0},{3,1},{4,2},{5,3},{6,4},{7,5},{8,6},{9,7},{10,... | collective-permute-start | bytes 491528 | tf_op jit(solution)/shard_map/ppermute | solution.py:219
  35.7 8.3 %collective-permute-start.6 = (bf16[16,5120]{1,0:T(8,128)(2,1)S(1)}, bf16[16,5120]{1,0:T(8,128)(2,1)S(1)}, u32[]{:S(2)}, u32[]{:S(2)}) collective-permute-start(bf16[16,5120]{1,0:T(8,128)(2,1)S(1)} %slice.85), channel_id=1, source_target_pairs={{0,2},{1,3},{2,4},{3,5},{4,6},{5,7},{6,8},{7,9},{8,10},{9,11},{10,... | collective-permute-start | bytes 491528 | tf_op jit(solution)/shard_map/ppermute | solution.py:218
  36.4 74.6 %all-to-all-start.1 = ((bf16[16,128,768]{2,1,0:T(8,128)(2,1)}), bf16[16,128,768]{2,1,0:T(8,128)(2,1)}, u32[]{:S(2)}, u32[]{:S(2)}) async-start(bf16[16,128,768]{2,1,0:T(8,128)(2,1)} %hold.8), calls=%async_computation.1 | async-start | bytes 6291456 | tf_op jit(solution)/shard_map/all_to_all | solution.py:278
  41.2 2.8 %copy-start.2 = (bf16[320,1024]{1,0:T(8,128)(2,1)}, bf16[320,1024]{1,0:T(8,128)(2,1)S(1)}, u32[]{:S(2)}) copy-start(bf16[320,1024]{1,0:T(8,128)(2,1)S(1)} %collective-permute-done.9.refs_0_) | copy-start | bytes 1966084
  41.2 2.8 %copy-start.8 = (bf16[16,5120]{1,0:T(8,128)(2,1)}, bf16[16,5120]{1,0:T(8,128)(2,1)S(1)}, u32[]{:S(2)}) copy-start(bf16[16,5120]{1,0:T(8,128)(2,1)S(1)} %collective-permute-done.7.refs_8_.refs_2_) | copy-start | bytes 491524
  47.0 27.9 %collective-permute-start.10 = (bf16[640,1024]{1,0:T(8,128)(2,1)}, bf16[640,1024]{1,0:T(8,128)(2,1)}, u32[]{:S(2)}, u32[]{:S(2)}) collective-permute-start(bf16[640,1024]{1,0:T(8,128)(2,1)} %pad_maximum_fusion), channel_id=1, source_target_pairs={{0,192},{16,208},{32,224},{48,240},{64,0},{80,16},{96,32},{112,48}... | collective-permute-start | bytes 3932168 | tf_op jit(solution)/shard_map/ppermute | solution.py:188
  47.4 28.7 %collective-permute-start.11 = (bf16[640,1024]{1,0:T(8,128)(2,1)}, bf16[640,1024]{1,0:T(8,128)(2,1)}, u32[]{:S(2)}, u32[]{:S(2)}) collective-permute-start(bf16[640,1024]{1,0:T(8,128)(2,1)} %pad_maximum_fusion), channel_id=1, source_target_pairs={{0,64},{16,80},{32,96},{48,112},{64,128},{80,144},{96,160},{112,17... | collective-permute-start | bytes 3932168 | tf_op jit(solution)/shard_map/ppermute | solution.py:187
  54.2 29.9 %collective-permute-start.14 = (bf16[256,2560]{1,0:T(8,128)(2,1)}, bf16[256,2560]{1,0:T(8,128)(2,1)S(1)}, u32[]{:S(2)}, u32[]{:S(2)}) collective-permute-start(bf16[256,2560]{1,0:T(8,128)(2,1)} %get-tuple-element.11), channel_id=1, source_target_pairs={{0,16},{16,0},{32,48},{48,32},{64,80},{80,64},{96,112},{112,96},{1... | collective-permute-start | bytes 3932168 | tf_op jit(solution)/shard_map/ppermute | solution.py:290
  56.3 23.3 %copy-start.4 = (bf16[256,2560]{1,0:T(8,128)(2,1)S(1)}, bf16[256,2560]{1,0:T(8,128)(2,1)}, u32[]{:S(2)}) copy-start(bf16[256,2560]{1,0:T(8,128)(2,1)} %get-tuple-element.9) | copy-start | bytes 3932164
  76.0 14.0 %collective-permute-start.13 = (bf16[640,512]{1,0:T(8,128)(2,1)S(1)}, bf16[640,512]{1,0:T(8,128)(2,1)S(1)}, u32[]{:S(2)}, u32[]{:S(2)}) collective-permute-start(bf16[640,512]{1,0:T(8,128)(2,1)S(1)} %slice.92), channel_id=1, source_target_pairs={{0,192},{16,208},{32,224},{48,240},{64,0},{80,16},{96,32},{112,48}... | collective-permute-start | bytes 1966088 | tf_op jit(solution)/shard_map/ppermute | solution.py:190
  77.3 12.3 %collective-permute-start.12 = (bf16[640,512]{1,0:T(8,128)(2,1)S(1)}, bf16[640,512]{1,0:T(8,128)(2,1)S(1)}, u32[]{:S(2)}, u32[]{:S(2)}) collective-permute-start(bf16[640,512]{1,0:T(8,128)(2,1)S(1)} %slice.90), channel_id=1, source_target_pairs={{0,64},{16,80},{32,96},{48,112},{64,128},{80,144},{96,160},{112,17... | collective-permute-start | bytes 1966088 | tf_op jit(solution)/shard_map/ppermute | solution.py:189
  81.4 2.0 %copy-start.1 = (bf16[320,1024]{1,0:T(8,128)(2,1)S(1)}, bf16[320,1024]{1,0:T(8,128)(2,1)}, u32[]{:S(2)}) copy-start(bf16[320,1024]{1,0:T(8,128)(2,1)} %copy-done) | copy-start | bytes 1966084
  89.9 2.0 %collective-permute-start.15 = (f32[256,512]{1,0:T(8,128)S(1)}, f32[256,512]{1,0:T(8,128)S(1)}, u32[]{:S(2)}, u32[]{:S(2)}) collective-permute-start(f32[256,512]{1,0:T(8,128)S(1)} %slice_add_fusion.1), channel_id=1, source_target_pairs={{0,16},{16,0},{32,48},{48,32},{64,80},{80,64},{96,112},{112,96},{1... | collective-permute-start | bytes 1572872 | tf_op jit(solution)/shard_map/ppermute | solution.py:294
  90.4 2.3 %collective-permute-start.16 = (f32[256,512]{1,0:T(8,128)S(1)}, f32[256,512]{1,0:T(8,128)S(1)}, u32[]{:S(2)}, u32[]{:S(2)}) collective-permute-start(f32[256,512]{1,0:T(8,128)S(1)} %slice_add_fusion), channel_id=1, source_target_pairs={{0,16},{16,0},{32,48},{48,32},{64,80},{80,64},{96,112},{112,96},{1... | collective-permute-start | bytes 1572872 | tf_op jit(solution)/shard_map/ppermute | solution.py:294
  93.4 22.5 %copy-start.12 = (s32[8]{0:T(128)S(1)}, s32[8]{0:T(128)}, u32[]{:S(2)}) copy-start(s32[8]{0:T(128)} %constant.80.clone) | copy-start | bytes 100
  111.1 31.9 %all-to-all-start = ((bf16[16,128,256]{2,1,0:T(8,128)(2,1)}), bf16[16,128,256]{2,1,0:T(8,128)(2,1)S(1)}, u32[]{:S(2)}, u32[]{:S(2)}) async-start(bf16[16,128,256]{2,1,0:T(8,128)(2,1)} %hold.7), calls=%async_computation | async-start | bytes 2097152 | tf_op jit(solution)/shard_map/all_to_all | solution.py:278
  116.1 17.1 %collective-permute-start.17 = (bf16[256,512]{1,0:T(8,128)(2,1)S(1)}, bf16[256,512]{1,0:T(8,128)(2,1)S(1)}, u32[]{:S(2)}, u32[]{:S(2)}) collective-permute-start(bf16[256,512]{1,0:T(8,128)(2,1)S(1)} %add_convert_fusion), channel_id=1, source_target_pairs={{0,1},{1,0},{2,3},{3,2},{4,5},{5,4},{6,7},{7,6},{8,9},{9,8},{10,11... | collective-permute-start | bytes 786440 | tf_op jit(solution)/shard_map/ppermute | solution.py:297
  (4 other events, 4.1 us)
